TPU v7x, 32 devices: a whole 2x2x4 slice. The times are simulated.
32 devices in a mesh: task: 4 (over x, core), dp: 8 (over z, y).
Axes of the slice: x: 2, y: 2, z: 4, core: 2. Of those that a mesh axis runs over, the one named last changes fastest.
Arguments:
- layer_input: float32 [4, 8, 1024, 384], P('task', 'dp'), may hold values from -6 to 6
- cotangent: float32 [4, 8, 1024, 384], P('task', 'dp'), may hold values from -6 to 6
- norm_gain: float32 [2, 384], replicated, may hold values from 0.1 to 1.9
- norm_bias: float32 [2, 384], replicated, may hold values from -2 to 2
- w_qkv: bfloat16 [384, 1152], P('dp'), may hold values from -0.5 to 0.5
- w_proj: bfloat16 [384, 384], P('dp'), may hold values from -0.3125 to 0.3125
- router: float32 [4, 384, 16], P('task'), may hold values from -0.15 to 0.15
- w_in: bfloat16 [16, 384, 1536], P('task', 'dp'), may hold values from -0.3125 to 0.3125
- w_out: bfloat16 [16, 1536, 384], P('task', 'dp'), may hold values from -1.25 to 1.25
- choices: int32 [4, 8, 1024, 4], P('task', 'dp'), may hold values from 0 to 15, all different within a row; in each aligned block of 1024 rows (0 to 1023, 1024 to 2047, ..., all dimensions but the last counted through in order) at most 320 rows name the same one
- top_count: int32 [4], P('task'), may hold values from 1 to 4, as said below
Outputs:
- activations: float32 [4, 8, 1024, 384], P('task', 'dp')
- input_grad: float32 [4, 8, 1024, 384], P('task', 'dp')
- grad_norm_gain: float32 [2, 384], replicated
- grad_norm_bias: float32 [2, 384], replicated
- grad_w_qkv: float32 [384, 1152], P('dp')
- grad_w_proj: float32 [384, 384], P('dp')
- grad_router: float32 [4, 384, 16], P('task')
- grad_w_in: float32 [16, 384, 1536], P('task', 'dp')
- grad_w_out: float32 [16, 1536, 384], P('task', 'dp')
Inputs may be any that keep to these rules, and one draw needn't show every extreme that they name: `choices`: each token's row names 4 different experts and the token uses the first top_count of its task. Within the rows of one device no expert is named by more than 320 rows. `top_count`: the 4 tasks use different numbers of choices.
All inputs are finite; a program needn't handle non-finite values.
Results may differ from a plain program's by a relative error of at most 0.017.
The roundings to bfloat16 on the way count: a program that leaves them out, or rounds other values in their place, can miss the bound.
Values may be sent and summed in bfloat16 or wider, within the bound.
A program may use at most 192 MiB of HBM per device.

v0:
```python
import jax
import jax.numpy as jnp
from jax import lax
from jax.sharding import PartitionSpec as P

D = 384
HEADS = 6
HEAD_DIM = 64
EXPERTS = 16
TOPMAX = 4
SEQ = 1024
QBLOCK = 512
CAP = 320


highest = lax.Precision.HIGHEST
epsilon = 1e-06


def layer_norm(inputs, norm_scale, norm_shift):
    mean_val = jnp.mean(inputs, axis=-1, keepdims=True)
    centered = inputs - mean_val
    variance = jnp.mean(centered * centered, axis=-1, keepdims=True)
    return centered * lax.rsqrt(variance + epsilon) * norm_scale + norm_shift


def norm_back(inputs, norm_scale, norm_shift, grad_rows):
    _, pullback = jax.vjp(layer_norm, inputs, norm_scale, norm_shift)
    return pullback(grad_rows)


def gelu_exact(inputs):
    return jax.nn.gelu(inputs, approximate=False)


def split_blocks(packed):
    split_qkv = packed.reshape(SEQ, 3, HEADS, HEAD_DIM)
    query_blocks = split_qkv[:, 0].reshape(SEQ // QBLOCK, QBLOCK, HEADS, HEAD_DIM)
    return (query_blocks, split_qkv[:, 1], split_qkv[:, 2])


def attention_forward(image_rows, norm_gain, norm_bias, weight_qkv, weight_proj):
    score_scale = HEAD_DIM ** (-0.5)
    normed = layer_norm(image_rows, norm_gain[0], norm_bias[0])
    packed = jnp.dot(
        normed.astype(jnp.bfloat16), weight_qkv, preferred_element_type=jnp.float32
    ).astype(jnp.bfloat16)
    query_blocks, key_rows, value_rows = split_blocks(packed)

    def one_block(query_rows):
        scores = (
            jnp.einsum("qhd,khd->hqk", query_rows, key_rows, preferred_element_type=jnp.float32)
            * score_scale
        )
        row_max = jnp.max(scores, axis=-1, keepdims=True)
        exp_scores = jnp.exp(scores - row_max)
        row_total = jnp.sum(exp_scores, axis=-1, keepdims=True)
        prob_rows = (exp_scores / row_total).astype(jnp.bfloat16)
        mixed_rows = jnp.einsum(
            "hqk,khd->qhd", prob_rows, value_rows, preferred_element_type=jnp.float32
        )
        return (mixed_rows, row_max + jnp.log(row_total))

    mixed_rows, log_total = lax.map(one_block, query_blocks)
    mixed_low = mixed_rows.reshape(SEQ, D).astype(jnp.bfloat16)
    branch = jnp.dot(mixed_low, weight_proj, preferred_element_type=jnp.float32)
    return (image_rows + branch, packed, mixed_low, log_total)


def attention_backward(
    image_rows,
    grad_mid,
    packed,
    mixed_low,
    log_total,
    norm_gain,
    norm_bias,
    weight_qkv,
    weight_proj,
):
    score_scale = HEAD_DIM ** (-0.5)
    grad_low = grad_mid.astype(jnp.bfloat16)
    grad_proj = jnp.einsum("sd,se->de", mixed_low, grad_low, preferred_element_type=jnp.float32)
    grad_heads = jnp.einsum(
        "se,de->sd", grad_low, weight_proj, preferred_element_type=jnp.float32
    ).astype(jnp.bfloat16)
    grad_heads = grad_heads.reshape(SEQ // QBLOCK, QBLOCK, HEADS, HEAD_DIM)
    query_blocks, key_rows, value_rows = split_blocks(packed)

    def one_block(running, operands):
        grad_keys, grad_values = running
        query_rows, grad_rows, block_total = operands
        scores = (
            jnp.einsum("qhd,khd->hqk", query_rows, key_rows, preferred_element_type=jnp.float32)
            * score_scale
        )
        prob_rows = jnp.exp(scores - block_total)
        grad_probs = jnp.einsum(
            "qhd,khd->hqk", grad_rows, value_rows, preferred_element_type=jnp.float32
        )
        grad_scores = (
            prob_rows * (grad_probs - jnp.sum(prob_rows * grad_probs, axis=-1, keepdims=True))
        ).astype(jnp.bfloat16)
        grad_query = (
            jnp.einsum("hqk,khd->qhd", grad_scores, key_rows, preferred_element_type=jnp.float32)
            * score_scale
        )
        grad_keys = (
            grad_keys
            + jnp.einsum(
                "hqk,qhd->khd", grad_scores, query_rows, preferred_element_type=jnp.float32
            )
            * score_scale
        )
        grad_values = grad_values + jnp.einsum(
            "hqk,qhd->khd",
            prob_rows.astype(jnp.bfloat16),
            grad_rows,
            preferred_element_type=jnp.float32,
        )
        return ((grad_keys, grad_values), grad_query)

    zero_block = jnp.zeros((SEQ, HEADS, HEAD_DIM), jnp.float32)
    (grad_keys, grad_values), grad_query = lax.scan(
        one_block, (zero_block, zero_block), (query_blocks, grad_heads, log_total)
    )
    grad_packed = jnp.stack(
        [grad_query.reshape(SEQ, HEADS, HEAD_DIM), grad_keys, grad_values], axis=1
    )
    grad_packed = grad_packed.reshape(SEQ, 3 * D).astype(jnp.bfloat16)
    normed = layer_norm(image_rows, norm_gain[0], norm_bias[0])
    grad_qkv_part = jnp.einsum(
        "sd,se->de", normed.astype(jnp.bfloat16), grad_packed, preferred_element_type=jnp.float32
    )
    grad_normed = jnp.einsum(
        "se,de->sd", grad_packed, weight_qkv, preferred_element_type=jnp.float32
    )
    grad_image, grad_gain, grad_bias = norm_back(
        image_rows, norm_gain[0], norm_bias[0], grad_normed
    )
    return (grad_mid + grad_image, grad_qkv_part, grad_proj, grad_gain, grad_bias)


def expert_forward(operands):
    rows_in, weight_in, weight_out = operands
    pre_act = jnp.dot(rows_in, weight_in, preferred_element_type=jnp.float32)
    hidden_units = gelu_exact(pre_act).astype(jnp.bfloat16)
    return jnp.dot(hidden_units, weight_out, preferred_element_type=jnp.float32).astype(
        jnp.bfloat16
    )


def expert_backward(operands):
    rows_in, grad_rows, weight_in, weight_out = operands
    pre_act = jnp.dot(rows_in, weight_in, preferred_element_type=jnp.float32)
    hidden_units, pullback = jax.vjp(gelu_exact, pre_act)
    grad_hidden = jnp.einsum("md,fd->mf", grad_rows, weight_out, preferred_element_type=jnp.float32)
    grad_weight_out = jnp.einsum(
        "mf,md->fd",
        hidden_units.astype(jnp.bfloat16),
        grad_rows,
        preferred_element_type=jnp.float32,
    )
    grad_pre = pullback(grad_hidden)[0].astype(jnp.bfloat16)
    grad_weight_in = jnp.einsum("md,mf->df", rows_in, grad_pre, preferred_element_type=jnp.float32)
    grad_input = jnp.einsum(
        "mf,df->md", grad_pre, weight_in, preferred_element_type=jnp.float32
    ).astype(jnp.bfloat16)
    return (grad_weight_in, grad_weight_out, grad_input)


def local(
    layer_input,
    cotangent,
    norm_gain,
    norm_bias,
    w_qkv,
    w_proj,
    router,
    w_in,
    w_out,
    choices,
    top_count,
):
    groups = lax.axis_size("task")
    local_count = w_in.shape[0]
    full_qkv, full_proj, full_in, full_out = (
        lax.all_gather(w_qkv, "dp", axis=0, tiled=True),
        lax.all_gather(w_proj, "dp", axis=0, tiled=True),
        lax.all_gather(w_in, "dp", axis=1, tiled=True),
        lax.all_gather(w_out, "dp", axis=1, tiled=True),
    )
    images = layer_input[0]
    image_count = images.shape[0]
    row_count = image_count * SEQ

    def attend_one(image_rows):
        return attention_forward(image_rows, norm_gain, norm_bias, full_qkv, full_proj)

    mid_images, packed_all, mixed_all, totals_all = lax.map(attend_one, images)
    mid_rows = mid_images.reshape(row_count, D)
    normed = layer_norm(mid_rows, norm_gain[1], norm_bias[1])
    logits = jnp.dot(normed, router[0], precision=highest)
    logit_max = jnp.max(logits, axis=-1, keepdims=True)
    logit_exp = jnp.exp(logits - logit_max)
    route_probs = logit_exp / jnp.sum(logit_exp, axis=-1, keepdims=True)
    routes = choices.reshape(row_count, TOPMAX)
    live_mask = jnp.arange(TOPMAX, dtype=jnp.int32)[None, :] < top_count[0]
    onehot = (
        (routes[:, :, None] == jnp.arange(EXPERTS, dtype=jnp.int32)[None, None, :])
        & live_mask[:, :, None]
    ).astype(jnp.int32)
    flat_hot = onehot.reshape(row_count * TOPMAX, EXPERTS)
    before = jnp.cumsum(flat_hot, axis=0) - flat_hot
    slot_rows = jnp.sum(before * flat_hot, axis=1).reshape(row_count, TOPMAX)
    target = jnp.where(live_mask, routes * CAP + slot_rows, EXPERTS * CAP).reshape(-1)
    hot_float = onehot.astype(jnp.float32)
    gate_rows = jnp.sum(route_probs[:, None, :] * hot_float, axis=2)
    spread = jnp.broadcast_to(
        normed.astype(jnp.bfloat16)[:, None, :], (row_count, TOPMAX, D)
    ).reshape(-1, D)
    buffer = jnp.zeros((EXPERTS * CAP, D), jnp.bfloat16).at[target].set(spread, mode="drop")
    outgoing = buffer.reshape(groups, local_count, CAP, D)
    received = lax.all_to_all(outgoing, "task", split_axis=0, concat_axis=2, tiled=True)
    expert_rows = received.reshape(local_count, groups * CAP, D)
    outputs = lax.map(expert_forward, (expert_rows, full_in, full_out))
    returned = lax.all_to_all(
        outputs.reshape(1, local_count, groups * CAP, D),
        "task",
        split_axis=2,
        concat_axis=0,
        tiled=True,
    )
    zero_row = jnp.zeros((1, D), jnp.bfloat16)
    picked = jnp.concatenate([returned.reshape(EXPERTS * CAP, D), zero_row], axis=0)[target]
    picked = picked.reshape(row_count, TOPMAX, D)
    mix_rows = jnp.sum(gate_rows[:, :, None] * picked, axis=1)
    activations = (mid_rows + mix_rows).reshape(layer_input.shape)
    grad_out = cotangent[0].reshape(row_count, D)
    grad_gate = jnp.sum(grad_out[:, None, :] * picked, axis=2) * live_mask
    grad_picked = (gate_rows[:, :, None] * grad_out[:, None, :]).astype(jnp.bfloat16).reshape(-1, D)
    grad_buffer = (
        jnp.zeros((EXPERTS * CAP, D), jnp.bfloat16).at[target].set(grad_picked, mode="drop")
    )
    grad_expert_rows = lax.all_to_all(
        grad_buffer.reshape(groups, local_count, CAP, D),
        "task",
        split_axis=0,
        concat_axis=2,
        tiled=True,
    )
    grad_expert_rows = grad_expert_rows.reshape(local_count, groups * CAP, D)
    back_in, back_out = (
        lax.all_gather(w_in, "dp", axis=1, tiled=True),
        lax.all_gather(w_out, "dp", axis=1, tiled=True),
    )
    back_rows = lax.all_to_all(outgoing, "task", split_axis=0, concat_axis=2, tiled=True).reshape(
        local_count, groups * CAP, D
    )
    grad_in_w, grad_out_w, grad_rows = lax.map(
        expert_backward, (back_rows, grad_expert_rows, back_in, back_out)
    )
    grad_back = lax.all_to_all(
        grad_rows.reshape(1, local_count, groups * CAP, D),
        "task",
        split_axis=2,
        concat_axis=0,
        tiled=True,
    )
    grad_spread = jnp.concatenate([grad_back.reshape(EXPERTS * CAP, D), zero_row], axis=0)[target]
    grad_normed = jnp.sum(grad_spread.reshape(row_count, TOPMAX, D).astype(jnp.float32), axis=1)
    grad_route = jnp.sum(hot_float * grad_gate[:, :, None], axis=1)
    grad_logits = route_probs * (
        grad_route - jnp.sum(route_probs * grad_route, axis=-1, keepdims=True)
    )
    grad_router = jnp.dot(normed.T, grad_logits, precision=highest)[None]
    grad_normed = grad_normed + jnp.dot(grad_logits, router[0].T, precision=highest)
    grad_mid, grad_gain_two, grad_bias_two = norm_back(
        mid_rows, norm_gain[1], norm_bias[1], grad_normed
    )
    grad_mid = (grad_out + grad_mid).reshape(image_count, SEQ, D)

    def back_one(running, operands):
        image_rows, grad_image_rows, packed, mixed_low, log_total = operands
        grad_image, part_qkv, part_proj, part_gain, part_bias = attention_backward(
            image_rows,
            grad_image_rows,
            packed,
            mixed_low,
            log_total,
            norm_gain,
            norm_bias,
            full_qkv,
            full_proj,
        )
        return (
            (
                running[0] + part_qkv,
                running[1] + part_proj,
                running[2] + part_gain,
                running[3] + part_bias,
            ),
            grad_image,
        )

    start_sums = (
        jnp.zeros((D, 3 * D), jnp.float32),
        jnp.zeros((D, D), jnp.float32),
        jnp.zeros((D,), jnp.float32),
        jnp.zeros((D,), jnp.float32),
    )
    (grad_qkv_w, grad_proj_w, grad_gain_one, grad_bias_one), grad_images = lax.scan(
        back_one, start_sums, (images, grad_mid, packed_all, mixed_all, totals_all)
    )
    grad_gain = jnp.stack([grad_gain_one, grad_gain_two])
    grad_bias = jnp.stack([grad_bias_one, grad_bias_two])
    grad_router, grad_gain, grad_bias = lax.psum((grad_router, grad_gain, grad_bias), "dp")
    grad_qkv_w, grad_proj_w, grad_gain, grad_bias = (
        lax.psum(grad_qkv_w.astype(jnp.bfloat16), "task").astype(jnp.float32),
        lax.psum(grad_proj_w.astype(jnp.bfloat16), "task").astype(jnp.float32),
        lax.psum(grad_gain.astype(jnp.bfloat16), "task").astype(jnp.float32),
        lax.psum(grad_bias.astype(jnp.bfloat16), "task").astype(jnp.float32),
    )
    grad_qkv_w, grad_proj_w, grad_in_w, grad_out_w = (
        lax.psum_scatter(grad_qkv_w, "dp", scatter_dimension=0, tiled=True),
        lax.psum_scatter(grad_proj_w, "dp", scatter_dimension=0, tiled=True),
        lax.psum_scatter(grad_in_w, "dp", scatter_dimension=1, tiled=True),
        lax.psum_scatter(grad_out_w, "dp", scatter_dimension=1, tiled=True),
    )
    return (
        activations,
        grad_images[None],
        grad_gain,
        grad_bias,
        grad_qkv_w,
        grad_proj_w,
        grad_router,
        grad_in_w,
        grad_out_w,
    )


def solution(mesh):
    in_specs = (
        P("task", "dp", None, None),
        P("task", "dp", None, None),
        P(),
        P(),
        P("dp", None),
        P("dp", None),
        P("task", None, None),
        P("task", "dp", None),
        P("task", "dp", None),
        P("task", "dp", None, None),
        P("task"),
    )
    out_specs = (
        P("task", "dp", None, None),
        P("task", "dp", None, None),
        P(),
        P(),
        P("dp", None),
        P("dp", None),
        P("task", None, None),
        P("task", "dp", None),
        P("task", "dp", None),
    )
    return jax.shard_map(local, mesh=mesh, in_specs=in_specs, out_specs=out_specs, check_vma=False)
```

profile of v0, /device:TPU:0, one launch (start us, length us, event | category | flops | bytes accessed | tf_op | source)
XLA Modules:
  0.0 1267.6 jit_solution(10805658162368401957)
XLA Ops:
  11.1 36.1 %all_gather.14 = bf16[384,1152]{1,0:T(8,128)(2,1)S(1)} all-gather(bf16[48,1152]{1,0:T(8,128)(2,1)S(1)} %copy-done.46), channel_id=1, replica_groups=mesh['task'=4,'dp'=8] {'dp'}, dimensions={0}, use_global_device_ids=true | all-gather | bytes 995328 | tf_op jit(solution)/shard_map/all_gather | solution.py:188
  58.2 19.2 %while.75 = (s32[]{:T(128)}, bf16[2,512,6,64]{1,3,2,0:T(8,128)(2,1)}, f32[2,6,512,1]{2,1,3,0:T(8,128)}, bf16[2,512,6,64]{1,3,2,0:T(8,128)(2,1)S(1)}, bf16[1024,6...) while((s32[]{:T(128)}, bf16[2,512,6,64]{1,3,2,0:T(8,128)(2,1)}, ...), condition=%wide.region_5.0_spmd, body=%wide.region_2.5_spmd.sunk | while | flops 833614848 | bytes 46903948 | solution.py:64
  80.2 31.7 %all_gather.15 = bf16[384,384]{1,0:T(8,128)(2,1)S(1)} all-gather(bf16[48,384]{1,0:T(8,128)(2,1)S(1)} %copy-done.67), channel_id=1, replica_groups=mesh['task'=4,'dp'=8] {'dp'}, dimensions={0}, use_global_device_ids=true | all-gather | bytes 331776 | tf_op jit(solution)/shard_map/all_gather | solution.py:189
  119.6 6.0 reshape.399
  125.8 4.6 reduce-window.6
  132.7 20.9 %scatter_custom_fusion = bf16[5120,384]{1,0:T(8,128)(2,1)} fusion(s32[4096]{0:T(1024)S(1)} %bitcast.314, bf16[4096,384]{1,0:T(8,128)(2,1)} %reshape.399, bf16[]{:T(256)} %constant.245.clone.1), kind=kCustom, calls=%fused_computation.163 | custom fusion | bytes 3932672 | tf_op jit(solution)/shard_map/scatter | solution.py:222
  153.6 5.3 all-to-all-start
  162.1 5.1 mul.340
  167.2 7.7 mul.341
  174.9 22.9 %scatter_custom_fusion.1 = bf16[5120,384]{1,0:T(8,128)(2,1)} fusion(s32[4096]{0:T(1024)S(1)} %bitcast.315, f32[4096,384]{1,0:T(8,128)} %mul.341, f32[4096]{0:T(1024)S(1)} %mul.338, bf16[]{:T(256)} %constant.245.clone.1), kind=kCustom, calls=%fused_computation.157 | custom fusion | flops 3145728 | bytes 10240002 | tf_op jit(solution)/shard_map/scatter | solution.py:243
  197.8 6.5 all-to-all-done
  204.3 4.8 all-to-all-start.2
  209.1 4.4 copy.181
  213.5 41.0 %all-to-all-done.2 = bf16[4,4,320,384]{3,2,1,0:T(8,128)(2,1)} async-done(((bf16[4,4,320,384]{3,2,1,0:T(8,128)(2,1)}), bf16[4,4,320,384]{3,2,1,0:T(8,128)(2,1)}, u32[]{:S(2)}, u32[]{:S(2)}) %all-to-all-start.2) | async-done | bytes 3932192 | tf_op jit(solution)/shard_map/all_to_all | solution.py:245
  254.5 4.4 copy.188
  261.3 87.6 %while.76 = (s32[]{:T(128)}, bf16[4,1280,384]{2,1,0:T(8,128)(2,1)}, bf16[4,1280,384]{2,1,0:T(8,128)(2,1)}, bf16[4,384,1536]{2,1,0:T(8,128)(2,1)}, bf16[4,1536,384]{2,1,0:T(8,128)(2,1)}, /*index=5*/s32[]{:T(128)}) while((s32[]{:T(128)}, bf16[4,1280,384]{2,1,0:T(8,128)(2,1)}, bf16[4,1280,384]{2,1,0:T(8,128)(2,1)}, ...), condition=%wide.region_16.17_spmd, body=%wide.region_15.16_spmd.sunk | while | flops 3148185600 | bytes 4327493 | solution.py:226
  261.4 21.8 %fusion.221 = bf16[4,1280,384]{2,1,0:T(8,128)(2,1)} fusion(bf16[4,1280,384]{2,1,0:T(8,128)(2,1)} %get-tuple-element.774, s32[]{:T(128)} %get-tuple-element.773, bf16[4,1536,384]{2,1,0:T(8,128)(2,1)} %get-tuple-element.783, bf16[4,384,1536]{2,1,0:T(8,128)(2,1)} %get-tuple-element.782, bf16[4,1280,384]{2,1,0:T(8,128)(2,1)} %get-tuple-element.781), kind=kOutput, calls=%fused_computation.38.clone.1 | convolution fusion | flops 3148185600 | bytes 4327424 | tf_op jit(solution)/shard_map/while/body/eval_jaxpr/dot_general | solution.py:148
  283.3 21.8 %fusion.221 = bf16[4,1280,384]{2,1,0:T(8,128)(2,1)} fusion(bf16[4,1280,384]{2,1,0:T(8,128)(2,1)} %get-tuple-element.774, s32[]{:T(128)} %get-tuple-element.773, bf16[4,1536,384]{2,1,0:T(8,128)(2,1)} %get-tuple-element.783, bf16[4,384,1536]{2,1,0:T(8,128)(2,1)} %get-tuple-element.782, bf16[4,1280,384]{2,1,0:T(8,128)(2,1)} %get-tuple-element.781), kind=kOutput, calls=%fused_computation.38.clone.1 | convolution fusion | flops 3148185600 | bytes 4327424 | tf_op jit(solution)/shard_map/while/body/eval_jaxpr/dot_general | solution.py:148
  305.0 21.8 %fusion.221 = bf16[4,1280,384]{2,1,0:T(8,128)(2,1)} fusion(bf16[4,1280,384]{2,1,0:T(8,128)(2,1)} %get-tuple-element.774, s32[]{:T(128)} %get-tuple-element.773, bf16[4,1536,384]{2,1,0:T(8,128)(2,1)} %get-tuple-element.783, bf16[4,384,1536]{2,1,0:T(8,128)(2,1)} %get-tuple-element.782, bf16[4,1280,384]{2,1,0:T(8,128)(2,1)} %get-tuple-element.781), kind=kOutput, calls=%fused_computation.38.clone.1 | convolution fusion | flops 3148185600 | bytes 4327424 | tf_op jit(solution)/shard_map/while/body/eval_jaxpr/dot_general | solution.py:148
  326.8 21.7 %fusion.221 = bf16[4,1280,384]{2,1,0:T(8,128)(2,1)} fusion(bf16[4,1280,384]{2,1,0:T(8,128)(2,1)} %get-tuple-element.774, s32[]{:T(128)} %get-tuple-element.773, bf16[4,1536,384]{2,1,0:T(8,128)(2,1)} %get-tuple-element.783, bf16[4,384,1536]{2,1,0:T(8,128)(2,1)} %get-tuple-element.782, bf16[4,1280,384]{2,1,0:T(8,128)(2,1)} %get-tuple-element.781), kind=kOutput, calls=%fused_computation.38.clone.1 | convolution fusion | flops 3148185600 | bytes 4327424 | tf_op jit(solution)/shard_map/while/body/eval_jaxpr/dot_general | solution.py:148
  348.9 15.3 %copy.231 = bf16[4,1280,384]{2,0,1:T(4,128)(2,1)} copy(bf16[4,1280,384]{2,1,0:T(8,128)(2,1)} %get-tuple-element.238) | data formatting | bytes 7864320 | tf_op jit(solution)/shard_map/while | solution.py:226
  364.2 4.9 all-to-all-start.1
  371.4 147.5 %while.77 = (s32[]{:T(128)}, f32[4,384,1536]{2,1,0:T(8,128)}, f32[4,1536,384]{2,1,0:T(8,128)}, bf16[4,1280,384]{2,1,0:T(8,128)(2,1)}, bf16[4,1280,384]{2,1,0:T(8...) while((s32[]{:T(128)}, f32[4,384,1536]{2,1,0:T(8,128)}, ...), condition=%wide.region_20.21_spmd, body=%wide.region_19.20_spmd.sunk | while | flops 7705559040 | bytes 87889016 | solution.py:260
  371.4 18.6 %fusion.229 = (f32[1280,1536]{1,0:T(8,128)S(1)}, f32[1280,1536]{1,0:T(8,128)S(1)}) fusion(bf16[4,384,1536]{2,1,0:T(8,128)(2,1)} %get-tuple-element.763, s32[]{:T(128)} %get-tuple-element.749, bf16[4,1280,384]{2,1,0:T(8,128)(2,1)} %get-tuple-element.762), kind=kOutput, calls=%fused_computation.77.clone.1 | convolution fusion | flops 1631846400 | bytes 17892352 | tf_op jit(solution)/shard_map/while/body/eval_jaxpr/dot_general | solution.py:155
  393.9 5.6 add_convert_fusion.5
  403.8 4.5 fusion.232
  408.3 18.6 %fusion.229 = (f32[1280,1536]{1,0:T(8,128)S(1)}, f32[1280,1536]{1,0:T(8,128)S(1)}) fusion(bf16[4,384,1536]{2,1,0:T(8,128)(2,1)} %get-tuple-element.763, s32[]{:T(128)} %get-tuple-element.749, bf16[4,1280,384]{2,1,0:T(8,128)(2,1)} %get-tuple-element.762), kind=kOutput, calls=%fused_computation.77.clone.1 | convolution fusion | flops 1631846400 | bytes 17892352 | tf_op jit(solution)/shard_map/while/body/eval_jaxpr/dot_general | solution.py:155
  430.7 5.6 add_convert_fusion.5
  440.6 4.5 fusion.232
  445.1 18.6 %fusion.229 = (f32[1280,1536]{1,0:T(8,128)S(1)}, f32[1280,1536]{1,0:T(8,128)S(1)}) fusion(bf16[4,384,1536]{2,1,0:T(8,128)(2,1)} %get-tuple-element.763, s32[]{:T(128)} %get-tuple-element.749, bf16[4,1280,384]{2,1,0:T(8,128)(2,1)} %get-tuple-element.762), kind=kOutput, calls=%fused_computation.77.clone.1 | convolution fusion | flops 1631846400 | bytes 17892352 | tf_op jit(solution)/shard_map/while/body/eval_jaxpr/dot_general | solution.py:155
  467.5 5.6 add_convert_fusion.5
  477.5 4.5 fusion.232
  482.0 18.6 %fusion.229 = (f32[1280,1536]{1,0:T(8,128)S(1)}, f32[1280,1536]{1,0:T(8,128)S(1)}) fusion(bf16[4,384,1536]{2,1,0:T(8,128)(2,1)} %get-tuple-element.763, s32[]{:T(128)} %get-tuple-element.749, bf16[4,1280,384]{2,1,0:T(8,128)(2,1)} %get-tuple-element.762), kind=kOutput, calls=%fused_computation.77.clone.1 | convolution fusion | flops 1631846400 | bytes 17892352 | tf_op jit(solution)/shard_map/while/body/eval_jaxpr/dot_general | solution.py:155
  504.4 5.6 add_convert_fusion.5
  514.4 4.5 fusion.232
  518.9 15.5 %copy.230 = bf16[4,1280,384]{2,0,1:T(4,128)(2,1)} copy(bf16[4,1280,384]{2,1,0:T(8,128)(2,1)} %get-tuple-element.239) | data formatting | bytes 7864320 | tf_op jit(solution)/shard_map/while | solution.py:260
  534.4 4.9 all-to-all-start.3
  546.1 19.4 %gather_fusion = bf16[4096,384]{1,0:T(8,128)(2,1)} fusion(bf16[5121,384]{1,0:T(8,128)(2,1)} %concatenate.6, s32[4096]{0:T(1024)S(1)} %broadcast_clamp_fusion), kind=kCustom, calls=%fused_computation | custom fusion | bytes 6307840 | tf_op jit(solution)/shard_map/gather | solution.py:235
  565.5 6.7 reshape.377
  572.2 14.9 %multiply_reduce_fusion.2 = (f32[1024,4]{1,0:T(8,128)}, f32[1024,384]{1,0:T(8,128)}) fusion(f32[1024,4,384]{2,1,0:T(4,128)} %reshape.377, f32[1024,384]{1,0:T(8,128)S(1)} %bitcast.300, f32[1024,4]{1,0:T(8,128)} %copy-done.21), kind=kLoop, calls=%fused_computation.150 | loop fusion | flops 5894144 | bytes 9469952 | tf_op jit(solution)/shard_map/reduce_sum | solution.py:240
  593.7 19.4 %gather_fusion.1 = bf16[4096,384]{1,0:T(8,128)(2,1)} fusion(bf16[5121,384]{1,0:T(8,128)(2,1)} %concatenate.7, s32[4096]{0:T(1024)S(1)} %broadcast_clamp_fusion), kind=kCustom, calls=%fused_computation.1 | custom fusion | bytes 6307840 | tf_op jit(solution)/shard_map/gather | solution.py:270
  613.0 6.9 reshape.378
  620.0 7.8 reduce_sum.236
  630.9 5.1 multiply_reduce_fusion.4
  654.6 88.7 %while.78 = (s32[]{:T(128)}, f32[1024,6,64]{0,2,1:T(8,128)S(1)}, f32[1024,6,64]{0,2,1:T(8,128)}, bf16[2,512,6,64]{1,0,3,2:T(2,128)(2,1)}, bf16[2,512,6,64]{1,3,2...) while((s32[]{:T(128)}, f32[1024,6,64]{0,2,1:T(8,128)S(1)}, ...), condition=%wide.region_29.30_spmd.clone, body=%wide.region_27.29_spmd.clone.sunk | while | flops 2053370880 | bytes 210458864 | solution.py:124
  658.6 4.9 multiply_reduce_fusion.16
  663.5 4.7 multiply_convert_fusion.12
  668.2 4.8 fusion.243
  673.6 14.1 %dynamic_update_slice.60 = bf16[2,512,6,64]{1,0,3,2:T(2,128)(2,1)} dynamic-update-slice(bf16[2,512,6,64]{1,0,3,2:T(2,128)(2,1)} %get-tuple-element.799, bf16[1,512,6,64]{1,0,3,2:T(2,128)(2,1)S(1)} %copy.233, s32[]{:T(128)} %get-tuple-element.796, s32[]{:T(128)} %constant.225.clone.1..sunk, s32[]{:T(128)} %constant.225.clone.1..sunk, s32[]{:T(128)} %constant.225.clone.1..sunk) | dynamic-update-slice | bytes 786436 | tf_op jit(solution)/shard_map/while/body/eval_jaxpr/while/body/jit(dynamic_update_index_in_dim)/dynamic_update_slice | solution.py:64
  687.7 4.4 bitcast_add_fusion.6
  694.2 4.7 bitcast_add_fusion.7
  702.5 4.9 multiply_reduce_fusion.16
  707.4 4.7 multiply_convert_fusion.12
  712.1 4.8 fusion.243
  717.6 14.1 %dynamic_update_slice.60 = bf16[2,512,6,64]{1,0,3,2:T(2,128)(2,1)} dynamic-update-slice(bf16[2,512,6,64]{1,0,3,2:T(2,128)(2,1)} %get-tuple-element.799, bf16[1,512,6,64]{1,0,3,2:T(2,128)(2,1)S(1)} %copy.233, s32[]{:T(128)} %get-tuple-element.796, s32[]{:T(128)} %constant.225.clone.1..sunk, s32[]{:T(128)} %constant.225.clone.1..sunk, s32[]{:T(128)} %constant.225.clone.1..sunk) | dynamic-update-slice | bytes 786436 | tf_op jit(solution)/shard_map/while/body/eval_jaxpr/while/body/jit(dynamic_update_index_in_dim)/dynamic_update_slice | solution.py:64
  731.6 4.4 bitcast_add_fusion.6
  738.1 5.2 bitcast_add_fusion.7
  753.0 39.0 %all-reduce.7.cloned.1.call-done = (bf16[384,1152]{1,0:T(8,128)(2,1)}, bf16[384,384]{1,0:T(8,128)(2,1)}) async-done(((bf16[384,1152]{1,0:T(8,128)(2,1)}, bf16[384,384]{1,0:T(8,128)(2,1)}), (bf16[384,1152]{1,0:T(8,128)(2,1)}, bf16[384,384]{1,0:T(8,128)(2,1)})) %all-reduce.7.cloned.1.call-update) | async-done | bytes 1179664 | tf_op jit(solution)/shard_map/psum | solution.py:319
  798.2 4.5 fusion.164
  811.6 37.8 %all-reduce.2 = (bf16[2,384]{1,0:T(2,128)(2,1)S(1)}, bf16[2,384]{1,0:T(2,128)(2,1)S(1)}, f32[1,384,16]{1,2,0:T(8,128)}) all-reduce(f32[2,384]{1,0:T(2,128)S(1)} %pad_maximum_fusion, f32[2,384]{1,0:T(2,128)S(1)} %pad_maximum_fusion.1, f32[1,384,16]{1,2,0:T(8,128)S(1)} %convolution_bitcast_fusion.1), channel_id=1, replica_groups=mesh['task'=4,'dp'=8] {'dp'}, use_global_device_ids=true, to_apply=%region_34.35 | all-reduce | flops 7680 | bytes 58368 | tf_op jit(solution)/shard_map/psum | solution.py:317
  849.4 6.0 all-reduce.3
  865.5 61.9 %reduce-scatter.5.cloned.1.call-done = f32[48,1152]{1,0:T(8,128)} async-done(((f32[384,1152]{1,0:T(8,128)}), f32[48,1152]{1,0:T(8,128)}) %reduce-scatter.5.cloned.1.call-update) | async-done | bytes 221200 | tf_op jit(solution)/shard_map/reduce_scatter | solution.py:325
  927.4 166.3 %reduce-scatter.11.cloned.1.call-done = f32[4,192,384]{2,1,0:T(8,128)} async-done(((f32[4,1536,384]{2,1,0:T(8,128)}), f32[4,192,384]{2,1,0:T(8,128)}) %reduce-scatter.11.cloned.1.call-update) | async-done | bytes 1179664 | tf_op jit(solution)/shard_map/reduce_scatter | solution.py:328
  1093.8 166.8 %reduce-scatter.9.cloned.1.call-done = f32[4,48,1536]{2,1,0:T(8,128)} async-done(((f32[4,384,1536]{2,1,0:T(8,128)}), f32[4,48,1536]{2,1,0:T(8,128)}) %reduce-scatter.9.cloned.1.call-update) | async-done | bytes 1179664 | tf_op jit(solution)/shard_map/reduce_scatter | solution.py:327
  (314 shorter events, 168.4 us)
Async XLA Ops:
  7.2 151.8 %copy-start = (f32[1,384,16]{1,2,0:T(8,128)S(1)}, f32[1,384,16]{1,2,0:T(8,128)}, u32[]{:S(2)}) copy-start(f32[1,384,16]{1,2,0:T(8,128)} %param.25) | copy-start | bytes 73732
  7.2 40.0 %copy-start.77 = (f32[2,384]{1,0:T(2,128)S(1)}, f32[2,384]{1,0:T(2,128)}, u32[]{:S(2)}) copy-start(f32[2,384]{1,0:T(2,128)} %param.21) | copy-start | bytes 9220
  7.2 40.0 %copy-start.76 = (f32[2,384]{1,0:T(2,128)S(1)}, f32[2,384]{1,0:T(2,128)}, u32[]{:S(2)}) copy-start(f32[2,384]{1,0:T(2,128)} %param.22) | copy-start | bytes 9220
  7.2 251.7 %all-gather.3.cloned.1.call-start = ((), (), s32[]{:S(2)}) async-start(), calls=%async_computation.8 | async-start | bytes 5308416 | tf_op jit(solution)/shard_map/all_gather | solution.py:190
  8.0 251.0 %all-gather.5.cloned.1.call-start = ((), (), s32[]{:S(2)}) async-start(), calls=%async_computation.9 | async-start | bytes 5308416 | tf_op jit(solution)/shard_map/all_gather | solution.py:191
  10.6 40.6 %copy-start.9 = (f32[1,1,1024,384]{2,3,1,0:T(8,128)}, f32[1,1,1024,384]{2,3,1,0:T(8,128)S(1)}, u32[]{:S(2)}) copy-start(f32[1,1,1024,384]{2,3,1,0:T(8,128)S(1)} %copy.172) | copy-start | bytes 4718596
  10.9 40.4 %copy-start.47 = (f32[1024]{0:T(1024)}, f32[1024]{0:T(1024)S(1)}, u32[]{:S(2)}) copy-start(f32[1024]{0:T(1024)S(1)} %broadcast_multiply_fusion.3) | copy-start | bytes 12292
  11.1 40.2 %copy-start.61 = (f32[1024]{0:T(1024)}, f32[1024]{0:T(1024)S(1)}, u32[]{:S(2)}) copy-start(f32[1024]{0:T(1024)S(1)} %multiply_reduce_fusion.9) | copy-start | bytes 12292
  11.1 40.1 %copy-start.57 = (f32[1024]{0:T(1024)}, f32[1024]{0:T(1024)S(1)}, u32[]{:S(2)}) copy-start(f32[1024]{0:T(1024)S(1)} %fusion.157) | copy-start | bytes 12292
  47.3 111.6 %copy-start.49 = (f32[384]{0:T(512)}, f32[384]{0:T(512)S(1)}, u32[]{:S(2)}) copy-start(f32[384]{0:T(512)S(1)} %get-tuple-element.534) | copy-start | bytes 4612
  47.3 111.6 %copy-start.68 = (f32[384]{0:T(512)}, f32[384]{0:T(512)S(1)}, u32[]{:S(2)}) copy-start(f32[384]{0:T(512)S(1)} %get-tuple-element.447) | copy-start | bytes 4612
  58.2 21.9 %copy-start.67 = (bf16[48,384]{1,0:T(8,128)(2,1)S(1)}, bf16[48,384]{1,0:T(8,128)(2,1)}, u32[]{:S(2)}) copy-start(bf16[48,384]{1,0:T(8,128)(2,1)} %param.24) | copy-start | bytes 110596
  77.4 34.4 %copy-start.8 = (bf16[2,512,6,64]{1,3,2,0:T(8,128)(2,1)}, bf16[2,512,6,64]{1,3,2,0:T(8,128)(2,1)S(1)}, u32[]{:S(2)}) copy-start(bf16[2,512,6,64]{1,3,2,0:T(8,128)(2,1)S(1)} %get-tuple-element.829) | copy-start | bytes 2359300
  77.4 34.4 %copy-start.11 = (bf16[1024,6,64]{0,2,1:T(8,128)(2,1)}, bf16[1024,6,64]{0,2,1:T(8,128)(2,1)S(1)}, u32[]{:S(2)}) copy-start(bf16[1024,6,64]{0,2,1:T(8,128)(2,1)S(1)} %get-tuple-element.830) | copy-start | bytes 2359300
  77.4 37.8 %copy-start.3 = (bf16[1024,6,64]{0,2,1:T(8,128)(2,1)}, bf16[1024,6,64]{0,2,1:T(8,128)(2,1)S(1)}, u32[]{:S(2)}) copy-start(bf16[1024,6,64]{0,2,1:T(8,128)(2,1)S(1)} %get-tuple-element.828) | copy-start | bytes 2359300
  77.4 37.5 %copy-start.38 = (s32[1,1,1024,4]{2,3,1,0:T(4,128)S(1)}, s32[1,1,1024,4]{2,3,1,0:T(4,128)}, u32[]{:S(2)}) copy-start(s32[1,1,1024,4]{2,3,1,0:T(4,128)} %param.28) | copy-start | bytes 49156
  80.2 34.8 %copy-start.22 = (bf16[48,8,2,512]{3,1,2,0:T(8,128)(2,1)}, bf16[48,8,2,512]{3,1,2,0:T(8,128)(2,1)S(1)}, u32[]{:S(2)}) copy-start(bf16[48,8,2,512]{3,1,2,0:T(8,128)(2,1)S(1)} %copy.225) | copy-start | bytes 2359300
  114.0 44.9 %copy-start.5 = (f32[1024,384]{0,1:T(8,128)}, f32[1024,384]{0,1:T(8,128)S(1)}, u32[]{:S(2)}) copy-start(f32[1024,384]{0,1:T(8,128)S(1)} %get-tuple-element.527) | copy-start | bytes 4718596
  114.0 44.9 %copy-start.40 = (f32[1024]{0:T(1024)}, f32[1024]{0:T(1024)S(1)}, u32[]{:S(2)}) copy-start(f32[1024]{0:T(1024)S(1)} %broadcast_multiply_fusion.2) | copy-start | bytes 12292
  115.0 45.8 %copy-start.74 = (pred[4]{0:T(512)(128)(4,1)}, pred[4]{0:T(512)(128)(4,1)S(1)}, u32[]{:S(2)}) copy-start(pred[4]{0:T(512)(128)(4,1)S(1)} %iota_compare_fusion.3) | copy-start | bytes 16
  116.5 42.4 %copy-start.43 = (f32[1024]{0:T(1024)}, f32[1024]{0:T(1024)S(1)}, u32[]{:S(2)}) copy-start(f32[1024]{0:T(1024)S(1)} %fusion.158) | copy-start | bytes 12292
  153.6 50.7 %all-to-all-start = ((bf16[4,4,320,384]{3,2,1,0:T(8,128)(2,1)}), bf16[4,4,320,384]{3,2,1,0:T(8,128)(2,1)}, u32[]{:S(2)}, u32[]{:S(2)}) async-start(bf16[4,4,320,384]{3,2,1,0:T(8,128)(2,1)} %bitcast.295), calls=%async_computation | async-start | bytes 7864320 | tf_op jit(solution)/shard_map/all_to_all | solution.py:224
  160.2 14.8 %copy-start.52 = (f32[1024]{0:T(1024)}, f32[1024]{0:T(1024)S(1)}, u32[]{:S(2)}) copy-start(f32[1024]{0:T(1024)S(1)} %get-tuple-element.528) | copy-start | bytes 12292
  161.8 13.1 %copy-start.21 = (f32[1024,4]{1,0:T(8,128)}, f32[1024,4]{1,0:T(8,128)S(1)}, u32[]{:S(2)}) copy-start(f32[1024,4]{1,0:T(8,128)S(1)} %copy.176) | copy-start | bytes 49156
  204.3 50.2 %all-to-all-start.2 = ((bf16[4,4,320,384]{3,2,1,0:T(8,128)(2,1)}), bf16[4,4,320,384]{3,2,1,0:T(8,128)(2,1)}, u32[]{:S(2)}, u32[]{:S(2)}) async-start(bf16[4,4,320,384]{3,2,1,0:T(8,128)(2,1)} %bitcast.296), calls=%async_computation.2 | async-start | bytes 7864320 | tf_op jit(solution)/shard_map/all_to_all | solution.py:245
  364.2 170.2 %all-to-all-start.1 = ((bf16[1,4,1280,384]{3,1,0,2:T(4,128)(2,1)}), bf16[1,4,1280,384]{3,1,0,2:T(4,128)(2,1)}, u32[]{:S(2)}, u32[]{:S(2)}) async-start(bf16[1,4,1280,384]{3,1,0,2:T(4,128)(2,1)} %bitcast.293), calls=%async_computation.1 | async-start | bytes 7864320 | tf_op jit(solution)/shard_map/all_to_all | solution.py:227
  371.4 18.6 %copy-start.14 = (bf16[4,1280,384]{2,1,0:T(8,128)(2,1)S(1)}, bf16[4,1280,384]{2,1,0:T(8,128)(2,1)}, u32[]{:S(2)}) copy-start(bf16[4,1280,384]{2,1,0:T(8,128)(2,1)} %get-tuple-element.764) | copy-start | bytes 11796484 | tf_op jit(solution)/shard_map/while
  408.3 18.6 %copy-start.14 = (bf16[4,1280,384]{2,1,0:T(8,128)(2,1)S(1)}, bf16[4,1280,384]{2,1,0:T(8,128)(2,1)}, u32[]{:S(2)}) copy-start(bf16[4,1280,384]{2,1,0:T(8,128)(2,1)} %get-tuple-element.764) | copy-start | bytes 11796484 | tf_op jit(solution)/shard_map/while
  445.1 18.6 %copy-start.14 = (bf16[4,1280,384]{2,1,0:T(8,128)(2,1)S(1)}, bf16[4,1280,384]{2,1,0:T(8,128)(2,1)}, u32[]{:S(2)}) copy-start(bf16[4,1280,384]{2,1,0:T(8,128)(2,1)} %get-tuple-element.764) | copy-start | bytes 11796484 | tf_op jit(solution)/shard_map/while
  482.0 18.6 %copy-start.14 = (bf16[4,1280,384]{2,1,0:T(8,128)(2,1)S(1)}, bf16[4,1280,384]{2,1,0:T(8,128)(2,1)}, u32[]{:S(2)}) copy-start(bf16[4,1280,384]{2,1,0:T(8,128)(2,1)} %get-tuple-element.764) | copy-start | bytes 11796484 | tf_op jit(solution)/shard_map/while
  534.4 54.2 %all-to-all-start.3 = ((bf16[1,4,1280,384]{3,1,0,2:T(4,128)(2,1)}), bf16[1,4,1280,384]{3,1,0,2:T(4,128)(2,1)}, u32[]{:S(2)}, u32[]{:S(2)}) async-start(bf16[1,4,1280,384]{3,1,0,2:T(4,128)(2,1)} %bitcast.294), calls=%async_computation.3 | async-start | bytes 7864320 | tf_op jit(solution)/shard_map/all_to_all | solution.py:263
  539.3 252.7 %all-reduce.7.cloned.1.call-start = ((), (), s32[]{:S(2)}) async-start(), calls=%async_computation.14 | async-start | bytes 2359296 | tf_op jit(solution)/shard_map/psum | solution.py:319
  572.2 16.2 %copy-start.39 = (s32[1,1,1024,4]{2,3,1,0:T(4,128)S(1)}, s32[1,1,1024,4]{2,3,1,0:T(4,128)}, u32[]{:S(2)}) copy-start(s32[1,1,1024,4]{2,3,1,0:T(4,128)} %param.28) | copy-start | bytes 49156
  572.2 16.2 %copy-start.75 = (pred[4]{0:T(512)(128)(4,1)S(1)}, pred[4]{0:T(512)(128)(4,1)}, u32[]{:S(2)}) copy-start(pred[4]{0:T(512)(128)(4,1)} %copy-done.74) | copy-start | bytes 16
  572.2 16.3 %copy-start.33 = (f32[1024,16]{0,1:T(8,128)S(1)}, f32[1024,16]{0,1:T(8,128)}, u32[]{:S(2)}) copy-start(f32[1024,16]{0,1:T(8,128)} %copy-done.32) | copy-start | bytes 196612
  572.2 16.3 %copy-start.53 = (f32[1024]{0:T(1024)S(1)}, f32[1024]{0:T(1024)}, u32[]{:S(2)}) copy-start(f32[1024]{0:T(1024)} %copy-done.52) | copy-start | bytes 12292
  572.2 16.3 %copy-start.66 = (f32[1024]{0:T(1024)S(1)}, f32[1024]{0:T(1024)}, u32[]{:S(2)}) copy-start(f32[1024]{0:T(1024)} %copy-done.65) | copy-start | bytes 12292
  588.5 42.3 %copy-start.30 = (f32[1024,16]{0,1:T(8,128)}, f32[1024,16]{0,1:T(8,128)S(1)}, u32[]{:S(2)}) copy-start(f32[1024,16]{0,1:T(8,128)S(1)} %multiply_reduce_fusion.10) | copy-start | bytes 196612
  588.6 42.2 %copy-start.55 = (f32[1024]{0:T(1024)}, f32[1024]{0:T(1024)S(1)}, u32[]{:S(2)}) copy-start(f32[1024]{0:T(1024)S(1)} %multiply_reduce_fusion.12) | copy-start | bytes 12292
  619.9 10.9 copy-start.6
  619.9 10.9 copy-start.28
  620.0 10.9 copy-start.41
  620.0 10.9 copy-start.44
  620.0 10.9 copy-start.50
  627.8 8.2 copy-start.64
  644.0 10.6 copy-start.4
  644.0 10.6 copy-start.12
  743.4 7.1 copy-start.48
  753.0 112.5 %reduce-scatter.7.cloned.1.call-start = ((), (), s32[]{:S(2)}) async-start(), calls=%async_computation.11 | async-start | bytes 663552 | tf_op jit(solution)/shard_map/reduce_scatter | solution.py:326
  793.9 133.5 %reduce-scatter.5.cloned.1.call-start = ((), (), s32[]{:S(2)}) async-start(), calls=%async_computation.10 | async-start | bytes 1990656 | tf_op jit(solution)/shard_map/reduce_scatter | solution.py:325
  796.4 297.3 %reduce-scatter.11.cloned.1.call-start = ((), (), s32[]{:S(2)}) async-start(), calls=%async_computation.13 | async-start | bytes 10616832 | tf_op jit(solution)/shard_map/reduce_scatter | solution.py:328
  797.0 463.5 %reduce-scatter.9.cloned.1.call-start = ((), (), s32[]{:S(2)}) async-start(), calls=%async_computation.12 | async-start | bytes 10616832 | tf_op jit(solution)/shard_map/reduce_scatter | solution.py:327
  798.2 7.8 copy-start.10
  802.7 7.1 copy-start.72
  802.7 7.1 copy-start.7
  802.8 7.1 copy-start.29
  802.8 7.1 copy-start.31
  802.8 7.1 copy-start.42
  802.8 7.1 copy-start.45
  802.8 7.1 copy-start.51
  802.8 7.1 copy-start.56
  802.8 7.1 copy-start.69
  806.0 50.6 %copy-start.60 = (f32[1024]{0:T(1024)S(1)}, f32[1024]{0:T(1024)}, u32[]{:S(2)}) copy-start(f32[1024]{0:T(1024)} %copy-done.59) | copy-start | bytes 12292
  856.6 7.3 copy-start.20
  (35 other events, 132.3 us)
Sparse Core Ops, SparseCore 0:
  10.3 91.4 all-gather.2
  103.9 78.5 all-gather.4
  753.1 38.8 all-reduce.6
  795.7 62.2 reduce-scatter.6
  862.3 65.0 reduce-scatter.4
  931.4 162.2 reduce-scatter.10
  1097.9 162.5 reduce-scatter.8
where the time goes:
time: 1280 us; the launch traced here: 1270 us
  waiting for transfers between devices  484 us (38%)
  matrix products  312 us (24%)
  local copies, waits for them, and re-layouts  234 us (18%)
  blocking collectives  112 us (9%)
  other arithmetic  88.4 us (7%)
  starting transfers between devices  20.2 us (2%)
  between operations  16.1 us (1%)
    reduce_scatter x1, waiting for transfers between devices, local(): lax.psum_scatter(grad_in_w, 'dp', scatter_dimension=1, tiled=True)  167 us
    reduce_scatter x1, waiting for transfers between devices, local(): lax.psum_scatter(grad_out_w, 'dp', scatter_dimension=1, tiled=True)  166 us
    dot_general x4, matrix products, expert_forward(): jnp.dot(hidden_units, weight_out, preferred_element_type=jnp.float32)  87 us
    dot_general x4, matrix products, expert_backward(): pre_act = jnp.dot(rows_in, weight_in, preferred_element_type=jnp.float32)  74.2 us
    reduce_scatter x1, waiting for transfers between devices, local(): lax.psum_scatter(grad_qkv_w, 'dp', scatter_dimension=0, tiled=True)  61.9 us
    all_to_all x1, waiting for transfers between devices, local(): lax.all_to_all(grad_buffer.reshape(groups, local_count, CAP, D), 'task',...  41 us
    psum x1, waiting for transfers between devices, local(): lax.psum(grad_qkv_w.astype(jnp.bfloat16), 'task').astype(jnp.float32)  39 us
    psum x1, blocking collectives, local(): lax.psum((grad_router, grad_gain, grad_bias), 'dp')  37.8 us
  transfers between devices with their start and end apart: 11, of which 6 were waited for; matrix products, arithmetic and copies ran while one was open for 28% of the time, Pallas kernels for 0%

commit v1 on v0

v1 whole, which is shorter than its diff:
```python
import functools

import jax
import jax.numpy as jnp
from jax import lax
from jax.experimental import pallas as pl
from jax.experimental.pallas import tpu as pltpu
from jax.sharding import PartitionSpec as P

D = 384
FF = 1536
HEADS = 6
HEAD_DIM = 64
PAIR = 2 * HEAD_DIM
TOPMAX = 4
SEQ = 1024
CAP = 320

f32 = jnp.float32
bf16 = jnp.bfloat16
HIGHEST = lax.Precision.HIGHEST
EPSILON = 1e-06
ROOT_HALF = 0.7071067811865476
NORMAL = 0.3989422804014327

FF_TILE = 512
ROW_TILE = 640
QUERY_FWD = 512
QUERY_BWD = 256
ROWS = 256

VMEM = pl.BlockSpec(memory_space=pltpu.VMEM)
SMEM = pl.BlockSpec(memory_space=pltpu.SMEM)


def shape(*dims, dtype=f32):
    return jax.ShapeDtypeStruct(dims, dtype)


def params(**more):
    return pltpu.CompilerParams(vmem_limit_bytes=60 * 2**20, **more)


def dot(a, b):
    return lax.dot_general(a, b, (((1,), (0,)), ((), ())), preferred_element_type=f32)


def dot_rt(a, b):
    return lax.dot_general(a, b, (((1,), (1,)), ((), ())), preferred_element_type=f32)


def dot_lt(a, b):
    return lax.dot_general(a, b, (((0,), (0,)), ((), ())), preferred_element_type=f32)


def rows_at(index, size):
    return pl.ds(pl.multiple_of(index * size, size), size)


def normalize(rows):
    centered = rows - jnp.mean(rows, axis=1, keepdims=True)
    scale = lax.rsqrt(jnp.mean(centered * centered, axis=1, keepdims=True) + EPSILON)
    return centered * scale, scale


def norm_back(rows, grad_rows, gain):
    unit, scale = normalize(rows)
    scaled = grad_rows * gain
    grad_in = scale * (
        scaled
        - jnp.mean(scaled, axis=1, keepdims=True)
        - unit * jnp.mean(scaled * unit, axis=1, keepdims=True)
    )
    grad_gain = jnp.sum(grad_rows * unit, axis=0, keepdims=True)
    return grad_in, grad_gain, jnp.sum(grad_rows, axis=0, keepdims=True), unit


def half_lanes(rows, half):
    lanes = lax.broadcasted_iota(jnp.int32, (rows, PAIR), 1)
    return (lanes < HEAD_DIM) if half == 0 else (lanes >= HEAD_DIM)


def attend(packed, mixed, totals):
    zero = jnp.array(0, bf16)

    def head_pair(pair, _):
        queries, keys, values = (rows_at(pair + part * (D // PAIR), PAIR) for part in range(3))
        key_rows, value_rows = packed[:, keys], packed[:, values]

        def block(index, _):
            rows = rows_at(index, QUERY_FWD)
            query_rows = packed[rows, queries] * jnp.array(HEAD_DIM**-0.5, bf16)
            outs, logs = [], []
            for half in range(2):
                own = jnp.where(half_lanes(QUERY_FWD, half), query_rows, zero)
                scores = dot_rt(own, key_rows)
                top = jnp.max(scores, axis=1, keepdims=True)
                weights = jnp.exp(scores - top)
                total = jnp.sum(weights, axis=1, keepdims=True)
                outs.append(dot(weights.astype(bf16), value_rows) * (1.0 / total))
                logs.append(top + jnp.log(total))
            mixed[rows, queries] = jnp.where(half_lanes(QUERY_FWD, 0), outs[0], outs[1]).astype(
                bf16
            )
            lanes = lax.broadcasted_iota(jnp.int32, (QUERY_FWD, 8), 1)
            totals[rows, :] = jnp.where(
                lanes == 2 * pair,
                logs[0],
                jnp.where(lanes == 2 * pair + 1, logs[1], totals[rows, :]),
            )
            return 0

        return lax.fori_loop(0, SEQ // QUERY_FWD, block, 0)

    lax.fori_loop(0, HEADS // 2, head_pair, 0)


def forward_kernel(
    top_count,
    image,
    gain,
    bias,
    w_qkv,
    w_proj,
    router,
    choices,
    mid,
    packed,
    mixed,
    logs,
    normed,
    slots,
    gates,
    probs,
    normed_first,
    totals,
):
    experts = router.shape[0]

    def first_norm(index, _):
        rows = rows_at(index, ROWS)
        unit, _ = normalize(image[rows, :])
        normed_first[rows, :] = (unit * gain[0:1, :] + bias[0:1, :]).astype(bf16)
        return 0

    lax.fori_loop(0, SEQ // ROWS, first_norm, 0)
    named = choices[...].T
    numbers = lax.broadcasted_iota(jnp.int32, (experts, SEQ), 0)
    used = jnp.zeros((experts, SEQ), f32)
    for choice in range(TOPMAX):
        hit = (named[choice : choice + 1, :] == numbers) & (choice < top_count[0])
        used = used + jnp.where(hit, 1.0, 0.0)
    earlier = lax.broadcasted_iota(jnp.int32, (SEQ, SEQ), 0) < lax.broadcasted_iota(
        jnp.int32, (SEQ, SEQ), 1
    )
    before = dot(used.astype(bf16), jnp.where(earlier, 1.0, 0.0).astype(bf16))
    slots[...] = jnp.where(used > 0, before, -1.0).astype(jnp.int32)
    packed[...] = dot(normed_first[...], w_qkv[...]).astype(bf16)
    totals[...] = jnp.zeros_like(totals)
    attend(packed, mixed, totals)
    logs[...] = totals[...].T

    def second_norm(index, _):
        rows = rows_at(index, ROWS)
        mid_rows = image[rows, :] + dot(mixed[rows, :], w_proj[...])
        mid[rows, :] = mid_rows
        unit, _ = normalize(mid_rows)
        normed_rows = unit * gain[1:2, :] + bias[1:2, :]
        normed[rows, :] = normed_rows.astype(bf16)
        logits = lax.dot_general(
            router[...],
            normed_rows,
            (((1,), (1,)), ((), ())),
            precision=HIGHEST,
            preferred_element_type=f32,
        )
        powers = jnp.exp(logits - jnp.max(logits, axis=0, keepdims=True))
        probs[:, rows] = powers / jnp.sum(powers, axis=0, keepdims=True)
        return 0

    lax.fori_loop(0, SEQ // ROWS, second_norm, 0)
    gates[...] = jnp.where(slots[...] >= 0, probs[...], 0.0)


def forward_part(top_count, image, gain, bias, w_qkv, w_proj, router, choices):
    experts = router.shape[0]
    return pl.pallas_call(
        forward_kernel,
        out_shape=(
            shape(SEQ, D),
            shape(SEQ, 3 * D, dtype=bf16),
            shape(SEQ, D, dtype=bf16),
            shape(8, SEQ),
            shape(SEQ, D, dtype=bf16),
            shape(experts, SEQ, dtype=jnp.int32),
            shape(experts, SEQ),
            shape(experts, SEQ),
        ),
        in_specs=[SMEM] + [VMEM] * 7,
        out_specs=[VMEM] * 8,
        scratch_shapes=[pltpu.VMEM((SEQ, D), bf16), pltpu.VMEM((SEQ, 8), f32)],
        compiler_params=params(),
    )(top_count, image, gain, bias, w_qkv, w_proj, router, choices)


def slot_hits(slots, source, expert):
    return lax.broadcasted_iota(jnp.int32, (CAP, SEQ), 0) == slots[source, pl.ds(expert, 1), :]


def ones_at(hits):
    return jnp.where(hits, 1.0, 0.0).astype(bf16)


def expert_kernel(
    normed,
    cotangent,
    slots,
    gates,
    w_in,
    w_out,
    grad_in,
    grad_out,
    mixes,
    grad_normed,
    grad_gates,
    rows_in,
    rows_grad,
    rows_cot,
    rows_gate,
    hidden,
    grad_pre,
    sent,
    columns,
):
    groups, local_count = normed.shape[0], w_in.shape[0]
    width = groups * CAP

    def one_expert(expert, _):
        for source in range(groups):
            own = slice(source * CAP, (source + 1) * CAP)
            hits = slot_hits(slots, source, expert)
            picks = ones_at(hits)
            rows_in[own, :] = dot(picks, normed[source]).astype(bf16)
            cot_rows = dot(picks, cotangent[source])
            gate = jnp.sum(
                jnp.where(hits, gates[source, pl.ds(expert, 1), :], 0.0), axis=1, keepdims=True
            )
            rows_cot[own, :] = cot_rows.astype(bf16)
            rows_grad[own, :] = (gate * cot_rows).astype(bf16)
            rows_gate[own, :] = jnp.broadcast_to(gate, (CAP, 128))

        def tile(index, _):
            units = rows_at(index // (width // ROW_TILE), FF_TILE)
            rows = rows_at(lax.rem(index, width // ROW_TILE), ROW_TILE)
            pre = dot(rows_in[rows, :], w_in[expert, :, units])
            grad_hidden = dot_rt(rows_grad[rows, :], w_out[expert, units, :])
            share = 0.5 * lax.erf(pre * ROOT_HALF) + 0.5
            slope = share + pre * (NORMAL * jnp.exp(-0.5 * pre * pre))
            hidden[rows, units] = (pre * share).astype(bf16)
            grad_pre[rows, units] = (grad_hidden * slope).astype(bf16)
            return 0

        lax.fori_loop(0, (FF // FF_TILE) * (width // ROW_TILE), tile, 0)
        for source in range(groups):
            own = slice(source * CAP, (source + 1) * CAP)
            kept = rows_at(expert, CAP)
            out_rows = dot(hidden[own, :], w_out[expert]).astype(bf16).astype(f32)
            sent[source, kept, :D] = (rows_gate[own, 0:1] * out_rows).astype(bf16)
            sent[source, kept, D:] = dot_rt(grad_pre[own, :], w_in[expert]).astype(bf16)
            grad_gate = jnp.sum(rows_cot[own, :].astype(f32) * out_rows, axis=1, keepdims=True)
            hits = slot_hits(slots, source, expert)
            grad_gates[source, pl.ds(expert, 1), :] = jnp.sum(
                jnp.where(hits, grad_gate, 0.0), axis=0, keepdims=True
            )
        grad_in[expert] = dot_lt(rows_in[...], grad_pre[...]).astype(bf16)
        grad_out[expert] = dot_lt(rows_grad[...], hidden[...]).astype(bf16).T
        return 0

    lax.fori_loop(0, local_count, one_expert, 0)
    for source in range(groups):
        columns[...] = slots[source].T

        def combine(index, _):
            rows = rows_at(index, 512)
            lanes = lax.broadcasted_iota(jnp.int32, (512, CAP), 1)
            picks = jnp.concatenate(
                [ones_at(lanes == columns[rows, e : e + 1]) for e in range(local_count)], axis=1
            )
            back = dot(picks, sent[source])
            mixes[source, rows, :] = back[:, :D].astype(bf16)
            grad_normed[source, rows, :] = back[:, D:].astype(bf16)
            return 0

        lax.fori_loop(0, SEQ // 512, combine, 0)


def expert_part(normed, cotangent, slots, gates, w_in, w_out):
    groups, local_count = normed.shape[0], w_in.shape[0]
    width = groups * CAP
    return pl.pallas_call(
        expert_kernel,
        out_shape=(
            shape(local_count, D, FF, dtype=bf16),
            shape(local_count, FF, D, dtype=bf16),
            shape(groups, SEQ, D, dtype=bf16),
            shape(groups, SEQ, D, dtype=bf16),
            shape(groups, local_count, SEQ),
        ),
        in_specs=[VMEM] * 6,
        out_specs=[VMEM] * 5,
        scratch_shapes=[
            pltpu.VMEM((width, D), bf16),
            pltpu.VMEM((width, D), bf16),
            pltpu.VMEM((width, D), bf16),
            pltpu.VMEM((width, 128), f32),
            pltpu.VMEM((width, FF), bf16),
            pltpu.VMEM((width, FF), bf16),
            pltpu.VMEM((groups, local_count * CAP, 2 * D), bf16),
            pltpu.VMEM((SEQ, local_count), jnp.int32),
        ],
        compiler_params=params(),
    )(normed, cotangent, slots, gates, w_in, w_out)


def attend_back(packed, grad_mixed, logs, grad_packed, grad_keys, grad_values):
    zero = jnp.array(0, bf16)

    def head_pair(pair, _):
        queries, keys, values = (rows_at(pair + part * (D // PAIR), PAIR) for part in range(3))
        key_rows, value_rows = packed[:, keys], packed[:, values]

        def block(index, _):
            rows = rows_at(index, QUERY_BWD)
            query_rows = packed[rows, queries] * jnp.array(HEAD_DIM**-0.5, bf16)
            grad_rows = grad_mixed[rows, queries]
            grad_query, part_keys, part_values = [], 0.0, 0.0
            for half in range(2):
                lanes = half_lanes(QUERY_BWD, half)
                own = jnp.where(lanes, query_rows, zero)
                own_grad = jnp.where(lanes, grad_rows, zero)
                probs = jnp.exp(dot_rt(key_rows, own) - logs[pl.ds(2 * pair + half, 1), rows])
                grad_probs = dot_rt(value_rows, own_grad)
                mean = jnp.sum(probs * grad_probs, axis=0, keepdims=True)
                grad_scores = (probs * (grad_probs - mean)).astype(bf16)
                part_values += dot(probs.astype(bf16), own_grad)
                part_keys += dot(grad_scores, own)
                grad_query.append(dot_lt(grad_scores, key_rows))
            grad_packed[rows, queries] = (
                jnp.where(half_lanes(QUERY_BWD, 0), grad_query[0], grad_query[1])
                * HEAD_DIM**-0.5
            ).astype(bf16)
            grad_keys[...] = jnp.where(index == 0, part_keys, grad_keys[...] + part_keys)
            grad_values[...] = jnp.where(index == 0, part_values, grad_values[...] + part_values)
            return 0

        lax.fori_loop(0, SEQ // QUERY_BWD, block, 0)
        grad_packed[:, keys] = grad_keys[...].astype(bf16)
        grad_packed[:, values] = grad_values[...].astype(bf16)
        return 0

    lax.fori_loop(0, HEADS // 2, head_pair, 0)


def backward_kernel(
    image,
    cotangent,
    gain,
    bias,
    mid,
    w_qkv,
    w_proj,
    router,
    packed,
    mixed,
    logs,
    mixes,
    grad_normed,
    grad_gates,
    probs,
    activations,
    grad_image,
    grad_norm,
    grad_router,
    grad_shared,
    grad_mid,
    grad_low,
    grad_mixed,
    grad_packed,
    grad_keys,
    grad_values,
    normed_first,
):
    groups = mixes.shape[0]
    route = grad_gates[...]
    grad_logits = probs[...] * (route - jnp.sum(probs[...] * route, axis=0, keepdims=True))
    grad_norm[...] = jnp.zeros_like(grad_norm)
    grad_router[...] = jnp.zeros_like(grad_router)
    for index in range(SEQ // ROWS):
        rows = slice(index * ROWS, (index + 1) * ROWS)
        mid_rows = mid[rows, :]
        mix_rows, grad_rows = mixes[0, rows, :].astype(f32), grad_normed[0, rows, :].astype(f32)
        for source in range(1, groups):
            mix_rows += mixes[source, rows, :].astype(f32)
            grad_rows += grad_normed[source, rows, :].astype(f32)
        activations[rows, :] = mid_rows + mix_rows
        own_logits = grad_logits[:, rows]
        grad_rows += lax.dot_general(
            own_logits,
            router[...],
            (((0,), (0,)), ((), ())),
            precision=HIGHEST,
            preferred_element_type=f32,
        )
        grad_in, grad_gain, grad_bias, unit = norm_back(mid_rows, grad_rows, gain[1:2, :])
        grad_router[...] += jnp.dot(
            own_logits,
            unit * gain[1:2, :] + bias[1:2, :],
            precision=HIGHEST,
            preferred_element_type=f32,
        )
        grad_norm[1:2, :] += grad_gain
        grad_norm[3:4, :] += grad_bias
        grad_mid_rows = cotangent[rows, :] + grad_in
        grad_mid[rows, :] = grad_mid_rows
        low_rows = grad_mid_rows.astype(bf16)
        grad_low[rows, :] = low_rows
        grad_mixed[rows, :] = dot_rt(low_rows, w_proj[...]).astype(bf16)
    grad_shared[:, 3 * D :] = dot_lt(mixed[...], grad_low[...]).astype(bf16)
    attend_back(packed, grad_mixed, logs, grad_packed, grad_keys, grad_values)

    def first_norm(index, _):
        rows = rows_at(index, ROWS)
        grad_rows = dot_rt(grad_packed[rows, :], w_qkv[...])
        grad_in, grad_gain, grad_bias, unit = norm_back(image[rows, :], grad_rows, gain[0:1, :])
        normed_first[rows, :] = (unit * gain[0:1, :] + bias[0:1, :]).astype(bf16)
        grad_image[rows, :] = grad_mid[rows, :] + grad_in
        grad_norm[0:1, :] += grad_gain
        grad_norm[2:3, :] += grad_bias
        return 0

    lax.fori_loop(0, SEQ // ROWS, first_norm, 0)
    grad_shared[:, : 3 * D] = dot_lt(normed_first[...], grad_packed[...]).astype(bf16)


def backward_part(*operands):
    router = operands[7]
    return pl.pallas_call(
        backward_kernel,
        out_shape=(
            shape(SEQ, D),
            shape(SEQ, D),
            shape(4, D),
            shape(router.shape[0], D),
            shape(D, 4 * D, dtype=bf16),
        ),
        in_specs=[VMEM] * 15,
        out_specs=[VMEM] * 5,
        scratch_shapes=[
            pltpu.VMEM((SEQ, D), f32),
            pltpu.VMEM((SEQ, D), bf16),
            pltpu.VMEM((SEQ, D), bf16),
            pltpu.VMEM((SEQ, 3 * D), bf16),
            pltpu.VMEM((SEQ, PAIR), f32),
            pltpu.VMEM((SEQ, PAIR), f32),
            pltpu.VMEM((SEQ, D), bf16),
        ],
        compiler_params=params(),
    )(*operands)


def local(
    layer_input,
    cotangent,
    norm_gain,
    norm_bias,
    w_qkv,
    w_proj,
    router,
    w_in,
    w_out,
    choices,
    top_count,
):
    groups = lax.axis_size("task")
    local_count = w_in.shape[0]
    full_qkv, full_proj, full_in, full_out = (
        lax.all_gather(w_qkv, "dp", axis=0, tiled=True),
        lax.all_gather(w_proj, "dp", axis=0, tiled=True),
        lax.all_gather(w_in, "dp", axis=1, tiled=True),
        lax.all_gather(w_out, "dp", axis=1, tiled=True),
    )
    image = layer_input.reshape(SEQ, D)
    grad_rows = cotangent.reshape(SEQ, D)
    router_rows = router[0].T
    experts = router_rows.shape[0]
    mid, packed, mixed, logs, normed, slots, gates, probs = forward_part(
        top_count,
        image,
        norm_gain,
        norm_bias,
        full_qkv,
        full_proj,
        router_rows,
        choices.reshape(SEQ, TOPMAX),
    )

    def swap(array):
        return lax.all_to_all(array, "task", split_axis=0, concat_axis=0, tiled=True)

    grad_in, grad_out, mixes, grad_normed, grad_gates = expert_part(
        lax.all_gather(normed, "task"),
        lax.all_gather(grad_rows.astype(bf16), "task"),
        swap(slots.reshape(groups, local_count, SEQ)),
        swap(gates.reshape(groups, local_count, SEQ)),
        full_in,
        full_out,
    )
    activations, grad_image, grad_norm, grad_router, grad_shared = backward_part(
        image,
        grad_rows,
        norm_gain,
        norm_bias,
        mid,
        full_qkv,
        full_proj,
        router_rows,
        packed,
        mixed,
        logs,
        swap(mixes),
        swap(grad_normed),
        swap(grad_gates).reshape(experts, SEQ),
        probs,
    )
    grad_in = lax.psum_scatter(grad_in, "dp", scatter_dimension=1, tiled=True)
    grad_out = lax.psum_scatter(grad_out, "dp", scatter_dimension=1, tiled=True)
    grad_shared = lax.psum_scatter(grad_shared, "dp", scatter_dimension=0, tiled=True)
    grad_shared = lax.psum(grad_shared, "task").astype(f32)
    grad_router = lax.psum(grad_router, "dp")
    grad_norm = lax.psum(grad_norm, ("task", "dp"))
    return (
        activations.reshape(layer_input.shape),
        grad_image.reshape(layer_input.shape),
        grad_norm[:2],
        grad_norm[2:],
        grad_shared[:, : 3 * D],
        grad_shared[:, 3 * D :],
        grad_router.T[None],
        grad_in.astype(f32),
        grad_out.astype(f32),
    )


def solution(mesh):
    tokens = P("task", "dp", None, None)
    rows = P("dp", None)
    blocks = P("task", "dp", None)
    routed = P("task", None, None)
    return jax.shard_map(
        local,
        mesh=mesh,
        in_specs=(tokens, tokens, P(), P(), rows, rows, routed, blocks, blocks, tokens, P("task")),
        out_specs=(tokens, tokens, P(), P(), rows, rows, routed, blocks, blocks),
        check_vma=False,
    )
```

time: 1280 us -> 821 us (0.64)
  matrix products: 312 us -> 0 us
  local copies, waits for them, and re-layouts: 234 us -> 9.28 us
  Pallas kernels: 0 us -> 152 us
  blocking collectives: 112 us -> 205 us
  other arithmetic: 88.4 us -> 6.77 us
  waiting for transfers between devices: 484 us -> 425 us
  starting transfers between devices: 20.2 us -> 7.3 us
    dot_general x47 -> x0, matrix products: 312 us -> none  [the longest x4 87 us: expert_forward(): jnp.dot(hidden_units, weight_out, preferred_element_type=jnp.float32)]
    reduce_scatter x4 -> x3, waiting for transfers between devices: 395 us -> 208 us  [the longest x1 97.2 us: local(): grad_in = lax.psum_scatter(grad_in, 'dp', scatter_dimension=1, tiled=True)]
    pallas_call x0 -> x3, Pallas kernels: none -> 152 us  [the longest x1 90.9 us: expert_part(): pl.pallas_call(expert_kernel, out_shape=(shape(local_count, D, FF, dtype=...]
    all_gather x1, waiting for transfers between devices: 0.01 us -> 82.1 us  [local(): lax.all_gather(w_in, 'dp', axis=1, tiled=True)]
    all_gather x1, waiting for transfers between devices: 0.01 us -> 80.1 us  [local(): lax.all_gather(w_out, 'dp', axis=1, tiled=True)]
    all_to_all x0 -> x3, blocking collectives: none -> 57.6 us  [swap(): lax.all_to_all(array, 'task', split_axis=0, concat_axis=0, tiled=True)]
    psum x1, waiting for transfers between devices: 39 us -> 0.01 us  [local(): grad_shared = lax.psum(grad_shared, 'task').astype(f32)]
    gather x2 -> x0, local copies, waits for them, and re-layouts: 38.7 us -> none  [the longest x1 19.4 us: local(): jnp.concatenate([grad_back.reshape(EXPERTS * CAP, D), zero_row], axis=0)]
  transfers between devices with their start and end apart: 11 -> 10, of which waited for: 6 -> 8; matrix products, arithmetic and copies ran while one was open for 28% -> 1% of each run, Pallas kernels for 0% -> 3%
where the time goes in v1:
time: 821 us; the launch traced here: 820 us
  waiting for transfers between devices  425 us (52%)
  blocking collectives  205 us (25%)
  Pallas kernels  152 us (19%)
  between operations  14.9 us (2%)
  local copies, waits for them, and re-layouts  9.28 us (1%)
    reduce_scatter x1, waiting for transfers between devices, local(): grad_in = lax.psum_scatter(grad_in, 'dp', scatter_dimension=1, tiled=True)  97.2 us
    pallas_call x1, Pallas kernels, expert_part(): pl.pallas_call(expert_kernel, out_shape=(shape(local_count, D, FF, dtype=...  90.9 us
    all_gather x1, waiting for transfers between devices, local(): lax.all_gather(w_in, 'dp', axis=1, tiled=True)  82.1 us
    all_gather x1, waiting for transfers between devices, local(): lax.all_gather(w_out, 'dp', axis=1, tiled=True)  80.1 us
    reduce_scatter x1, waiting for transfers between devices, local(): lax.psum_scatter(grad_shared, 'dp', scatter_dimension=0, tiled=True)  61.4 us
    all_to_all x3, blocking collectives, swap(): lax.all_to_all(array, 'task', split_axis=0, concat_axis=0, tiled=True)  57.6 us
    reduce_scatter x1, waiting for transfers between devices, local(): grad_out = lax.psum_scatter(grad_out, 'dp', scatter_dimension=1, tiled=True)  49.1 us
    psum x1, blocking collectives, local(): grad_norm = lax.psum(grad_norm, ('task', 'dp'))  40.1 us
  transfers between devices with their start and end apart: 10, of which 8 were waited for; matrix products, arithmetic and copies ran while one was open for 1% of the time, Pallas kernels for 3%

profile of v1, /device:TPU:0, one launch (start us, length us, event | category | flops | bytes accessed | tf_op | source)
XLA Modules:
  0.0 819.6 jit_solution(3445212610204496233)
XLA Ops:
  7.2 0.0 copy-start.5
  7.2 0.0 copy-start.3
  7.2 0.0 copy-start.2
  7.2 0.0 all-gather.13.cloned.1.call-start
  7.3 2.4 convert_element_type.22
  9.7 0.0 all-gather.13.cloned.1.call-update
  9.7 0.0 all-gather.11.cloned.1.call-start
  10.4 0.0 copy-done.5
  10.4 1.0 copy.22
  11.4 0.0 copy-done.3
  11.4 34.8 %all_gather.23.w_proj = bf16[384,384]{1,0:T(8,128)(2,1)} all-gather(bf16[48,384]{1,0:T(8,128)(2,1)S(1)} %copy-done.3), channel_id=1, replica_groups=mesh['task'=4,'dp'=8] {'dp'}, dimensions={0}, use_global_device_ids=true | all-gather | bytes 331776 | tf_op jit(solution)/shard_map/all_gather | solution.py:488
  46.2 0.0 copy-done.2
  46.2 34.1 %all_gather.22.w_qkv = bf16[384,1152]{1,0:T(8,128)(2,1)} all-gather(bf16[48,1152]{1,0:T(8,128)(2,1)S(1)} %copy-done.2), channel_id=1, replica_groups=mesh['task'=4,'dp'=8] {'dp'}, dimensions={0}, use_global_device_ids=true | all-gather | bytes 995328 | tf_op jit(solution)/shard_map/all_gather | solution.py:487
  80.3 22.8 %shard_map.178 = (f32[1024,384]{1,0:T(8,128)}, bf16[1024,1152]{1,0:T(8,128)(2,1)}, bf16[1024,384]{1,0:T(8,128)(2,1)}, f32[8,1024]{1,0:T(8,128)}, bf16[1024,384]{...) custom-call(s32[1]{0:T(128)S(6)} %copy.24.top_count, f32[1024,384]{1,0:T(8,128)} %bitcast.13, ...), custom_call_target="tpu_custom_call" | custom-call | tf_op jit(solution)/shard_map/pallas_call | solution.py:187
  103.1 0.0 all-gather.11.cloned.1.call-update
  103.2 0.0 all-gather.7.cloned.1.call-start
  103.2 0.7 all-gather.7.cloned.1.call-update
  103.9 0.0 all-gather.9.cloned.1.call-start
  103.9 0.5 all-gather.9.cloned.1.call-update
  104.5 1.5 reshape.56
  106.0 3.3 all-to-all-start
  109.3 0.9 reshape.57
  110.1 3.2 all-to-all-done.slots
  113.3 0.0 copy-start.1
  113.3 8.0 all_to_all.25.gates
  121.3 0.0 all-gather.13.cloned.1.call-done
  121.3 12.6 %all-gather.11.cloned.1.call-done = bf16[4096,384]{1,0:T(8,128)(2,1)} async-done(((bf16[1024,384]{1,0:T(8,128)(2,1)}), bf16[4096,384]{1,0:T(8,128)(2,1)}) %all-gather.11.cloned.1.call-update) | async-done | bytes 3145744 | tf_op jit(solution)/shard_map/all_gather | solution.py:511
  133.9 82.1 %all-gather.7.cloned.1.call-done.w_in = bf16[4,384,1536]{2,1,0:T(8,128)(2,1)} async-done(((bf16[4,48,1536]{2,1,0:T(8,128)(2,1)}), bf16[4,384,1536]{2,1,0:T(8,128)(2,1)}) %all-gather.7.cloned.1.call-update) | async-done | bytes 4718608 | tf_op jit(solution)/shard_map/all_gather | solution.py:489
  216.0 80.1 %all-gather.9.cloned.1.call-done.w_out = bf16[4,1536,384]{2,1,0:T(8,128)(2,1)} async-done(((bf16[4,192,384]{2,1,0:T(8,128)(2,1)}), bf16[4,1536,384]{2,1,0:T(8,128)(2,1)}) %all-gather.9.cloned.1.call-update) | async-done | bytes 4718608 | tf_op jit(solution)/shard_map/all_gather | solution.py:490
  296.2 0.0 copy-done.1
  296.2 90.9 %shard_map.179 = (bf16[4,384,1536]{2,1,0:T(8,128)(2,1)}, bf16[4,1536,384]{2,1,0:T(8,128)(2,1)}, bf16[4,1024,384]{2,1,0:T(8,128)(2,1)}, bf16[4,1024,384]{2,1,0:T(8,128)(2,1)}, f32[4,4,1024]{2,1,0:T(4,128)}) custom-call(bf16[4,1024,384]{2,1,0:T(8,128)(2,1)} %bitcast.17, bf16[4,1024,384]{2,1,0:T(8,128)(2,1)} %bitcast.16, s32[4,4,1024]{2,1,0:T(4,128)} %copy-done.1, ...), custom_call_target="tpu_custom_call" | custom-call | tf_op jit(solution)/shard_map/pallas_call | solution.py:300
  387.1 7.4 all_to_all.26
  394.5 42.2 %all_to_all.27.mixes = bf16[4,1024,384]{2,1,0:T(8,128)(2,1)} all-to-all(bf16[4,1024,384]{2,1,0:T(8,128)(2,1)} %get-tuple-element.34), channel_id=1, replica_groups=mesh['task'=4,'dp'=8] {'task'}, dimensions={0} | all-to-all | bytes 6291456 | tf_op jit(solution)/shard_map/all_to_all | solution.py:508
  436.7 3.7 all-to-all-start.3
  440.4 0.0 reduce-scatter.4.cloned.1.call-start
  440.5 0.7 reshape.58.grad_gates
  441.1 36.2 %all-to-all-done.3.grad_normed = bf16[4,1024,384]{2,1,0:T(8,128)(2,1)S(1)} async-done(((bf16[4,1024,384]{2,1,0:T(8,128)(2,1)}), bf16[4,1024,384]{2,1,0:T(8,128)(2,1)S(1)}, u32[]{:S(2)}, u32[]{:S(2)}) %all-to-all-start.3) | async-done | bytes 3145760 | tf_op jit(solution)/shard_map/all_to_all | solution.py:508
  477.3 0.0 copy-start
  477.3 1.6 copy-done
  479.0 38.0 %shard_map.180 = (f32[1024,384]{1,0:T(8,128)}, f32[1024,384]{1,0:T(8,128)}, f32[4,384]{1,0:T(4,128)}, f32[16,384]{1,0:T(8,128)}, bf16[384,1536]{1,0:T(8,128)(2,1)}) custom-call(f32[1024,384]{1,0:T(8,128)} %bitcast.14, f32[1024,384]{1,0:T(8,128)} %bitcast.15, f32[2,384]{1,0:T(2,128)} %gain.3, f32[2,384]{1,0:T(2,128)} %bias.3, ...), custom_call_target="tpu_custom_call" | custom-call | tf_op jit(solution)/shard_map/pallas_call | solution.py:447
  516.9 0.0 reduce-scatter.4.cloned.1.call-update
  516.9 0.0 all-reduce.2.cloned.1.call-start
  517.0 61.4 %reduce-scatter.4.cloned.1.call-done = bf16[48,1536]{1,0:T(8,128)(2,1)} async-done(((bf16[384,1536]{1,0:T(8,128)(2,1)}), bf16[48,1536]{1,0:T(8,128)(2,1)}) %reduce-scatter.4.cloned.1.call-update) | async-done | bytes 147472 | tf_op jit(solution)/shard_map/reduce_scatter | solution.py:537
  578.4 0.0 all-reduce.2.cloned.1.call-update
  578.4 0.0 reduce-scatter.8.cloned.1.call-start
  578.5 0.7 reduce-scatter.8.cloned.1.call-update
  579.2 0.0 copy-start.6
  579.2 0.0 copy-start.4
  579.2 0.0 reduce-scatter.6.cloned.1.call-start
  579.2 0.7 reduce-scatter.6.cloned.1.call-update
  579.9 0.0 copy-done.6
  579.9 40.1 %psum.21 = f32[4,384]{1,0:T(4,128)S(1)} all-reduce(f32[4,384]{1,0:T(4,128)S(1)} %copy-done.6), channel_id=1, replica_groups=mesh['task'=4,'dp'=8] {'task','dp'}, use_global_device_ids=true, to_apply=%region_0.0 | all-reduce | flops 1536 | bytes 12288 | tf_op jit(solution)/shard_map/psum | solution.py:540
  620.0 0.0 copy-done.4
  620.0 38.5 %psum.23 = f32[1,384,16]{1,2,0:T(8,128)} all-reduce(f32[1,384,16]{1,2,0:T(8,128)S(1)} %bitcast.21), channel_id=1, replica_groups=mesh['task'=4,'dp'=8] {'dp'}, use_global_device_ids=true, to_apply=%region_3.0 | all-reduce | flops 6144 | bytes 49152 | tf_op jit(solution)/shard_map/psum | solution.py:539
  658.5 0.6 fusion
  659.1 0.0 all-reduce.2.cloned.1.call-done
  659.1 1.4 slice.19
  660.5 1.6 slice.18
  662.1 49.1 %reduce-scatter.8.cloned.1.call-done = bf16[4,192,384]{2,1,0:T(8,128)(2,1)} async-done(((bf16[4,1536,384]{2,1,0:T(8,128)(2,1)}), bf16[4,192,384]{2,1,0:T(8,128)(2,1)}) %reduce-scatter.8.cloned.1.call-update) | async-done | bytes 589840 | tf_op jit(solution)/shard_map/reduce_scatter | solution.py:536
  711.2 2.2 convert_element_type.26
  713.3 97.2 %reduce-scatter.6.cloned.1.call-done = bf16[4,48,1536]{2,1,0:T(8,128)(2,1)} async-done(((bf16[4,384,1536]{2,1,0:T(8,128)(2,1)}), bf16[4,48,1536]{2,1,0:T(8,128)(2,1)}) %reduce-scatter.6.cloned.1.call-update) | async-done | bytes 589840 | tf_op jit(solution)/shard_map/reduce_scatter | solution.py:535
  810.5 2.2 convert_element_type.25
Async XLA Ops:
  7.2 3.2 copy-start.5
  7.2 4.2 copy-start.3
  7.2 39.0 %copy-start.2 = (bf16[48,1152]{1,0:T(8,128)(2,1)S(1)}, bf16[48,1152]{1,0:T(8,128)(2,1)}, u32[]{:S(2)}) copy-start(bf16[48,1152]{1,0:T(8,128)(2,1)} %param.15) | copy-start | bytes 331780
  7.2 114.1 %all-gather.13.cloned.1.call-start = ((), (), s32[]{:S(2)}) async-start(), calls=%async_computation.15 | async-start | bytes 3932160 | tf_op jit(solution)/shard_map/all_gather | solution.py:512
  9.7 124.2 %all-gather.11.cloned.1.call-start = ((), (), s32[]{:S(2)}) async-start(), calls=%async_computation.14 | async-start | bytes 3932160 | tf_op jit(solution)/shard_map/all_gather | solution.py:511
  103.2 112.9 %all-gather.7.cloned.1.call-start = ((), (), s32[]{:S(2)}) async-start(), calls=%async_computation.8 | async-start | bytes 5308416 | tf_op jit(solution)/shard_map/all_gather | solution.py:489
  103.9 192.3 %all-gather.9.cloned.1.call-start = ((), (), s32[]{:S(2)}) async-start(), calls=%async_computation.9 | async-start | bytes 5308416 | tf_op jit(solution)/shard_map/all_gather | solution.py:490
  106.0 7.4 all-to-all-start
  113.3 182.8 %copy-start.1 = (s32[4,4,1024]{2,1,0:T(4,128)}, s32[4,4,1024]{2,1,0:T(4,128)S(1)}, u32[]{:S(2)}) copy-start(s32[4,4,1024]{2,1,0:T(4,128)S(1)} %all-to-all-done.slots) | copy-start | bytes 196612
  436.7 40.6 %all-to-all-start.3 = ((bf16[4,1024,384]{2,1,0:T(8,128)(2,1)}), bf16[4,1024,384]{2,1,0:T(8,128)(2,1)S(1)}, u32[]{:S(2)}, u32[]{:S(2)}) async-start(bf16[4,1024,384]{2,1,0:T(8,128)(2,1)} %get-tuple-element.35), calls=%async_computation.3 | async-start | bytes 6291456 | tf_op jit(solution)/shard_map/all_to_all | solution.py:508
  440.4 138.0 %reduce-scatter.4.cloned.1.call-start = ((), (), s32[]{:S(2)}) async-start(), calls=%async_computation.10 | async-start | bytes 1327104 | tf_op jit(solution)/shard_map/reduce_scatter | solution.py:537
  477.3 1.6 copy-start
  516.9 142.2 %all-reduce.2.cloned.1.call-start = ((), (), s32[]{:S(2)}) async-start(), calls=%async_computation.11 | async-start | bytes 294912 | tf_op jit(solution)/shard_map/psum | solution.py:538
  578.4 132.8 %reduce-scatter.8.cloned.1.call-start = ((), (), s32[]{:S(2)}) async-start(), calls=%async_computation.13 | async-start | bytes 5308416 | tf_op jit(solution)/shard_map/reduce_scatter | solution.py:536
  579.2 0.8 copy-start.6
  579.2 40.9 %copy-start.4 = (f32[16,384]{1,0:T(8,128)S(1)}, f32[16,384]{1,0:T(8,128)}, u32[]{:S(2)}) copy-start(f32[16,384]{1,0:T(8,128)} %get-tuple-element.42) | copy-start | bytes 73732
  579.2 231.3 %reduce-scatter.6.cloned.1.call-start = ((), (), s32[]{:S(2)}) async-start(), calls=%async_computation.12 | async-start | bytes 5308416 | tf_op jit(solution)/shard_map/reduce_scatter | solution.py:535
Sparse Core Ops, SparseCore 0:
  10.2 31.2 all-gather.12
  103.3 30.5 all-gather.10
  136.1 79.8 all-gather.6
  218.1 78.0 all-gather.8
  517.1 61.2 reduce-scatter.3
  580.6 29.7 all-reduce.1
  614.5 96.6 reduce-scatter.7
  715.3 95.2 reduce-scatter.5

commit v2 on v1

--- a/solution.py
+++ b/solution.py
@@ -25,12 +25,13 @@
 
 FF_TILE = 512
 ROW_TILE = 640
-QUERY_FWD = 512
+QUERY_FWD = 256
 QUERY_BWD = 256
 ROWS = 256
 
 VMEM = pl.BlockSpec(memory_space=pltpu.VMEM)
 SMEM = pl.BlockSpec(memory_space=pltpu.SMEM)
+ANY = pl.BlockSpec(memory_space=pl.ANY)
 
 
 def shape(*dims, dtype=f32):
@@ -80,39 +81,204 @@
     return (lanes < HEAD_DIM) if half == 0 else (lanes >= HEAD_DIM)
 
 
-def attend(packed, mixed, totals):
+def remote(source, target, sent, landed, **device):
+    return pltpu.make_async_remote_copy(
+        src_ref=source,
+        dst_ref=target,
+        send_sem=sent,
+        recv_sem=landed,
+        device_id=device,
+        device_id_type=pl.DeviceIdType.MESH,
+    )
+
+
+class Place:
+    def __init__(self, outers):
+        self.dp = lax.axis_index("dp")
+        self.task = lax.axis_index("task")
+        self.outers = outers
+        self.outer, self.inner = self.dp // 2, self.dp % 2
+        self.has_up, self.has_down = self.outer + 1 < outers, self.outer > 0
+        self.up, self.down = self.dp + 2, self.dp - 2
+        self.side = self.dp + 1 - 2 * self.inner
+        self.core = self.task + 1 - 2 * (self.task % 2)
+        self.across = self.task + 2 - 4 * (self.task // 2)
+
+    def greet(self):
+        barrier = pltpu.get_barrier_semaphore()
+
+        def signal(**device):
+            pl.semaphore_signal(
+                barrier, inc=1, device_id=device, device_id_type=pl.DeviceIdType.MESH
+            )
+
+        pl.when(self.has_up)(lambda: signal(dp=self.up))
+        pl.when(self.has_down)(lambda: signal(dp=self.down))
+        signal(dp=self.side)
+        signal(task=self.core)
+        signal(task=self.across)
+        pl.semaphore_wait(
+            barrier, 3 + self.has_up.astype(jnp.int32) + self.has_down.astype(jnp.int32)
+        )
+
+
+class Gather:
+    def __init__(self, place, shards, sent, landed, stay):
+        self.place, self.shards = place, shards
+        self.sent, self.landed, self.stay = sent, landed, stay
+
+    def move(self, unit, source, way, device, first=False):
+        own, full = self.shards[unit]
+        return remote(
+            own if first else full(source),
+            full(source),
+            self.sent.at[unit, source, way],
+            self.landed.at[unit, source],
+            dp=device,
+        )
+
+    def local(self, unit):
+        own, full = self.shards[unit]
+        return pltpu.make_async_copy(own, full(self.place.dp), self.stay.at[unit])
+
+    def start(self, unit):
+        place = self.place
+        pl.when(place.has_up)(lambda: self.move(unit, place.dp, 0, place.up, True).start())
+        pl.when(place.has_down)(lambda: self.move(unit, place.dp, 1, place.down, True).start())
+        self.move(unit, place.dp, 2, place.side, True).start()
+        self.local(unit).start()
+
+    def step(self, unit, hop):
+        place = self.place
+
+        @pl.when(place.outer >= hop)
+        def _():
+            source = place.dp - 2 * hop
+            self.move(unit, source, 0, place.dp).wait_recv()
+            pl.when(place.has_up)(lambda: self.move(unit, source, 0, place.up).start())
+            self.move(unit, source, 2, place.side).start()
+
+        @pl.when(place.outer + hop < place.outers)
+        def _():
+            source = place.dp + 2 * hop
+            self.move(unit, source, 1, place.dp).wait_recv()
+            pl.when(place.has_down)(lambda: self.move(unit, source, 1, place.down).start())
+            self.move(unit, source, 2, place.side).start()
+
+    def finish(self, unit):
+        place = self.place
+        self.local(unit).wait()
+        for outer in range(place.outers):
+            own, other = 2 * outer + place.inner, 2 * outer + 1 - place.inner
+            self.move(unit, other, 2, place.dp).wait_recv()
+            self.move(unit, own, 2, place.side).wait_send()
+            pl.when((outer <= place.outer) & place.has_up)(
+                lambda own=own: self.move(unit, own, 0, place.up).wait_send()
+            )
+            pl.when((outer >= place.outer) & place.has_down)(
+                lambda own=own: self.move(unit, own, 1, place.down).wait_send()
+            )
+
+
+class Share:
+    def __init__(self, place, view, sent, landed):
+        self.place, self.view, self.sent, self.landed = place, view, sent, landed
+
+    def move(self, source, way, **device):
+        return remote(
+            self.view(source),
+            self.view(source),
+            self.sent.at[way],
+            self.landed.at[way],
+            **device,
+        )
+
+    def start(self):
+        place = self.place
+        self.move(place.task, 0, task=place.across).start()
+        self.move(place.task, 1, task=place.core).start()
+
+    def relay(self):
+        place = self.place
+        self.move(place.across, 0, task=place.across).wait_recv()
+        self.move(place.across, 2, task=place.core).start()
+
+    def finish(self):
+        place = self.place
+        self.move(place.task, 0, task=place.across).wait_send()
+        self.move(place.core, 1, task=place.core).wait()
+        self.move(place.across, 2, task=place.core).wait()
+
+
+def attend(packed, mixed, totals, index):
     zero = jnp.array(0, bf16)
+    rows = rows_at(index, QUERY_FWD)
 
     def head_pair(pair, _):
         queries, keys, values = (rows_at(pair + part * (D // PAIR), PAIR) for part in range(3))
         key_rows, value_rows = packed[:, keys], packed[:, values]
-
-        def block(index, _):
-            rows = rows_at(index, QUERY_FWD)
-            query_rows = packed[rows, queries] * jnp.array(HEAD_DIM**-0.5, bf16)
-            outs, logs = [], []
-            for half in range(2):
-                own = jnp.where(half_lanes(QUERY_FWD, half), query_rows, zero)
-                scores = dot_rt(own, key_rows)
-                top = jnp.max(scores, axis=1, keepdims=True)
-                weights = jnp.exp(scores - top)
-                total = jnp.sum(weights, axis=1, keepdims=True)
-                outs.append(dot(weights.astype(bf16), value_rows) * (1.0 / total))
-                logs.append(top + jnp.log(total))
-            mixed[rows, queries] = jnp.where(half_lanes(QUERY_FWD, 0), outs[0], outs[1]).astype(
-                bf16
-            )
-            lanes = lax.broadcasted_iota(jnp.int32, (QUERY_FWD, 8), 1)
-            totals[rows, :] = jnp.where(
-                lanes == 2 * pair,
-                logs[0],
-                jnp.where(lanes == 2 * pair + 1, logs[1], totals[rows, :]),
-            )
-            return 0
-
-        return lax.fori_loop(0, SEQ // QUERY_FWD, block, 0)
+        query_rows = packed[rows, queries] * jnp.array(HEAD_DIM**-0.5, bf16)
+        outs, logs = [], []
+        for half in range(2):
+            own = jnp.where(half_lanes(QUERY_FWD, half), query_rows, zero)
+            scores = dot_rt(own, key_rows)
+            top = jnp.max(scores, axis=1, keepdims=True)
+            weights = jnp.exp(scores - top)
+            total = jnp.sum(weights, axis=1, keepdims=True)
+            outs.append(dot(weights.astype(bf16), value_rows) * (1.0 / total))
+            logs.append(top + jnp.log(total))
+        mixed[rows, queries] = jnp.where(half_lanes(QUERY_FWD, 0), outs[0], outs[1]).astype(bf16)
+        lanes = lax.broadcasted_iota(jnp.int32, (QUERY_FWD, 8), 1)
+        totals[rows, :] = jnp.where(
+            lanes == 2 * pair,
+            logs[0],
+            jnp.where(lanes == 2 * pair + 1, logs[1], totals[rows, :]),
+        )
+        return 0
 
     lax.fori_loop(0, HEADS // 2, head_pair, 0)
+
+
+def first_norm(image, gain, bias, normed_first):
+    def block(index, _):
+        rows = rows_at(index, ROWS)
+        unit, _ = normalize(image[rows, :])
+        normed_first[rows, :] = (unit * gain[0:1, :] + bias[0:1, :]).astype(bf16)
+        return 0
+
+    lax.fori_loop(0, SEQ // ROWS, block, 0)
+
+
+def number_slots(choices, top_count, experts):
+    named = choices[...].T
+    numbers = lax.broadcasted_iota(jnp.int32, (experts, SEQ), 0)
+    used = jnp.zeros((experts, SEQ), f32)
+    for choice in range(TOPMAX):
+        hit = (named[choice : choice + 1, :] == numbers) & (choice < top_count[0])
+        used = used + jnp.where(hit, 1.0, 0.0)
+    earlier = lax.broadcasted_iota(jnp.int32, (SEQ, SEQ), 0) < lax.broadcasted_iota(
+        jnp.int32, (SEQ, SEQ), 1
+    )
+    before = dot(used.astype(bf16), jnp.where(earlier, 1.0, 0.0).astype(bf16))
+    return jnp.where(used > 0, before, -1.0).astype(jnp.int32)
+
+
+def mid_block(index, image, gain, bias, w_proj, router, mixed, mid, probs):
+    rows = rows_at(index, QUERY_FWD)
+    mid_rows = image[rows, :] + dot(mixed[rows, :], w_proj[...])
+    mid[rows, :] = mid_rows
+    unit, _ = normalize(mid_rows)
+    normed_rows = unit * gain[1:2, :] + bias[1:2, :]
+    logits = lax.dot_general(
+        router[...],
+        normed_rows,
+        (((1,), (1,)), ((), ())),
+        precision=HIGHEST,
+        preferred_element_type=f32,
+    )
+    powers = jnp.exp(logits - jnp.max(logits, axis=0, keepdims=True))
+    probs[:, rows] = powers / jnp.sum(powers, axis=0, keepdims=True)
+    return normed_rows.astype(bf16)
 
 
 def forward_kernel(
@@ -135,50 +301,20 @@
     normed_first,
     totals,
 ):
-    experts = router.shape[0]
-
-    def first_norm(index, _):
-        rows = rows_at(index, ROWS)
-        unit, _ = normalize(image[rows, :])
-        normed_first[rows, :] = (unit * gain[0:1, :] + bias[0:1, :]).astype(bf16)
-        return 0
-
-    lax.fori_loop(0, SEQ // ROWS, first_norm, 0)
-    named = choices[...].T
-    numbers = lax.broadcasted_iota(jnp.int32, (experts, SEQ), 0)
-    used = jnp.zeros((experts, SEQ), f32)
-    for choice in range(TOPMAX):
-        hit = (named[choice : choice + 1, :] == numbers) & (choice < top_count[0])
-        used = used + jnp.where(hit, 1.0, 0.0)
-    earlier = lax.broadcasted_iota(jnp.int32, (SEQ, SEQ), 0) < lax.broadcasted_iota(
-        jnp.int32, (SEQ, SEQ), 1
-    )
-    before = dot(used.astype(bf16), jnp.where(earlier, 1.0, 0.0).astype(bf16))
-    slots[...] = jnp.where(used > 0, before, -1.0).astype(jnp.int32)
+    first_norm(image, gain, bias, normed_first)
+    slots[...] = number_slots(choices, top_count, router.shape[0])
     packed[...] = dot(normed_first[...], w_qkv[...]).astype(bf16)
     totals[...] = jnp.zeros_like(totals)
-    attend(packed, mixed, totals)
+
+    def block(index, _):
+        attend(packed, mixed, totals, index)
+        normed[rows_at(index, QUERY_FWD), :] = mid_block(
+            index, image, gain, bias, w_proj, router, mixed, mid, probs
+        )
+        return 0
+
+    lax.fori_loop(0, SEQ // QUERY_FWD, block, 0)
     logs[...] = totals[...].T
-
-    def second_norm(index, _):
-        rows = rows_at(index, ROWS)
-        mid_rows = image[rows, :] + dot(mixed[rows, :], w_proj[...])
-        mid[rows, :] = mid_rows
-        unit, _ = normalize(mid_rows)
-        normed_rows = unit * gain[1:2, :] + bias[1:2, :]
-        normed[rows, :] = normed_rows.astype(bf16)
-        logits = lax.dot_general(
-            router[...],
-            normed_rows,
-            (((1,), (1,)), ((), ())),
-            precision=HIGHEST,
-            preferred_element_type=f32,
-        )
-        powers = jnp.exp(logits - jnp.max(logits, axis=0, keepdims=True))
-        probs[:, rows] = powers / jnp.sum(powers, axis=0, keepdims=True)
-        return 0
-
-    lax.fori_loop(0, SEQ // ROWS, second_norm, 0)
     gates[...] = jnp.where(slots[...] >= 0, probs[...], 0.0)
 
 
@@ -201,6 +337,154 @@
         scratch_shapes=[pltpu.VMEM((SEQ, D), bf16), pltpu.VMEM((SEQ, 8), f32)],
         compiler_params=params(),
     )(top_count, image, gain, bias, w_qkv, w_proj, router, choices)
+
+
+def forward_sending_kernel(
+    outers,
+    top_count,
+    image,
+    cotangent,
+    gain,
+    bias,
+    w_qkv,
+    w_proj,
+    w_in,
+    w_out,
+    router,
+    choices,
+    mid,
+    packed,
+    mixed,
+    logs,
+    probs,
+    normed_all,
+    cot_all,
+    slots_all,
+    gates_all,
+    full_qkv,
+    full_proj,
+    full_in,
+    full_out,
+    normed_first,
+    totals,
+    sent,
+    landed,
+    stay,
+    share_sent,
+    share_landed,
+):
+    place = Place(outers)
+    task = place.task
+    local_count = w_in.shape[0]
+
+    def part(own, full, *lead):
+        size = own.shape[-2]
+        source = own.at[lead] if lead else own
+        return source, lambda index: full.at[(*lead, rows_at(index, size))]
+
+    shards = [part(w_qkv, full_qkv), part(w_proj, full_proj)]
+    for expert in range(local_count):
+        shards += [part(w_in, full_in, expert), part(w_out, full_out, expert)]
+    gather = Gather(place, shards, sent, landed, stay)
+    shared, routed = range(2), range(2, len(shards))
+    cot_all[task] = cotangent[...].astype(bf16)
+    place.greet()
+    for unit in shared:
+        gather.start(unit)
+
+    def share(index, view):
+        return Share(place, view, share_sent.at[index], share_landed.at[index])
+
+    cot = share(0, lambda source: cot_all.at[source])
+    slot = share(1, lambda source: slots_all.at[source])
+    gate = share(2, lambda source: gates_all.at[source])
+    cot.start()
+    first_norm(image, gain, bias, normed_first)
+    for hop in range(1, outers):
+        for unit in shared:
+            gather.step(unit, hop)
+    for unit in routed:
+        gather.start(unit)
+    slots_all[task] = number_slots(choices, top_count, router.shape[0])
+    slot.start()
+    totals[...] = jnp.zeros_like(totals)
+    for unit in shared:
+        gather.finish(unit)
+    packed[...] = dot(normed_first[...], full_qkv[...]).astype(bf16)
+    cot.relay()
+    slot.relay()
+
+    def chunk(index):
+        return share(3 + index, lambda source: normed_all.at[source, rows_at(index, QUERY_FWD)])
+
+    blocks = SEQ // QUERY_FWD
+
+    def block(index, _):
+        attend(packed, mixed, totals, index)
+        normed_all[task, rows_at(index, QUERY_FWD), :] = mid_block(
+            index, image, gain, bias, full_proj, router, mixed, mid, probs
+        )
+        chunk(index).start()
+        pl.when(index > 0)(lambda: chunk(index - 1).relay())
+        for hop in range(1, outers):
+
+            @pl.when(index == hop - 1)
+            def _():
+                for unit in routed:
+                    gather.step(unit, hop)
+
+        return 0
+
+    lax.fori_loop(0, blocks, block, 0)
+    for hop in range(blocks + 1, outers):
+        for unit in routed:
+            gather.step(unit, hop)
+    gates_all[task] = jnp.where(slots_all[task] >= 0, probs[...], 0.0)
+    gate.start()
+    logs[...] = totals[...].T
+    chunk(blocks - 1).relay()
+    gate.relay()
+    for one in [cot, slot, gate] + [chunk(index) for index in range(blocks)]:
+        one.finish()
+    for unit in routed:
+        gather.finish(unit)
+
+
+def forward_sending(top_count, image, cotangent, gain, bias, shards, router, choices):
+    w_qkv, w_proj, w_in, w_out = shards
+    experts, size = router.shape[0], lax.axis_size("dp")
+    groups, local_count = lax.axis_size("task"), w_in.shape[0]
+    units, shares = 2 + 2 * local_count, 3 + SEQ // QUERY_FWD
+    return pl.pallas_call(
+        functools.partial(forward_sending_kernel, size // 2),
+        out_shape=(
+            shape(SEQ, D),
+            shape(SEQ, 3 * D, dtype=bf16),
+            shape(SEQ, D, dtype=bf16),
+            shape(8, SEQ),
+            shape(experts, SEQ),
+            shape(groups, SEQ, D, dtype=bf16),
+            shape(groups, SEQ, D, dtype=bf16),
+            shape(groups, experts, SEQ, dtype=jnp.int32),
+            shape(groups, experts, SEQ),
+            shape(D, 3 * D, dtype=bf16),
+            shape(D, D, dtype=bf16),
+            shape(local_count, D, FF, dtype=bf16),
+            shape(local_count, FF, D, dtype=bf16),
+        ),
+        in_specs=[SMEM] + [VMEM] * 6 + [ANY] * 2 + [VMEM] * 2,
+        out_specs=[VMEM] * 11 + [ANY] * 2,
+        scratch_shapes=[
+            pltpu.VMEM((SEQ, D), bf16),
+            pltpu.VMEM((SEQ, 8), f32),
+            pltpu.SemaphoreType.DMA((units, size, 3)),
+            pltpu.SemaphoreType.DMA((units, size)),
+            pltpu.SemaphoreType.DMA((units,)),
+            pltpu.SemaphoreType.DMA((shares, 3)),
+            pltpu.SemaphoreType.DMA((shares, 3)),
+        ],
+        compiler_params=params(collective_id=0, has_side_effects=True),
+    )(top_count, image, cotangent, gain, bias, w_qkv, w_proj, w_in, w_out, router, choices)
 
 
 def slot_hits(slots, source, expert):
@@ -483,37 +767,67 @@
 ):
     groups = lax.axis_size("task")
     local_count = w_in.shape[0]
-    full_qkv, full_proj, full_in, full_out = (
-        lax.all_gather(w_qkv, "dp", axis=0, tiled=True),
-        lax.all_gather(w_proj, "dp", axis=0, tiled=True),
-        lax.all_gather(w_in, "dp", axis=1, tiled=True),
-        lax.all_gather(w_out, "dp", axis=1, tiled=True),
-    )
     image = layer_input.reshape(SEQ, D)
     grad_rows = cotangent.reshape(SEQ, D)
     router_rows = router[0].T
     experts = router_rows.shape[0]
-    mid, packed, mixed, logs, normed, slots, gates, probs = forward_part(
-        top_count,
-        image,
-        norm_gain,
-        norm_bias,
-        full_qkv,
-        full_proj,
-        router_rows,
-        choices.reshape(SEQ, TOPMAX),
-    )
+    routes = choices.reshape(SEQ, TOPMAX)
 
     def swap(array):
         return lax.all_to_all(array, "task", split_axis=0, concat_axis=0, tiled=True)
 
+    sending = groups == 4 and lax.axis_size("dp") in (4, 8) and w_in.shape[1] % 16 == 0
+    if sending:
+        (
+            mid,
+            packed,
+            mixed,
+            logs,
+            probs,
+            normed,
+            cot_rows,
+            slots,
+            gates,
+            full_qkv,
+            full_proj,
+            full_in,
+            full_out,
+        ) = forward_sending(
+            top_count,
+            image,
+            grad_rows,
+            norm_gain,
+            norm_bias,
+            (w_qkv, w_proj, w_in, w_out),
+            router_rows,
+            routes,
+        )
+        mine = lax.axis_index("task") * local_count
+        slots = lax.dynamic_slice_in_dim(slots, mine, local_count, 1)
+        gates = lax.dynamic_slice_in_dim(gates, mine, local_count, 1)
+    else:
+        full_qkv, full_proj, full_in, full_out = (
+            lax.all_gather(w_qkv, "dp", axis=0, tiled=True),
+            lax.all_gather(w_proj, "dp", axis=0, tiled=True),
+            lax.all_gather(w_in, "dp", axis=1, tiled=True),
+            lax.all_gather(w_out, "dp", axis=1, tiled=True),
+        )
+        mid, packed, mixed, logs, normed, slots, gates, probs = forward_part(
+            top_count,
+            image,
+            norm_gain,
+            norm_bias,
+            full_qkv,
+            full_proj,
+            router_rows,
+            routes,
+        )
+        normed = lax.all_gather(normed, "task")
+        cot_rows = lax.all_gather(grad_rows.astype(bf16), "task")
+        slots = swap(slots.reshape(groups, local_count, SEQ))
+        gates = swap(gates.reshape(groups, local_count, SEQ))
     grad_in, grad_out, mixes, grad_normed, grad_gates = expert_part(
-        lax.all_gather(normed, "task"),
-        lax.all_gather(grad_rows.astype(bf16), "task"),
-        swap(slots.reshape(groups, local_count, SEQ)),
-        swap(gates.reshape(groups, local_count, SEQ)),
-        full_in,
-        full_out,
+        normed, cot_rows, slots, gates, full_in, full_out
     )
     activations, grad_image, grad_norm, grad_router, grad_shared = backward_part(
         image,

time: 821 us -> 668 us (0.81)
  waiting for transfers between devices: 425 us -> 246 us
  Pallas kernels: 152 us -> 260 us
  blocking collectives: 205 us -> 128 us
    all_gather x4 -> x0, waiting for transfers between devices: 175 us -> none  [the longest x1 82.1 us: local(): lax.all_gather(w_in, 'dp', axis=1, tiled=True)]
    pallas_call x1, Pallas kernels: 22.8 us -> 131 us  [forward_sending(): pl.pallas_call(functools.partial(forward_sending_kernel, size // 2), out_...]
    all_gather x2 -> x0, blocking collectives: 68.9 us -> none  [the longest x1 34.8 us: local(): lax.all_gather(w_proj, 'dp', axis=0, tiled=True)]
    all_to_all x3 -> x2, blocking collectives: 57.6 us -> 49.6 us  [swap(): lax.all_to_all(array, 'task', split_axis=0, concat_axis=0, tiled=True)]
    all_to_all x2 -> x1, waiting for transfers between devices: 39.4 us -> 36.2 us  [swap(): lax.all_to_all(array, 'task', split_axis=0, concat_axis=0, tiled=True)]
  transfers between devices with their start and end apart: 10 -> 5, of which waited for: 8 -> 4; matrix products, arithmetic and copies ran while one was open for 1% -> 1% of each run, Pallas kernels for 3% -> 0%
where the time goes in v2:
time: 668 us; the launch traced here: 667 us
  Pallas kernels  260 us (39%)
  waiting for transfers between devices  246 us (37%)
  blocking collectives  128 us (19%)
  between operations  14.5 us (2%)
  local copies, waits for them, and re-layouts  10.8 us (2%)
    pallas_call x1, Pallas kernels, forward_sending(): pl.pallas_call(functools.partial(forward_sending_kernel, size // 2), out_...  131 us
    reduce_scatter x1, waiting for transfers between devices, local(): grad_in = lax.psum_scatter(grad_in, 'dp', scatter_dimension=1, tiled=True)  97 us
    pallas_call x1, Pallas kernels, expert_part(): pl.pallas_call(expert_kernel, out_shape=(shape(local_count, D, FF, dtype=...  90.9 us
    reduce_scatter x1, waiting for transfers between devices, local(): lax.psum_scatter(grad_shared, 'dp', scatter_dimension=0, tiled=True)  61.7 us
    all_to_all x2, blocking collectives, swap(): lax.all_to_all(array, 'task', split_axis=0, concat_axis=0, tiled=True)  49.6 us
    reduce_scatter x1, waiting for transfers between devices, local(): grad_out = lax.psum_scatter(grad_out, 'dp', scatter_dimension=1, tiled=True)  49.5 us
    psum x1, blocking collectives, local(): grad_norm = lax.psum(grad_norm, ('task', 'dp'))  40 us
    psum x1, blocking collectives, local(): grad_router = lax.psum(grad_router, 'dp')  38.5 us
  transfers between devices with their start and end apart: 5, of which 4 were waited for; matrix products, arithmetic and copies ran while one was open for 1% of the time, Pallas kernels for 0%

profile of v2, /device:TPU:0, one launch (start us, length us, event | category | flops | bytes accessed | tf_op | source)
XLA Modules:
  0.0 667.4 jit_solution(6677333302281218166)
XLA Ops:
  7.8 1.7 copy.20
  9.6 131.3 %shard_map.178 = (f32[1024,384]{1,0:T(8,128)}, bf16[1024,1152]{1,0:T(8,128)(2,1)}, bf16[1024,384]{1,0:T(8,128)(2,1)}, f32[8,1024]{1,0:T(8,128)}, f32[16,1024]{1,...) custom-call(s32[1]{0:T(128)S(6)} %copy.22.top_count, ...), custom_call_target="tpu_custom_call" | custom-call | tf_op jit(solution)/shard_map/pallas_call | solution.py:458
  140.9 1.6 constant_dynamic-slice_fusion.1.slots
  142.4 1.5 constant_dynamic-slice_fusion.gates
  144.0 90.9 %shard_map.179 = (bf16[4,384,1536]{2,1,0:T(8,128)(2,1)}, bf16[4,1536,384]{2,1,0:T(8,128)(2,1)}, bf16[4,1024,384]{2,1,0:T(8,128)(2,1)}, bf16[4,1024,384]{2,1,0:T(8,128)(2,1)}, f32[4,4,1024]{2,1,0:T(4,128)}) custom-call(bf16[4,1024,384]{2,1,0:T(8,128)(2,1)} %get-tuple-element.38.normed, bf16[4,1024,384]{2,1,0:T(8,128)(2,1)} %get-tuple-element.39.cotangent, ...), custom_call_target="tpu_custom_call" | custom-call | tf_op jit(solution)/shard_map/pallas_call | solution.py:584
  234.9 7.4 %all_to_all.15 = f32[4,4,1024]{2,1,0:T(4,128)S(1)} all-to-all(f32[4,4,1024]{2,1,0:T(4,128)} %get-tuple-element.46), channel_id=1, replica_groups=mesh['task'=4,'dp'=8] {'task'}, dimensions={0} | all-to-all | bytes 131072 | tf_op jit(solution)/shard_map/all_to_all | solution.py:777
  242.2 42.3 %all_to_all.16.mixes = bf16[4,1024,384]{2,1,0:T(8,128)(2,1)} all-to-all(bf16[4,1024,384]{2,1,0:T(8,128)(2,1)} %get-tuple-element.44), channel_id=1, replica_groups=mesh['task'=4,'dp'=8] {'task'}, dimensions={0} | all-to-all | bytes 6291456 | tf_op jit(solution)/shard_map/all_to_all | solution.py:777
  284.5 3.7 all-to-all-start.1
  288.2 0.0 reduce-scatter.4.cloned.1.call-start
  288.2 0.7 reshape.39.grad_gates
  288.9 36.2 %all-to-all-done.1.grad_normed = bf16[4,1024,384]{2,1,0:T(8,128)(2,1)S(1)} async-done(((bf16[4,1024,384]{2,1,0:T(8,128)(2,1)}), bf16[4,1024,384]{2,1,0:T(8,128)(2,1)S(1)}, u32[]{:S(2)}, u32[]{:S(2)}) %all-to-all-start.1) | async-done | bytes 3145760 | tf_op jit(solution)/shard_map/all_to_all | solution.py:777
  325.1 0.0 copy-start
  325.1 1.6 copy-done
  326.7 37.9 %shard_map.180 = (f32[1024,384]{1,0:T(8,128)}, f32[1024,384]{1,0:T(8,128)}, f32[4,384]{1,0:T(4,128)}, f32[16,384]{1,0:T(8,128)}, bf16[384,1536]{1,0:T(8,128)(2,1)}) custom-call(f32[1024,384]{1,0:T(8,128)} %bitcast.12, f32[1024,384]{1,0:T(8,128)} %bitcast.14, f32[2,384]{1,0:T(2,128)} %gain.3, f32[2,384]{1,0:T(2,128)} %bias.3, ...), custom_call_target="tpu_custom_call" | custom-call | tf_op jit(solution)/shard_map/pallas_call | solution.py:731
  364.6 0.0 reduce-scatter.4.cloned.1.call-update
  364.7 0.0 all-reduce.2.cloned.1.call-start
  364.7 61.7 %reduce-scatter.4.cloned.1.call-done = bf16[48,1536]{1,0:T(8,128)(2,1)} async-done(((bf16[384,1536]{1,0:T(8,128)(2,1)}), bf16[48,1536]{1,0:T(8,128)(2,1)}) %reduce-scatter.4.cloned.1.call-update) | async-done | bytes 147472 | tf_op jit(solution)/shard_map/reduce_scatter | solution.py:851
  426.4 0.0 all-reduce.2.cloned.1.call-update
  426.4 0.0 reduce-scatter.8.cloned.1.call-start
  426.5 0.7 reduce-scatter.8.cloned.1.call-update
  427.1 0.0 copy-start.2
  427.2 0.0 copy-start.1
  427.2 0.0 reduce-scatter.6.cloned.1.call-start
  427.2 0.5 reduce-scatter.6.cloned.1.call-update
  427.7 0.1 copy-done.2
  427.8 40.0 %psum.21 = f32[4,384]{1,0:T(4,128)S(1)} all-reduce(f32[4,384]{1,0:T(4,128)S(1)} %copy-done.2), channel_id=1, replica_groups=mesh['task'=4,'dp'=8] {'task','dp'}, use_global_device_ids=true, to_apply=%region_0.0 | all-reduce | flops 1536 | bytes 12288 | tf_op jit(solution)/shard_map/psum | solution.py:854
  467.8 0.0 copy-done.1
  467.9 38.5 %psum.23 = f32[1,384,16]{1,2,0:T(8,128)} all-reduce(f32[1,384,16]{1,2,0:T(8,128)S(1)} %bitcast.18), channel_id=1, replica_groups=mesh['task'=4,'dp'=8] {'dp'}, use_global_device_ids=true, to_apply=%region_3.0 | all-reduce | flops 6144 | bytes 49152 | tf_op jit(solution)/shard_map/psum | solution.py:853
  506.3 0.6 fusion
  506.9 0.0 all-reduce.2.cloned.1.call-done
  506.9 1.4 slice.19
  508.3 1.6 slice.18
  509.9 49.5 %reduce-scatter.8.cloned.1.call-done = bf16[4,192,384]{2,1,0:T(8,128)(2,1)} async-done(((bf16[4,1536,384]{2,1,0:T(8,128)(2,1)}), bf16[4,192,384]{2,1,0:T(8,128)(2,1)}) %reduce-scatter.8.cloned.1.call-update) | async-done | bytes 589840 | tf_op jit(solution)/shard_map/reduce_scatter | solution.py:850
  559.4 2.2 convert_element_type.11
  561.6 97.0 %reduce-scatter.6.cloned.1.call-done = bf16[4,48,1536]{2,1,0:T(8,128)(2,1)} async-done(((bf16[4,384,1536]{2,1,0:T(8,128)(2,1)}), bf16[4,48,1536]{2,1,0:T(8,128)(2,1)}) %reduce-scatter.6.cloned.1.call-update) | async-done | bytes 589840 | tf_op jit(solution)/shard_map/reduce_scatter | solution.py:849
  658.6 2.2 convert_element_type.10
Async XLA Ops:
  284.5 40.6 %all-to-all-start.1 = ((bf16[4,1024,384]{2,1,0:T(8,128)(2,1)}), bf16[4,1024,384]{2,1,0:T(8,128)(2,1)S(1)}, u32[]{:S(2)}, u32[]{:S(2)}) async-start(bf16[4,1024,384]{2,1,0:T(8,128)(2,1)} %get-tuple-element.45), calls=%async_computation.1 | async-start | bytes 6291456 | tf_op jit(solution)/shard_map/all_to_all | solution.py:777
  288.2 138.2 %reduce-scatter.4.cloned.1.call-start = ((), (), s32[]{:S(2)}) async-start(), calls=%async_computation.6 | async-start | bytes 1327104 | tf_op jit(solution)/shard_map/reduce_scatter | solution.py:851
  325.1 1.6 copy-start
  364.7 142.3 %all-reduce.2.cloned.1.call-start = ((), (), s32[]{:S(2)}) async-start(), calls=%async_computation.7 | async-start | bytes 294912 | tf_op jit(solution)/shard_map/psum | solution.py:852
  426.4 133.0 %reduce-scatter.8.cloned.1.call-start = ((), (), s32[]{:S(2)}) async-start(), calls=%async_computation.9 | async-start | bytes 5308416 | tf_op jit(solution)/shard_map/reduce_scatter | solution.py:850
  427.1 0.7 copy-start.2
  427.2 40.7 %copy-start.1 = (f32[16,384]{1,0:T(8,128)S(1)}, f32[16,384]{1,0:T(8,128)}, u32[]{:S(2)}) copy-start(f32[16,384]{1,0:T(8,128)} %get-tuple-element.52) | copy-start | bytes 73732
  427.2 231.5 %reduce-scatter.6.cloned.1.call-start = ((), (), s32[]{:S(2)}) async-start(), calls=%async_computation.8 | async-start | bytes 5308416 | tf_op jit(solution)/shard_map/reduce_scatter | solution.py:849
Sparse Core Ops, SparseCore 0:
  364.8 61.5 reduce-scatter.3
  428.7 29.8 all-reduce.1
  462.7 96.7 reduce-scatter.7
  563.4 95.2 reduce-scatter.5

commit v3 on v2

--- a/solution.py
+++ b/solution.py
@@ -28,6 +28,7 @@
 QUERY_FWD = 256
 QUERY_BWD = 256
 ROWS = 256
+RETURNS = 2
 
 VMEM = pl.BlockSpec(memory_space=pltpu.VMEM)
 SMEM = pl.BlockSpec(memory_space=pltpu.SMEM)
@@ -39,7 +40,7 @@
 
 
 def params(**more):
-    return pltpu.CompilerParams(vmem_limit_bytes=60 * 2**20, **more)
+    return pltpu.CompilerParams(vmem_limit_bytes=62 * 2**20, **more)
 
 
 def dot(a, b):
@@ -103,8 +104,12 @@
         self.side = self.dp + 1 - 2 * self.inner
         self.core = self.task + 1 - 2 * (self.task % 2)
         self.across = self.task + 2 - 4 * (self.task // 2)
-
-    def greet(self):
+        self.far = self.across + 1 - 2 * (self.task % 2)
+
+    def partner(self, bit):
+        return self.dp + bit - 2 * bit * (self.dp // bit % 2)
+
+    def greet(self, far=False, bits=()):
         barrier = pltpu.get_barrier_semaphore()
 
         def signal(**device):
@@ -117,8 +122,13 @@
         signal(dp=self.side)
         signal(task=self.core)
         signal(task=self.across)
+        if far:
+            signal(task=self.far)
+        for bit in bits:
+            signal(dp=self.partner(bit))
+        others = 3 + int(far) + len(bits)
         pl.semaphore_wait(
-            barrier, 3 + self.has_up.astype(jnp.int32) + self.has_down.astype(jnp.int32)
+            barrier, others + self.has_up.astype(jnp.int32) + self.has_down.astype(jnp.int32)
         )
 
 
@@ -128,18 +138,20 @@
         self.sent, self.landed, self.stay = sent, landed, stay
 
     def move(self, unit, source, way, device, first=False):
-        own, full = self.shards[unit]
+        own, size, full = self.shards[unit]
+        target = full.at[rows_at(source, size)]
         return remote(
-            own if first else full(source),
-            full(source),
+            own if first else target,
+            target,
             self.sent.at[unit, source, way],
             self.landed.at[unit, source],
             dp=device,
         )
 
     def local(self, unit):
-        own, full = self.shards[unit]
-        return pltpu.make_async_copy(own, full(self.place.dp), self.stay.at[unit])
+        own, size, full = self.shards[unit]
+        target = full.at[rows_at(self.place.dp, size)]
+        return pltpu.make_async_copy(own, target, self.stay.at[unit])
 
     def start(self, unit):
         place = self.place
@@ -208,6 +220,151 @@
         self.move(place.task, 0, task=place.across).wait_send()
         self.move(place.core, 1, task=place.core).wait()
         self.move(place.across, 2, task=place.core).wait()
+
+
+class Scatter:
+    def __init__(self, place, block, size, side, line, fold, sems):
+        self.place, self.block, self.size = place, block, size
+        self.side, self.line, self.fold = side, line, fold
+        self.side_sent, self.side_landed, self.line_sent, self.line_landed = sems
+
+    def own(self, outer, inner):
+        return self.block(rows_at(2 * outer + inner, self.size))
+
+    def to_side(self, outer):
+        place = self.place
+        return remote(
+            self.own(outer, 1 - place.inner),
+            self.side.at[outer],
+            self.side_sent.at[outer],
+            self.side_landed.at[outer],
+            dp=place.side,
+        )
+
+    def along(self, outer, slot, device):
+        return remote(
+            self.fold.at[outer],
+            self.line.at[slot],
+            self.line_sent.at[outer],
+            self.line_landed.at[slot],
+            dp=device,
+        )
+
+    def start(self):
+        outers = self.place.outers
+        for near in range(outers // 2):
+            self.to_side(outers - 1 - near).start()
+            self.to_side(near).start()
+
+    def total(self, outer, *slots):
+        self.to_side(outer).wait_recv()
+        rows = self.own(outer, self.place.inner)[...].astype(f32)
+        rows += self.side[outer].astype(f32)
+        for slot in slots:
+            self.along(outer, slot, self.place.dp).wait_recv()
+            rows += self.line[slot].astype(f32)
+        return rows
+
+    def hop(self, step):
+        place, outers = self.place, self.place.outers
+
+        @pl.when(place.outer == step)
+        def _():
+            for outer in range(outers - 1, step, -1):
+                rows = self.total(outer, *([outer] if step else []))
+                self.fold[outer] = rows.astype(bf16)
+                self.along(outer, outer, place.up).start()
+
+        @pl.when(place.outer == outers - 1 - step)
+        def _():
+            for outer in range(outers - 1 - step):
+                rows = self.total(outer, *([outer] if step else []))
+                self.fold[outer] = rows.astype(bf16)
+                slot = outers if outer == outers - 2 - step else outer
+                self.along(outer, slot, place.down).start()
+
+    def finish(self, store):
+        place, outers = self.place, self.place.outers
+        for outer in range(outers):
+
+            @pl.when(place.outer == outer)
+            def _():
+                below, above = [outer] * (outer > 0), [outers] * (outer < outers - 1)
+                store(self.total(outer, *below, *above))
+                for other in range(outers):
+                    if other != outer:
+                        self.along(other, other, place.dp).wait_send()
+
+            self.to_side(outer).wait_send()
+
+
+class PairSum:
+    def __init__(self, stage, land, sent, landed):
+        self.stage, self.land, self.sent, self.landed = stage, land, sent, landed
+
+    def swap(self, step, **device):
+        return remote(
+            self.stage.at[step],
+            self.land.at[step],
+            self.sent.at[step],
+            self.landed.at[step],
+            **device,
+        )
+
+    def give(self, step, rows, **device):
+        self.stage[step] = rows.astype(self.stage.dtype)
+        self.swap(step, **device).start()
+
+    def take(self, step, **device):
+        self.swap(step, **device).wait()
+        return self.stage[step].astype(f32) + self.land[step].astype(f32)
+
+
+class Return:
+    def __init__(self, place, parts, pieces, land, joint, sent, landed):
+        self.place, self.parts, self.pieces = place, parts, pieces
+        self.land, self.joint, self.sent, self.landed = land, joint, sent, landed
+        self.size = SEQ // pieces
+
+    def rows(self, piece):
+        return pl.ds(piece * self.size, self.size)
+
+    def move(self, way, piece):
+        place, rows = self.place, self.rows(piece)
+        source = [
+            self.parts(place.core).at[rows],
+            self.parts(place.far).at[rows],
+            self.joint.at[rows],
+        ][way]
+        return remote(
+            source,
+            self.land.at[way, rows],
+            self.sent.at[way, piece],
+            self.landed.at[way, piece],
+            task=place.across if way == 2 else place.core,
+        )
+
+    def to_core(self, piece):
+        self.move(0, piece).start()
+
+    def by_core(self, piece):
+        self.move(1, piece).start()
+
+    def to_across(self, piece):
+        rows = self.rows(piece)
+        self.move(1, piece).wait_recv()
+        joint = self.parts(self.place.across)[rows, :].astype(f32)
+        joint += self.land[1, rows, :].astype(f32)
+        self.joint[rows, :] = joint.astype(bf16)
+        self.move(2, piece).start()
+
+    def finish(self, piece):
+        rows = self.rows(piece)
+        self.move(0, piece).wait()
+        self.move(1, piece).wait_send()
+        self.move(2, piece).wait()
+        total = self.parts(self.place.task)[rows, :].astype(f32)
+        return total + self.land[0, rows, :].astype(f32) + self.land[2, rows, :].astype(f32)
 
 
 def attend(packed, mixed, totals, index):
@@ -375,16 +532,12 @@
 ):
     place = Place(outers)
     task = place.task
-    local_count = w_in.shape[0]
-
-    def part(own, full, *lead):
-        size = own.shape[-2]
-        source = own.at[lead] if lead else own
-        return source, lambda index: full.at[(*lead, rows_at(index, size))]
-
-    shards = [part(w_qkv, full_qkv), part(w_proj, full_proj)]
-    for expert in range(local_count):
-        shards += [part(w_in, full_in, expert), part(w_out, full_out, expert)]
+    shards = [(w_qkv, w_qkv.shape[0], full_qkv), (w_proj, w_proj.shape[0], full_proj)]
+    for expert in range(full_in.shape[0]):
+        shards += [
+            (w_in.at[expert], w_in.shape[1], full_in.at[expert]),
+            (w_out.at[expert], w_out.shape[1], full_out.at[expert]),
+        ]
     gather = Gather(place, shards, sent, landed, stay)
     shared, routed = range(2), range(2, len(shards))
     cot_all[task] = cotangent[...].astype(bf16)
@@ -453,8 +606,8 @@
 def forward_sending(top_count, image, cotangent, gain, bias, shards, router, choices):
     w_qkv, w_proj, w_in, w_out = shards
     experts, size = router.shape[0], lax.axis_size("dp")
-    groups, local_count = lax.axis_size("task"), w_in.shape[0]
-    units, shares = 2 + 2 * local_count, 3 + SEQ // QUERY_FWD
+    groups, early = lax.axis_size("task"), w_in.shape[0] // 2
+    units, shares = 2 + 2 * early, 3 + SEQ // QUERY_FWD
     return pl.pallas_call(
         functools.partial(forward_sending_kernel, size // 2),
         out_shape=(
@@ -469,8 +622,8 @@
             shape(groups, experts, SEQ),
             shape(D, 3 * D, dtype=bf16),
             shape(D, D, dtype=bf16),
-            shape(local_count, D, FF, dtype=bf16),
-            shape(local_count, FF, D, dtype=bf16),
+            shape(early, D, FF, dtype=bf16),
+            shape(early, FF, D, dtype=bf16),
         ),
         in_specs=[SMEM] + [VMEM] * 6 + [ANY] * 2 + [VMEM] * 2,
         out_specs=[VMEM] * 11 + [ANY] * 2,
@@ -495,122 +648,376 @@
     return jnp.where(hits, 1.0, 0.0).astype(bf16)
 
 
-def expert_kernel(
-    normed,
-    cotangent,
-    slots,
-    gates,
-    w_in,
-    w_out,
-    grad_in,
-    grad_out,
-    mixes,
-    grad_normed,
-    grad_gates,
-    rows_in,
-    rows_grad,
-    rows_cot,
-    rows_gate,
-    hidden,
-    grad_pre,
-    sent,
-    columns,
-):
-    groups, local_count = normed.shape[0], w_in.shape[0]
+def one_expert(operands, work, grads, expert, first, slot, between):
+    normed, cotangent, slots, gates, w_in, w_out = operands
+    rows_in, rows_grad, rows_cot, rows_gate, hidden, grad_pre, sent = work
+    grad_in, grad_out, grad_gates = grads
+    groups = normed.shape[0]
     width = groups * CAP
-
-    def one_expert(expert, _):
-        for source in range(groups):
-            own = slice(source * CAP, (source + 1) * CAP)
-            hits = slot_hits(slots, source, expert)
-            picks = ones_at(hits)
-            rows_in[own, :] = dot(picks, normed[source]).astype(bf16)
-            cot_rows = dot(picks, cotangent[source])
-            gate = jnp.sum(
-                jnp.where(hits, gates[source, pl.ds(expert, 1), :], 0.0), axis=1, keepdims=True
+    for source in range(groups):
+        own = slice(source * CAP, (source + 1) * CAP)
+        hits = slot_hits(slots, source, first + expert)
+        picks = ones_at(hits)
+        rows_in[own, :] = dot(picks, normed[source]).astype(bf16)
+        cot_rows = dot(picks, cotangent[source])
+        gate = jnp.sum(
+            jnp.where(hits, gates[source, pl.ds(first + expert, 1), :], 0.0),
+            axis=1,
+            keepdims=True,
+        )
+        rows_cot[own, :] = cot_rows.astype(bf16)
+        rows_grad[own, :] = (gate * cot_rows).astype(bf16)
+        rows_gate[own, :] = jnp.broadcast_to(gate, (CAP, 128))
+    between(0)
+
+    def tile(index, _):
+        units = rows_at(index // (width // ROW_TILE), FF_TILE)
+        rows = rows_at(lax.rem(index, width // ROW_TILE), ROW_TILE)
+        pre = dot(rows_in[rows, :], w_in[slot, :, units])
+        grad_hidden = dot_rt(rows_grad[rows, :], w_out[slot, units, :])
+        share = 0.5 * lax.erf(pre * ROOT_HALF) + 0.5
+        slope = share + pre * (NORMAL * jnp.exp(-0.5 * pre * pre))
+        hidden[rows, units] = (pre * share).astype(bf16)
+        grad_pre[rows, units] = (grad_hidden * slope).astype(bf16)
+        return 0
+
+    lax.fori_loop(0, (FF // FF_TILE) * (width // ROW_TILE), tile, 0)
+    between(1)
+    for source in range(groups):
+        own = slice(source * CAP, (source + 1) * CAP)
+        kept = rows_at(expert, CAP)
+        out_rows = dot(hidden[own, :], w_out[slot]).astype(bf16).astype(f32)
+        sent[source, kept, :D] = (rows_gate[own, 0:1] * out_rows).astype(bf16)
+        sent[source, kept, D:] = dot_rt(grad_pre[own, :], w_in[slot]).astype(bf16)
+        grad_gate = jnp.sum(rows_cot[own, :].astype(f32) * out_rows, axis=1, keepdims=True)
+        hits = slot_hits(slots, source, first + expert)
+        grad_gates[source, pl.ds(expert, 1), :] = jnp.sum(
+            jnp.where(hits, grad_gate, 0.0), axis=0, keepdims=True
+        )
+    between(2)
+    grad_in[expert] = dot_lt(rows_in[...], grad_pre[...]).astype(bf16)
+    grad_out[expert] = dot_lt(rows_grad[...], hidden[...]).astype(bf16).T
+    between(3)
+
+
+def combine(slots, first, local_count, sent, columns, source, store):
+    size = SEQ // RETURNS
+    columns[...] = slots[source].T
+    for piece in range(RETURNS):
+        rows = pl.ds(piece * size, size)
+        lanes = lax.broadcasted_iota(jnp.int32, (size, CAP), 1)
+        mine = lax.broadcasted_iota(jnp.int32, (size, columns.shape[1]), 1)
+        picks = []
+        for expert in range(local_count):
+            column = jnp.max(
+                jnp.where(mine == first + expert, columns[rows, :], -1), axis=1, keepdims=True
             )
-            rows_cot[own, :] = cot_rows.astype(bf16)
-            rows_grad[own, :] = (gate * cot_rows).astype(bf16)
-            rows_gate[own, :] = jnp.broadcast_to(gate, (CAP, 128))
-
-        def tile(index, _):
-            units = rows_at(index // (width // ROW_TILE), FF_TILE)
-            rows = rows_at(lax.rem(index, width // ROW_TILE), ROW_TILE)
-            pre = dot(rows_in[rows, :], w_in[expert, :, units])
-            grad_hidden = dot_rt(rows_grad[rows, :], w_out[expert, units, :])
-            share = 0.5 * lax.erf(pre * ROOT_HALF) + 0.5
-            slope = share + pre * (NORMAL * jnp.exp(-0.5 * pre * pre))
-            hidden[rows, units] = (pre * share).astype(bf16)
-            grad_pre[rows, units] = (grad_hidden * slope).astype(bf16)
-            return 0
-
-        lax.fori_loop(0, (FF // FF_TILE) * (width // ROW_TILE), tile, 0)
-        for source in range(groups):
-            own = slice(source * CAP, (source + 1) * CAP)
-            kept = rows_at(expert, CAP)
-            out_rows = dot(hidden[own, :], w_out[expert]).astype(bf16).astype(f32)
-            sent[source, kept, :D] = (rows_gate[own, 0:1] * out_rows).astype(bf16)
-            sent[source, kept, D:] = dot_rt(grad_pre[own, :], w_in[expert]).astype(bf16)
-            grad_gate = jnp.sum(rows_cot[own, :].astype(f32) * out_rows, axis=1, keepdims=True)
-            hits = slot_hits(slots, source, expert)
-            grad_gates[source, pl.ds(expert, 1), :] = jnp.sum(
-                jnp.where(hits, grad_gate, 0.0), axis=0, keepdims=True
-            )
-        grad_in[expert] = dot_lt(rows_in[...], grad_pre[...]).astype(bf16)
-        grad_out[expert] = dot_lt(rows_grad[...], hidden[...]).astype(bf16).T
+            picks.append(ones_at(lanes == column))
+        back = dot(jnp.concatenate(picks, axis=1), sent[source])
+        store(piece, rows, back[:, :D].astype(bf16), back[:, D:].astype(bf16))
+
+
+def expert_scratch(groups, local_count, experts):
+    width = groups * CAP
+    return [
+        pltpu.VMEM((width, D), bf16),
+        pltpu.VMEM((width, D), bf16),
+        pltpu.VMEM((width, D), bf16),
+        pltpu.VMEM((width, 128), f32),
+        pltpu.VMEM((width, FF), bf16),
+        pltpu.VMEM((width, FF), bf16),
+        pltpu.VMEM((groups, local_count * CAP, 2 * D), bf16),
+        pltpu.VMEM((SEQ, experts), jnp.int32),
+    ]
+
+
+def expert_kernel(*refs):
+    operands, grads, (mixes, grad_normed) = refs[:6], refs[6:9], refs[9:11]
+    work, columns = refs[11:18], refs[18]
+    groups, local_count = operands[0].shape[0], operands[4].shape[0]
+
+    def body(expert, _):
+        one_expert(operands, work, grads, expert, 0, expert, lambda point: None)
         return 0
 
-    lax.fori_loop(0, local_count, one_expert, 0)
+    lax.fori_loop(0, local_count, body, 0)
     for source in range(groups):
-        columns[...] = slots[source].T
-
-        def combine(index, _):
-            rows = rows_at(index, 512)
-            lanes = lax.broadcasted_iota(jnp.int32, (512, CAP), 1)
-            picks = jnp.concatenate(
-                [ones_at(lanes == columns[rows, e : e + 1]) for e in range(local_count)], axis=1
-            )
-            back = dot(picks, sent[source])
-            mixes[source, rows, :] = back[:, :D].astype(bf16)
-            grad_normed[source, rows, :] = back[:, D:].astype(bf16)
-            return 0
-
-        lax.fori_loop(0, SEQ // 512, combine, 0)
-
-
-def expert_part(normed, cotangent, slots, gates, w_in, w_out):
-    groups, local_count = normed.shape[0], w_in.shape[0]
-    width = groups * CAP
+
+        def store(piece, rows, mix, grad, source=source):
+            mixes[source, rows, :] = mix
+            grad_normed[source, rows, :] = grad
+
+        combine(operands[2], 0, local_count, work[6], columns, source, store)
+
+
+def expert_part(*operands):
+    groups, local_count = operands[0].shape[0], operands[4].shape[0]
     return pl.pallas_call(
         expert_kernel,
         out_shape=(
             shape(local_count, D, FF, dtype=bf16),
             shape(local_count, FF, D, dtype=bf16),
+            shape(groups, local_count, SEQ),
             shape(groups, SEQ, D, dtype=bf16),
             shape(groups, SEQ, D, dtype=bf16),
-            shape(groups, local_count, SEQ),
         ),
         in_specs=[VMEM] * 6,
         out_specs=[VMEM] * 5,
-        scratch_shapes=[
-            pltpu.VMEM((width, D), bf16),
-            pltpu.VMEM((width, D), bf16),
-            pltpu.VMEM((width, D), bf16),
-            pltpu.VMEM((width, 128), f32),
-            pltpu.VMEM((width, FF), bf16),
-            pltpu.VMEM((width, FF), bf16),
-            pltpu.VMEM((groups, local_count * CAP, 2 * D), bf16),
-            pltpu.VMEM((SEQ, local_count), jnp.int32),
-        ],
+        scratch_shapes=expert_scratch(groups, local_count, operands[2].shape[1]),
         compiler_params=params(),
-    )(normed, cotangent, slots, gates, w_in, w_out)
-
-
-def attend_back(packed, grad_mixed, logs, grad_packed, grad_keys, grad_values):
+    )(*operands)
+
+
+def expert_sending_kernel(outers, early, *refs):
+    normed, cotangent, slots, gates, early_in, early_out, w_in, w_out = refs[:8]
+    late_in, late_out, gate_all, mixes, grad_rows, shard_in, shard_out = refs[8:15]
+    full_in, full_out = refs[15:17]
+    work, columns = refs[17:24], refs[24]
+    slot_in, slot_out, grad_in, grad_out, grad_gates, land = refs[25:31]
+    in_bufs, out_bufs = refs[31:34], refs[34:37]
+    sent, landed, gate_sent, gate_landed, mix_sem, late_sem, slot_sem = refs[37:44]
+    gather_sems, scatter_sems = refs[44:47], refs[47:51]
+    place = Place(outers)
+    local_count, size = grad_in.shape[0], 2 * outers
+    late = local_count - early
+    first = place.task * local_count
+    place.greet(far=True)
+
+    shards = []
+    for expert in range(late):
+        shards += [
+            (w_in.at[early + expert], w_in.shape[1], full_in.at[expert]),
+            (w_out.at[early + expert], w_out.shape[1], full_out.at[expert]),
+        ]
+    gather = Gather(place, shards, *gather_sems)
+    for unit in range(len(shards)):
+        gather.start(unit)
+
+    def load(source, expert, slot):
+        return [
+            pltpu.make_async_copy(source[0].at[expert], slot_in.at[slot], slot_sem.at[slot, 0]),
+            pltpu.make_async_copy(source[1].at[expert], slot_out.at[slot], slot_sem.at[slot, 1]),
+        ]
+
+    for expert in range(early):
+        for copy in load((early_in, early_out), expert, expert):
+            copy.start()
+
+    scatters, stores = [], []
+    for expert in range(early):
+        for source, bufs, shard in ((grad_in, in_bufs, shard_in), (grad_out, out_bufs, shard_out)):
+            unit = len(scatters)
+            scatters.append(
+                Scatter(
+                    place,
+                    lambda rows, source=source, expert=expert: source.at[expert, rows],
+                    shard.shape[1],
+                    *[buf.at[expert] for buf in bufs],
+                    [sem.at[unit] for sem in scatter_sems],
+                )
+            )
+
+            def store(rows, shard=shard, expert=expert):
+                shard[expert] = rows
+
+            stores.append(store)
+
+    def keep(expert):
+        return [
+            pltpu.make_async_copy(
+                grad_in.at[early + expert], late_in.at[expert], late_sem.at[expert, 0]
+            ),
+            pltpu.make_async_copy(
+                grad_out.at[early + expert], late_out.at[expert], late_sem.at[expert, 1]
+            ),
+        ]
+
+    def plan(expert, point):
+        steps = []
+        if point == 0:
+            if expert < early:
+                steps += [copy.wait for copy in load((early_in, early_out), expert, expert)]
+            else:
+                steps += [
+                    copy.wait
+                    for copy in load((full_in, full_out), expert - early, expert - early)
+                ]
+        if expert == 0:
+            for unit in range(len(shards)):
+                hop = point - unit // 2 + 1
+                if 0 < hop < outers:
+                    steps.append(lambda unit=unit, hop=hop: gather.step(unit, hop))
+        if expert == 1 and point == 0:
+            for unit in range(len(shards)):
+                for hop in range(5 - unit // 2, outers):
+                    steps.append(lambda unit=unit, hop=hop: gather.step(unit, hop))
+        if point == 3:
+            if expert < early:
+                steps += [scatters[2 * expert].start, scatters[2 * expert + 1].start]
+            else:
+                steps += [copy.start for copy in keep(expert - early)]
+        return steps
+
+    def body(expert, _):
+        @pl.when(expert >= early)
+        def _():
+            for other in range(late):
+
+                @pl.when(expert == early + other)
+                def _():
+                    gather.finish(2 * other)
+                    gather.finish(2 * other + 1)
+                    for copy in load((full_in, full_out), other, other):
+                        copy.start()
+
+        def between(point):
+            for at in range(local_count):
+                steps = plan(at, point)
+                if steps:
+
+                    @pl.when(expert == at)
+                    def _():
+                        for step in steps:
+                            step()
+
+        one_expert(
+            (normed, cotangent, slots, gates, slot_in, slot_out),
+            work,
+            (grad_in, grad_out, grad_gates),
+            expert,
+            first,
+            lax.rem(expert, early),
+            between,
+        )
+        return 0
+
+    lax.fori_loop(0, local_count, body, 0)
+    gate_all[place.task] = grad_gates[place.task]
+    peers = (place.core, place.across, place.far)
+
+    def gate_move(way):
+        return remote(
+            grad_gates.at[peers[way]],
+            gate_all.at[place.task],
+            gate_sent.at[way],
+            gate_landed.at[way],
+            task=peers[way],
+        )
+
+    for way in range(3):
+        gate_move(way).start()
+    hidden, grad_pre, joint = work[4], work[5], work[2]
+
+    def part(ref, source):
+        return ref.at[pl.ds(0, SEQ), pl.ds(pl.multiple_of(source * D, 128), D)]
+
+    back = Return(
+        place, lambda source: part(hidden, source), RETURNS, land, joint, sent, landed
+    )
+    for source, after in (
+        (place.far, back.by_core),
+        (place.across, back.to_across),
+        (place.core, back.to_core),
+        (place.task, None),
+    ):
+
+        def store(piece, rows, mix, grad, source=source, after=after):
+            part(grad_pre, source)[rows, :] = mix
+            part(hidden, source)[rows, :] = grad
+            if after:
+                after(piece)
+
+        combine(slots, first, local_count, work[6], columns, source, store)
+    keeps = [
+        pltpu.make_async_copy(part(grad_pre, source), mixes.at[source], mix_sem.at[source])
+        for source in range(mixes.shape[0])
+    ]
+    for copy in keeps:
+        copy.start()
+    for turn in range(len(scatters) + outers):
+        for step in range(outers - 1):
+            if 0 <= turn - step < len(scatters):
+                scatters[turn - step].hop(step)
+        if 0 <= turn - outers + 1 < len(scatters):
+            scatters[turn - outers + 1].finish(stores[turn - outers + 1])
+    for piece in range(RETURNS):
+        grad_rows[back.rows(piece), :] = back.finish(piece)
+    for way in range(3):
+        gate_move(way).wait()
+    for copy in keeps:
+        copy.wait()
+    for expert in range(late):
+        for copy in keep(expert):
+            copy.wait()
+
+
+def scatter_buffers(number, outers, *dims):
+    return [pltpu.VMEM((number, slots, *dims), bf16) for slots in (outers, outers + 1, outers)]
+
+
+def scatter_semaphores(units, outers):
+    return [pltpu.SemaphoreType.DMA((units, outers))] * 3 + [
+        pltpu.SemaphoreType.DMA((units, outers + 1))
+    ]
+
+
+def expert_sending(*operands):
+    groups, experts = operands[2].shape[:2]
+    local_count, thin = operands[6].shape[:2]
+    wide, early = operands[7].shape[1], operands[4].shape[0]
+    late, size = local_count - early, lax.axis_size("dp")
+    outers = size // 2
+    return pl.pallas_call(
+        functools.partial(expert_sending_kernel, outers, early),
+        out_shape=(
+            shape(late, D, FF, dtype=bf16),
+            shape(late, FF, D, dtype=bf16),
+            shape(groups, local_count, SEQ),
+            shape(groups, SEQ, D, dtype=bf16),
+            shape(SEQ, D),
+            shape(early, thin, FF),
+            shape(early, wide, D),
+            shape(late, D, FF, dtype=bf16),
+            shape(late, FF, D, dtype=bf16),
+        ),
+        in_specs=[VMEM] * 4 + [ANY] * 4,
+        out_specs=[ANY] * 2 + [VMEM, ANY, VMEM, VMEM, VMEM] + [ANY] * 2,
+        scratch_shapes=expert_scratch(groups, local_count, experts)
+        + [
+            pltpu.VMEM((early, D, FF), bf16),
+            pltpu.VMEM((early, FF, D), bf16),
+            pltpu.VMEM((local_count, D, FF), bf16),
+            pltpu.VMEM((local_count, FF, D), bf16),
+            pltpu.VMEM((groups, local_count, SEQ), f32),
+            pltpu.VMEM((3, SEQ, D), bf16),
+        ]
+        + scatter_buffers(early, outers, thin, FF)
+        + scatter_buffers(early, outers, wide, D)
+        + [
+            pltpu.SemaphoreType.DMA((3, RETURNS)),
+            pltpu.SemaphoreType.DMA((3, RETURNS)),
+            pltpu.SemaphoreType.DMA((3,)),
+            pltpu.SemaphoreType.DMA((3,)),
+            pltpu.SemaphoreType.DMA((groups,)),
+            pltpu.SemaphoreType.DMA((late, 2)),
+            pltpu.SemaphoreType.DMA((early, 2)),
+            pltpu.SemaphoreType.DMA((2 * late, size, 3)),
+            pltpu.SemaphoreType.DMA((2 * late, size)),
+            pltpu.SemaphoreType.DMA((2 * late,)),
+        ]
+        + scatter_semaphores(2 * early, outers),
+        compiler_params=params(collective_id=1, has_side_effects=True),
+    )(*operands)
+
+
+def attend_back(packed, grad_mixed, logs, grad_packed, grad_keys, grad_values, between, done):
     zero = jnp.array(0, bf16)
-
-    def head_pair(pair, _):
-        queries, keys, values = (rows_at(pair + part * (D // PAIR), PAIR) for part in range(3))
+    blocks = SEQ // QUERY_BWD
+
+    def head_pair(pair):
+        queries, keys, values = (
+            slice(part * D + pair * PAIR, part * D + (pair + 1) * PAIR) for part in range(3)
+        )
         key_rows, value_rows = packed[:, keys], packed[:, values]
 
         def block(index, _):
@@ -622,7 +1029,8 @@
                 lanes = half_lanes(QUERY_BWD, half)
                 own = jnp.where(lanes, query_rows, zero)
                 own_grad = jnp.where(lanes, grad_rows, zero)
-                probs = jnp.exp(dot_rt(key_rows, own) - logs[pl.ds(2 * pair + half, 1), rows])
+                head = 2 * pair + half
+                probs = jnp.exp(dot_rt(key_rows, own) - logs[head : head + 1, rows])
                 grad_probs = dot_rt(value_rows, own_grad)
                 mean = jnp.sum(probs * grad_probs, axis=0, keepdims=True)
                 grad_scores = (probs * (grad_probs - mean)).astype(bf16)
@@ -635,67 +1043,36 @@
             ).astype(bf16)
             grad_keys[...] = jnp.where(index == 0, part_keys, grad_keys[...] + part_keys)
             grad_values[...] = jnp.where(index == 0, part_values, grad_values[...] + part_values)
+            between(pair, index)
             return 0
 
-        lax.fori_loop(0, SEQ // QUERY_BWD, block, 0)
+        lax.fori_loop(0, blocks, block, 0)
         grad_packed[:, keys] = grad_keys[...].astype(bf16)
         grad_packed[:, values] = grad_values[...].astype(bf16)
-        return 0
-
-    lax.fori_loop(0, HEADS // 2, head_pair, 0)
-
-
-def backward_kernel(
-    image,
-    cotangent,
-    gain,
-    bias,
-    mid,
-    w_qkv,
-    w_proj,
-    router,
-    packed,
-    mixed,
-    logs,
-    mixes,
-    grad_normed,
-    grad_gates,
-    probs,
-    activations,
-    grad_image,
-    grad_norm,
-    grad_router,
-    grad_shared,
-    grad_mid,
-    grad_low,
-    grad_mixed,
-    grad_packed,
-    grad_keys,
-    grad_values,
-    normed_first,
+        done(pair, (queries, keys, values))
+
+    for pair in range(HEADS // 2):
+        head_pair(pair)
+
+
+def second_back(
+    grad_rows, cotangent, gain, bias, mid, w_proj, router, grad_logits, grad_norm, grad_router, outs
 ):
-    groups = mixes.shape[0]
-    route = grad_gates[...]
-    grad_logits = probs[...] * (route - jnp.sum(probs[...] * route, axis=0, keepdims=True))
+    grad_mid, grad_low, grad_mixed = outs
     grad_norm[...] = jnp.zeros_like(grad_norm)
     grad_router[...] = jnp.zeros_like(grad_router)
     for index in range(SEQ // ROWS):
         rows = slice(index * ROWS, (index + 1) * ROWS)
         mid_rows = mid[rows, :]
-        mix_rows, grad_rows = mixes[0, rows, :].astype(f32), grad_normed[0, rows, :].astype(f32)
-        for source in range(1, groups):
-            mix_rows += mixes[source, rows, :].astype(f32)
-            grad_rows += grad_normed[source, rows, :].astype(f32)
-        activations[rows, :] = mid_rows + mix_rows
         own_logits = grad_logits[:, rows]
-        grad_rows += lax.dot_general(
+        grad_in_rows = grad_rows(rows) + lax.dot_general(
             own_logits,
             router[...],
             (((0,), (0,)), ((), ())),
             precision=HIGHEST,
             preferred_element_type=f32,
         )
-        grad_in, grad_gain, grad_bias, unit = norm_back(mid_rows, grad_rows, gain[1:2, :])
+        grad_in, grad_gain, grad_bias, unit = norm_back(mid_rows, grad_in_rows, gain[1:2, :])
         grad_router[...] += jnp.dot(
             own_logits,
             unit * gain[1:2, :] + bias[1:2, :],
@@ -709,20 +1086,78 @@
         low_rows = grad_mid_rows.astype(bf16)
         grad_low[rows, :] = low_rows
         grad_mixed[rows, :] = dot_rt(low_rows, w_proj[...]).astype(bf16)
-    grad_shared[:, 3 * D :] = dot_lt(mixed[...], grad_low[...]).astype(bf16)
-    attend_back(packed, grad_mixed, logs, grad_packed, grad_keys, grad_values)
-
-    def first_norm(index, _):
+
+
+def first_back(image, gain, w_qkv, grad_packed, grad_mid, grad_image, grad_norm):
+    def block(index, _):
         rows = rows_at(index, ROWS)
         grad_rows = dot_rt(grad_packed[rows, :], w_qkv[...])
-        grad_in, grad_gain, grad_bias, unit = norm_back(image[rows, :], grad_rows, gain[0:1, :])
-        normed_first[rows, :] = (unit * gain[0:1, :] + bias[0:1, :]).astype(bf16)
+        grad_in, grad_gain, grad_bias, _ = norm_back(image[rows, :], grad_rows, gain[0:1, :])
         grad_image[rows, :] = grad_mid[rows, :] + grad_in
         grad_norm[0:1, :] += grad_gain
         grad_norm[2:3, :] += grad_bias
         return 0
 
-    lax.fori_loop(0, SEQ // ROWS, first_norm, 0)
+    lax.fori_loop(0, SEQ // ROWS, block, 0)
+
+
+def logit_grads(probs, grad_gates):
+    route = jnp.concatenate([grad_gates[group] for group in range(grad_gates.shape[0])], axis=0)
+    return probs[...] * (route - jnp.sum(probs[...] * route, axis=0, keepdims=True))
+
+
+def backward_scratch():
+    return [
+        pltpu.VMEM((SEQ, D), f32),
+        pltpu.VMEM((SEQ, D), bf16),
+        pltpu.VMEM((SEQ, D), bf16),
+        pltpu.VMEM((SEQ, 3 * D), bf16),
+        pltpu.VMEM((SEQ, PAIR), f32),
+        pltpu.VMEM((SEQ, PAIR), f32),
+        pltpu.VMEM((SEQ, D), bf16),
+    ]
+
+
+def backward_kernel(*refs):
+    image, cotangent, gain, bias, mid, w_qkv, w_proj, router = refs[:8]
+    packed, mixed, logs, mixes, grad_normed, grad_gates, probs = refs[8:15]
+    activations, grad_image, grad_norm, grad_router, grad_shared = refs[15:20]
+    grad_mid, grad_low, grad_mixed, grad_packed, grad_keys, grad_values, normed_first = refs[20:]
+    groups = mixes.shape[0]
+
+    def added(parts, rows):
+        total = parts[0, rows, :].astype(f32)
+        for source in range(1, groups):
+            total += parts[source, rows, :].astype(f32)
+        return total
+
+    activations[...] = mid[...] + added(mixes, slice(None))
+    second_back(
+        lambda rows: added(grad_normed, rows),
+        cotangent,
+        gain,
+        bias,
+        mid,
+        w_proj,
+        router,
+        logit_grads(probs, grad_gates),
+        grad_norm,
+        grad_router,
+        (grad_mid, grad_low, grad_mixed),
+    )
+    first_norm(image, gain, bias, normed_first)
+    grad_shared[:, 3 * D :] = dot_lt(mixed[...], grad_low[...]).astype(bf16)
+    attend_back(
+        packed,
+        grad_mixed,
+        logs,
+        grad_packed,
+        grad_keys,
+        grad_values,
+        lambda pair, index: None,
+        lambda pair, columns: None,
+    )
+    first_back(image, gain, w_qkv, grad_packed, grad_mid, grad_image, grad_norm)
     grad_shared[:, : 3 * D] = dot_lt(normed_first[...], grad_packed[...]).astype(bf16)
 
 
@@ -739,16 +1174,190 @@
         ),
         in_specs=[VMEM] * 15,
         out_specs=[VMEM] * 5,
-        scratch_shapes=[
-            pltpu.VMEM((SEQ, D), f32),
+        scratch_shapes=backward_scratch(),
+        compiler_params=params(),
+    )(*operands)
+
+
+def backward_sending_kernel(outers, *refs):
+    image, cotangent, gain, bias, mid, w_qkv, w_proj, router = refs[:8]
+    packed, mixed, logs, mixes, grad_rows, grad_gates, probs, grad_in, grad_out = refs[8:17]
+    activations, grad_image, grad_norm, grad_router, shard_qkv, shard_proj = refs[17:23]
+    shard_in, shard_out = refs[23:25]
+    grad_mid, grad_low, grad_mixed, grad_packed, grad_keys, grad_values, normed_first = refs[25:32]
+    norm_sums, router_sums, shared = refs[32:35]
+    land, joint, back_sent, back_landed = refs[35:39]
+    in_bufs, out_bufs, shared_bufs = refs[39:42], refs[42:45], refs[45:48]
+    scatter_sems = refs[48:52]
+    norm_pair, router_pair, task_pair = refs[52:56], refs[56:60], refs[60:64]
+    place = Place(outers)
+    bits = [1 << step for step in range((2 * outers).bit_length() - 1)]
+    place.greet(bits=bits[2:])
+    count = grad_in.shape[0]
+
+    def scatter(unit, block, size, bufs, at):
+        return Scatter(
+            place,
+            block,
+            size,
+            *[buf.at[at] for buf in bufs],
+            [sem.at[unit] for sem in scatter_sems],
+        )
+
+    big, stores = [], []
+    for expert in range(count):
+        for source, bufs, shard in ((grad_in, in_bufs, shard_in), (grad_out, out_bufs, shard_out)):
+            big.append(
+                scatter(
+                    len(big),
+                    lambda rows, source=source, expert=expert: source.at[expert, rows],
+                    shard.shape[1],
+                    bufs,
+                    expert,
+                )
+            )
+
+            def store(rows, shard=shard, expert=expert):
+                shard[expert] = rows
+
+            stores.append(store)
+    pieces = HEADS // 2 + 1
+    small = [
+        scatter(
+            len(big) + piece,
+            lambda rows, piece=piece: shared.at[piece, rows],
+            shard_proj.shape[0],
+            shared_bufs,
+            piece,
+        )
+        for piece in range(pieces)
+    ]
+    for unit in big:
+        unit.start()
+    back = Return(
+        place, lambda source: mixes.at[source], 1, land, joint, back_sent, back_landed
+    )
+    back.by_core(0)
+    back.to_core(0)
+    second_back(
+        lambda rows: grad_rows[rows, :],
+        cotangent,
+        gain,
+        bias,
+        mid,
+        w_proj,
+        router,
+        logit_grads(probs, grad_gates),
+        norm_sums,
+        router_sums,
+        (grad_mid, grad_low, grad_mixed),
+    )
+    back.to_across(0)
+    first_norm(image, gain, bias, normed_first)
+    shared[pieces - 1] = dot_lt(mixed[...], grad_low[...]).astype(bf16)
+    small[pieces - 1].start()
+    routers = PairSum(*router_pair)
+
+    def between(pair, index):
+        if pair == 1:
+            for step, bit in enumerate(bits):
+
+                @pl.when(index == step)
+                def _():
+                    if step:
+                        rows = routers.take(step - 1, dp=place.partner(bits[step - 1]))
+                    else:
+                        rows = router_sums[...]
+                    routers.give(step, rows, dp=place.partner(bit))
+
+    def done(pair, columns):
+        both = jnp.concatenate([grad_packed[:, part] for part in columns], axis=1)
+        shared[pair] = dot_lt(normed_first[...], both).astype(bf16)
+        small[pair].start()
+
+    attend_back(
+        packed, grad_mixed, logs, grad_packed, grad_keys, grad_values, between, done
+    )
+    first_back(image, gain, w_qkv, grad_packed, grad_mid, grad_image, norm_sums)
+    norms = PairSum(*norm_pair)
+    ways = [dict(dp=place.partner(bit)) for bit in bits]
+    ways += [dict(task=place.core), dict(task=place.across)]
+    norms.give(0, norm_sums[...], **ways[0])
+    grad_router[...] = routers.take(len(bits) - 1, dp=place.partner(bits[-1]))
+    activations[...] = mid[...] + back.finish(0)
+    units = big + small
+    for turn in range(len(units) + outers):
+        if 0 < turn < len(ways):
+            norms.give(turn, norms.take(turn - 1, **ways[turn - 1]), **ways[turn])
+        for step in range(outers - 1):
+            if 0 <= turn - step < len(units):
+                units[turn - step].hop(step)
+        if 0 <= turn - outers + 1 < len(big):
+            big[turn - outers + 1].finish(stores[turn - outers + 1])
+    grad_norm[...] = norms.take(len(ways) - 1, **ways[-1])
+    tasks = PairSum(*task_pair)
+    stage, land_task = task_pair[0], task_pair[1]
+    for piece in range(pieces):
+
+        def keep(rows, piece=piece):
+            stage[0, :, piece * D : (piece + 1) * D] = rows.astype(bf16)
+
+        small[piece].finish(keep)
+    tasks.swap(0, task=place.core).start()
+    rows = tasks.take(0, task=place.core)
+    tasks.give(1, rows, task=place.across)
+    rows = tasks.take(1, task=place.across)
+    shard_proj[...] = rows[:, (pieces - 1) * D :]
+    for pair in range(pieces - 1):
+        for part in range(3):
+            at = pair * D + part * PAIR
+            shard_qkv[:, part * D + pair * PAIR : part * D + (pair + 1) * PAIR] = rows[
+                :, at : at + PAIR
+            ]
+
+
+def backward_sending(*operands):
+    router, grad_in = operands[7], operands[15]
+    experts, size = router.shape[0], lax.axis_size("dp")
+    outers, count = size // 2, grad_in.shape[0]
+    thin, wide, pieces = D // size, FF // size, HEADS // 2 + 1
+    units, steps = 2 * count + pieces, size.bit_length() - 1
+
+    def pair_sum(steps, *dims, dtype=f32):
+        return [pltpu.VMEM((steps, *dims), dtype)] * 2 + [pltpu.SemaphoreType.DMA((steps,))] * 2
+
+    return pl.pallas_call(
+        functools.partial(backward_sending_kernel, outers),
+        out_shape=(
+            shape(SEQ, D),
+            shape(SEQ, D),
+            shape(8, D),
+            shape(experts, D),
+            shape(thin, 3 * D),
+            shape(thin, D),
+            shape(count, thin, FF),
+            shape(count, wide, D),
+        ),
+        in_specs=[VMEM] * 17,
+        out_specs=[VMEM] * 8,
+        scratch_shapes=backward_scratch()
+        + [
+            pltpu.VMEM((8, D), f32),
+            pltpu.VMEM((experts, D), f32),
+            pltpu.VMEM((pieces, D, D), bf16),
+            pltpu.VMEM((3, SEQ, D), bf16),
             pltpu.VMEM((SEQ, D), bf16),
-            pltpu.VMEM((SEQ, D), bf16),
-            pltpu.VMEM((SEQ, 3 * D), bf16),
-            pltpu.VMEM((SEQ, PAIR), f32),
-            pltpu.VMEM((SEQ, PAIR), f32),
-            pltpu.VMEM((SEQ, D), bf16),
-        ],
-        compiler_params=params(),
+            pltpu.SemaphoreType.DMA((3, 1)),
+            pltpu.SemaphoreType.DMA((3, 1)),
+        ]
+        + scatter_buffers(count, outers, thin, FF)
+        + scatter_buffers(count, outers, wide, D)
+        + scatter_buffers(pieces, outers, thin, D)
+        + scatter_semaphores(units, outers)
+        + pair_sum(steps + 2, 8, D)
+        + pair_sum(steps, experts, D)
+        + pair_sum(2, thin, 4 * D, dtype=bf16),
+        compiler_params=params(collective_id=2, has_side_effects=True),
     )(*operands)
 
 
@@ -802,9 +1411,47 @@
             router_rows,
             routes,
         )
-        mine = lax.axis_index("task") * local_count
-        slots = lax.dynamic_slice_in_dim(slots, mine, local_count, 1)
-        gates = lax.dynamic_slice_in_dim(gates, mine, local_count, 1)
+        (
+            late_in,
+            late_out,
+            grad_gates,
+            mixes,
+            grad_normed,
+            early_in,
+            early_out,
+            _,
+            _,
+        ) = expert_sending(normed, cot_rows, slots, gates, full_in, full_out, w_in, w_out)
+        (
+            activations,
+            grad_image,
+            grad_norm,
+            grad_router,
+            grad_qkv,
+            grad_proj,
+            grad_in,
+            grad_out,
+        ) = backward_sending(
+            image,
+            grad_rows,
+            norm_gain,
+            norm_bias,
+            mid,
+            full_qkv,
+            full_proj,
+            router_rows,
+            packed,
+            mixed,
+            logs,
+            mixes,
+            grad_normed,
+            grad_gates,
+            probs,
+            late_in,
+            late_out,
+        )
+        grad_in = jnp.concatenate([early_in, grad_in], axis=0)
+        grad_out = jnp.concatenate([early_out, grad_out], axis=0)
     else:
         full_qkv, full_proj, full_in, full_out = (
             lax.all_gather(w_qkv, "dp", axis=0, tiled=True),
@@ -826,42 +1473,43 @@
         cot_rows = lax.all_gather(grad_rows.astype(bf16), "task")
         slots = swap(slots.reshape(groups, local_count, SEQ))
         gates = swap(gates.reshape(groups, local_count, SEQ))
-    grad_in, grad_out, mixes, grad_normed, grad_gates = expert_part(
-        normed, cot_rows, slots, gates, full_in, full_out
-    )
-    activations, grad_image, grad_norm, grad_router, grad_shared = backward_part(
-        image,
-        grad_rows,
-        norm_gain,
-        norm_bias,
-        mid,
-        full_qkv,
-        full_proj,
-        router_rows,
-        packed,
-        mixed,
-        logs,
-        swap(mixes),
-        swap(grad_normed),
-        swap(grad_gates).reshape(experts, SEQ),
-        probs,
-    )
-    grad_in = lax.psum_scatter(grad_in, "dp", scatter_dimension=1, tiled=True)
-    grad_out = lax.psum_scatter(grad_out, "dp", scatter_dimension=1, tiled=True)
-    grad_shared = lax.psum_scatter(grad_shared, "dp", scatter_dimension=0, tiled=True)
-    grad_shared = lax.psum(grad_shared, "task").astype(f32)
-    grad_router = lax.psum(grad_router, "dp")
-    grad_norm = lax.psum(grad_norm, ("task", "dp"))
+        grad_in, grad_out, grad_gates, mixes, grad_normed = expert_part(
+            normed, cot_rows, slots, gates, full_in, full_out
+        )
+        activations, grad_image, grad_norm, grad_router, grad_shared = backward_part(
+            image,
+            grad_rows,
+            norm_gain,
+            norm_bias,
+            mid,
+            full_qkv,
+            full_proj,
+            router_rows,
+            packed,
+            mixed,
+            logs,
+            swap(mixes),
+            swap(grad_normed),
+            swap(grad_gates),
+            probs,
+        )
+        grad_in = lax.psum_scatter(grad_in, "dp", scatter_dimension=1, tiled=True).astype(f32)
+        grad_out = lax.psum_scatter(grad_out, "dp", scatter_dimension=1, tiled=True).astype(f32)
+        grad_shared = lax.psum_scatter(grad_shared, "dp", scatter_dimension=0, tiled=True)
+        grad_shared = lax.psum(grad_shared, "task").astype(f32)
+        grad_qkv, grad_proj = grad_shared[:, : 3 * D], grad_shared[:, 3 * D :]
+        grad_router = lax.psum(grad_router, "dp")
+        grad_norm = lax.psum(grad_norm, ("task", "dp"))
     return (
         activations.reshape(layer_input.shape),
         grad_image.reshape(layer_input.shape),
         grad_norm[:2],
-        grad_norm[2:],
-        grad_shared[:, : 3 * D],
-        grad_shared[:, 3 * D :],
+        grad_norm[2:4],
+        grad_qkv,
+        grad_proj,
         grad_router.T[None],
-        grad_in.astype(f32),
-        grad_out.astype(f32),
+        grad_in,
+        grad_out,
     )
 
 

time: 668 us -> 415 us (0.62)
  waiting for transfers between devices: 246 us -> 0 us
  Pallas kernels: 260 us -> 397 us
  blocking collectives: 128 us -> 0 us
  between operations: 14.5 us -> 1.53 us
    reduce_scatter x3 -> x0, waiting for transfers between devices: 208 us -> none  [the longest x1 97 us: local(): grad_in = lax.psum_scatter(grad_in, 'dp', scatter_dimension=1, tiled=True)]
    pallas_call x2, Pallas kernels: 129 us -> 318 us  [the longest x1 170 us: expert_sending(): pl.pallas_call(functools.partial(expert_sending_kernel, outers, early), o...]
    psum x2 -> x0, blocking collectives: 78.5 us -> none  [the longest x1 40 us: local(): grad_norm = lax.psum(grad_norm, ('task', 'dp'))]
    pallas_call x1, Pallas kernels: 131 us -> 79.4 us  [forward_sending(): pl.pallas_call(functools.partial(forward_sending_kernel, size // 2), out_...]
    all_to_all x2 -> x0, blocking collectives: 49.6 us -> none  [swap(): lax.all_to_all(array, 'task', split_axis=0, concat_axis=0, tiled=True)]
    all_to_all x1 -> x0, waiting for transfers between devices: 36.2 us -> none  [swap(): lax.all_to_all(array, 'task', split_axis=0, concat_axis=0, tiled=True)]
  transfers between devices with their start and end apart: 5 -> 0, of which waited for: 4 -> 0; matrix products, arithmetic and copies ran while one was open for 1% -> 0% of each run, Pallas kernels for 0% -> 0%
where the time goes in v3:
time: 415 us; the launch traced here: 411 us
  Pallas kernels  397 us (96%)
  local copies, waits for them, and re-layouts  8.95 us (2%)
    pallas_call x1, Pallas kernels, expert_sending(): pl.pallas_call(functools.partial(expert_sending_kernel, outers, early), o...  170 us
    pallas_call x1, Pallas kernels, backward_sending(): pl.pallas_call(functools.partial(backward_sending_kernel, outers), out_sh...  147 us
    pallas_call x1, Pallas kernels, forward_sending(): pl.pallas_call(functools.partial(forward_sending_kernel, size // 2), out_...  79.4 us

profile of v3, /device:TPU:0, one launch (start us, length us, event | category | flops | bytes accessed | tf_op | source)
XLA Modules:
  0.0 410.9 jit_solution(16535459362956844353)
XLA Ops:
  1.3 1.7 copy.20
  3.0 79.4 %shard_map.178 = (f32[1024,384]{1,0:T(8,128)}, bf16[1024,1152]{1,0:T(8,128)(2,1)}, bf16[1024,384]{1,0:T(8,128)(2,1)}, f32[8,1024]{1,0:T(8,128)}, f32[16,1024]{1,...) custom-call(s32[1]{0:T(128)S(6)} %copy.26.top_count, ...), custom_call_target="tpu_custom_call" | custom-call | tf_op jit(solution)/shard_map/pallas_call | solution.py:611
  82.5 170.4 %shard_map.179 = (bf16[2,384,1536]{2,1,0:T(8,128)(2,1)}, bf16[2,1536,384]{2,1,0:T(8,128)(2,1)}, f32[4,4,1024]{2,1,0:T(4,128)}, bf16[4,1024,384]{2,1,0:T(8,128)(2...) custom-call(bf16[4,1024,384]{2,1,0:T(8,128)(2,1)} %get-tuple-element, ...), custom_call_target="tpu_custom_call" | custom-call | tf_op jit(solution)/shard_map/pallas_call | solution.py:970
  252.9 0.0 copy-start.3
  252.9 147.3 %shard_map.180 = (f32[1024,384]{1,0:T(8,128)}, f32[1024,384]{1,0:T(8,128)}, f32[8,384]{1,0:T(8,128)}, f32[16,384]{1,0:T(8,128)}, f32[48,1152]{1,0:T(8,128)}, /*i...) custom-call(f32[1024,384]{1,0:T(8,128)} %bitcast.12, f32[1024,384]{1,0:T(8,128)} %bitcast.14, ...), custom_call_target="tpu_custom_call" | custom-call | tf_op jit(solution)/shard_map/pallas_call | solution.py:1329
  400.2 0.0 copy-start.2
  400.2 0.0 copy-start.4
  400.3 1.4 fusion
  401.7 0.0 copy-done.3
  401.7 2.2 pad_maximum_fusion
  403.8 0.0 copy-done.2
  403.8 0.0 copy-done.4
  403.8 0.0 copy-start.1
  403.8 1.1 pad_maximum_fusion.1
  404.9 0.7 copy-done.1
  405.7 0.0 copy-start
  405.7 1.1 copy.27
  406.8 0.8 copy-done
  407.6 0.0 copy-start.5
  407.6 0.0 copy-start.6
  407.6 0.0 copy-start.7
  407.6 1.1 copy.28
  408.8 0.0 copy-done.5
  408.8 0.7 copy.29
  409.5 0.0 copy-done.6
  409.5 0.6 copy.30
  410.1 0.0 copy-done.7
  410.1 0.6 copy.31
Async XLA Ops:
  252.9 148.8 %copy-start.3 = (f32[2,48,1536]{2,1,0:T(8,128)S(1)}, f32[2,48,1536]{2,1,0:T(8,128)}, u32[]{:S(2)}) copy-start(f32[2,48,1536]{2,1,0:T(8,128)} %get-tuple-element.61) | copy-start | bytes 1769476
  400.2 3.6 copy-start.2
  400.2 3.6 copy-start.4
  403.8 1.8 copy-start.1
  405.7 2.0 copy-start
  407.6 1.2 copy-start.5
  407.6 1.8 copy-start.6
  407.6 2.5 copy-start.7

commit v4 on v3

--- a/solution.py
+++ b/solution.py
@@ -29,6 +29,7 @@
 QUERY_BWD = 256
 ROWS = 256
 RETURNS = 2
+TURNS = (3, 9)
 
 VMEM = pl.BlockSpec(memory_space=pltpu.VMEM)
 SMEM = pl.BlockSpec(memory_space=pltpu.SMEM)
@@ -296,6 +297,16 @@
                         self.along(other, other, place.dp).wait_send()
 
             self.to_side(outer).wait_send()
+
+
+def scatter_turn(units, stores, turn):
+    outers = units[0].place.outers
+    for step in range(outers - 1):
+        if 0 <= turn - step < len(units):
+            units[turn - step].hop(step)
+    last = turn - outers + 1
+    if 0 <= last < len(units) and stores[last]:
+        units[last].finish(stores[last])
 
 
 class PairSum:
@@ -856,6 +867,8 @@
                 steps += [scatters[2 * expert].start, scatters[2 * expert + 1].start]
             else:
                 steps += [copy.start for copy in keep(expert - early)]
+        if expert == local_count - 1 and point in (0, 2):
+            steps.append(lambda: scatter_turn(scatters, stores, point // 2))
         return steps
 
     def body(expert, _):
@@ -914,11 +927,13 @@
     back = Return(
         place, lambda source: part(hidden, source), RETURNS, land, joint, sent, landed
     )
-    for source, after in (
-        (place.far, back.by_core),
-        (place.across, back.to_across),
-        (place.core, back.to_core),
-        (place.task, None),
+    for order, (source, after) in enumerate(
+        (
+            (place.far, back.by_core),
+            (place.across, back.to_across),
+            (place.core, back.to_core),
+            (place.task, None),
+        )
     ):
 
         def store(piece, rows, mix, grad, source=source, after=after):
@@ -928,18 +943,16 @@
                 after(piece)
 
         combine(slots, first, local_count, work[6], columns, source, store)
+        if order:
+            scatter_turn(scatters, stores, 1 + order)
     keeps = [
         pltpu.make_async_copy(part(grad_pre, source), mixes.at[source], mix_sem.at[source])
         for source in range(mixes.shape[0])
     ]
     for copy in keeps:
         copy.start()
-    for turn in range(len(scatters) + outers):
-        for step in range(outers - 1):
-            if 0 <= turn - step < len(scatters):
-                scatters[turn - step].hop(step)
-        if 0 <= turn - outers + 1 < len(scatters):
-            scatters[turn - outers + 1].finish(stores[turn - outers + 1])
+    for turn in range(5, len(scatters) + outers):
+        scatter_turn(scatters, stores, turn)
     for piece in range(RETURNS):
         grad_rows[back.rows(piece), :] = back.finish(piece)
     for way in range(3):
@@ -1257,8 +1270,14 @@
     shared[pieces - 1] = dot_lt(mixed[...], grad_low[...]).astype(bf16)
     small[pieces - 1].start()
     routers = PairSum(*router_pair)
+    blocks = SEQ // QUERY_BWD
+
+    units, keeps = big + small, stores + [None] * pieces
 
     def between(pair, index):
+        for turn, at in enumerate(TURNS):
+            if at // blocks == pair:
+                pl.when(index == at % blocks)(lambda turn=turn: scatter_turn(units, keeps, turn))
         if pair == 1:
             for step, bit in enumerate(bits):
 
@@ -1285,15 +1304,11 @@
     norms.give(0, norm_sums[...], **ways[0])
     grad_router[...] = routers.take(len(bits) - 1, dp=place.partner(bits[-1]))
     activations[...] = mid[...] + back.finish(0)
-    units = big + small
-    for turn in range(len(units) + outers):
-        if 0 < turn < len(ways):
-            norms.give(turn, norms.take(turn - 1, **ways[turn - 1]), **ways[turn])
-        for step in range(outers - 1):
-            if 0 <= turn - step < len(units):
-                units[turn - step].hop(step)
-        if 0 <= turn - outers + 1 < len(big):
-            big[turn - outers + 1].finish(stores[turn - outers + 1])
+    for turn in range(len(TURNS), len(units) + outers):
+        step = turn - len(TURNS) + 1
+        if step < len(ways):
+            norms.give(step, norms.take(step - 1, **ways[step - 1]), **ways[step])
+        scatter_turn(units, keeps, turn)
     grad_norm[...] = norms.take(len(ways) - 1, **ways[-1])
     tasks = PairSum(*task_pair)
     stage, land_task = task_pair[0], task_pair[1]

time: 415 us -> 366 us (0.88)
  Pallas kernels: 397 us -> 348 us
    pallas_call x1, Pallas kernels: 170 us -> 139 us  [expert_sending(): pl.pallas_call(functools.partial(expert_sending_kernel, outers, early), o...]
    pallas_call x1, Pallas kernels: 147 us -> 130 us  [backward_sending(): pl.pallas_call(functools.partial(backward_sending_kernel, outers), out_sh...]
where the time goes in v4:
time: 366 us; the launch traced here: 362 us
  Pallas kernels  348 us (95%)
  local copies, waits for them, and re-layouts  8.95 us (2%)
    pallas_call x1, Pallas kernels, expert_sending(): pl.pallas_call(functools.partial(expert_sending_kernel, outers, early), o...  139 us
    pallas_call x1, Pallas kernels, backward_sending(): pl.pallas_call(functools.partial(backward_sending_kernel, outers), out_sh...  130 us
    pallas_call x1, Pallas kernels, forward_sending(): pl.pallas_call(functools.partial(forward_sending_kernel, size // 2), out_...  79.4 us
    unnamed x22, local copies, waits for them, and re-layouts  7.55 us

profile of v4, /device:TPU:0, one launch (start us, length us, event | category | flops | bytes accessed | tf_op | source)
XLA Modules:
  0.0 361.8 jit_solution(17655950083908428034)
XLA Ops:
  1.3 1.7 copy.20
  3.0 79.4 %shard_map.178 = (f32[1024,384]{1,0:T(8,128)}, bf16[1024,1152]{1,0:T(8,128)(2,1)}, bf16[1024,384]{1,0:T(8,128)(2,1)}, f32[8,1024]{1,0:T(8,128)}, f32[16,1024]{1,...) custom-call(s32[1]{0:T(128)S(6)} %copy.26.top_count, ...), custom_call_target="tpu_custom_call" | custom-call | tf_op jit(solution)/shard_map/pallas_call | solution.py:622
  82.5 138.5 %shard_map.179 = (bf16[2,384,1536]{2,1,0:T(8,128)(2,1)}, bf16[2,1536,384]{2,1,0:T(8,128)(2,1)}, f32[4,4,1024]{2,1,0:T(4,128)}, bf16[4,1024,384]{2,1,0:T(8,128)(2...) custom-call(bf16[4,1024,384]{2,1,0:T(8,128)(2,1)} %get-tuple-element, ...), custom_call_target="tpu_custom_call" | custom-call | tf_op jit(solution)/shard_map/pallas_call | solution.py:983
  221.0 0.0 copy-start.3
  221.0 129.9 %shard_map.180 = (f32[1024,384]{1,0:T(8,128)}, f32[1024,384]{1,0:T(8,128)}, f32[8,384]{1,0:T(8,128)}, f32[16,384]{1,0:T(8,128)}, f32[48,1152]{1,0:T(8,128)}, /*i...) custom-call(f32[1024,384]{1,0:T(8,128)} %bitcast.12, f32[1024,384]{1,0:T(8,128)} %bitcast.14, ...), custom_call_target="tpu_custom_call" | custom-call | tf_op jit(solution)/shard_map/pallas_call | solution.py:1344
  350.9 0.0 copy-start.2
  350.9 0.0 copy-start.4
  350.9 1.4 fusion
  352.3 0.0 copy-done.3
  352.3 2.2 pad_maximum_fusion
  354.5 0.0 copy-done.2
  354.5 0.0 copy-done.4
  354.5 0.0 copy-start.1
  354.5 1.1 pad_maximum_fusion.1
  355.6 0.7 copy-done.1
  356.3 0.0 copy-start
  356.3 1.1 copy.27
  357.4 0.8 copy-done
  358.3 0.0 copy-start.5
  358.3 0.0 copy-start.6
  358.3 0.0 copy-start.7
  358.3 1.1 copy.28
  359.4 0.0 copy-done.5
  359.4 0.7 copy.29
  360.1 0.0 copy-done.6
  360.1 0.6 copy.30
  360.7 0.0 copy-done.7
  360.7 0.6 copy.31
Async XLA Ops:
  221.0 131.3 %copy-start.3 = (f32[2,48,1536]{2,1,0:T(8,128)S(1)}, f32[2,48,1536]{2,1,0:T(8,128)}, u32[]{:S(2)}) copy-start(f32[2,48,1536]{2,1,0:T(8,128)} %get-tuple-element.61) | copy-start | bytes 1769476
  350.9 3.6 copy-start.2
  350.9 3.6 copy-start.4
  354.5 1.8 copy-start.1
  356.3 2.0 copy-start
  358.3 1.2 copy-start.5
  358.3 1.8 copy-start.6
  358.3 2.5 copy-start.7

commit v5 on v4

--- a/solution.py
+++ b/solution.py
@@ -29,7 +29,7 @@
 QUERY_BWD = 256
 ROWS = 256
 RETURNS = 2
-TURNS = (3, 9)
+TURNS = (2, 5, 8, 11)
 
 VMEM = pl.BlockSpec(memory_space=pltpu.VMEM)
 SMEM = pl.BlockSpec(memory_space=pltpu.SMEM)
@@ -107,30 +107,32 @@
         self.across = self.task + 2 - 4 * (self.task // 2)
         self.far = self.across + 1 - 2 * (self.task % 2)
 
-    def partner(self, bit):
-        return self.dp + bit - 2 * bit * (self.dp // bit % 2)
-
-    def greet(self, far=False, bits=()):
-        barrier = pltpu.get_barrier_semaphore()
-
-        def signal(**device):
-            pl.semaphore_signal(
-                barrier, inc=1, device_id=device, device_id_type=pl.DeviceIdType.MESH
-            )
-
-        pl.when(self.has_up)(lambda: signal(dp=self.up))
-        pl.when(self.has_down)(lambda: signal(dp=self.down))
-        signal(dp=self.side)
-        signal(task=self.core)
-        signal(task=self.across)
+    def signal(self, **device):
+        pl.semaphore_signal(
+            pltpu.get_barrier_semaphore(),
+            inc=1,
+            device_id=device,
+            device_id_type=pl.DeviceIdType.MESH,
+        )
+
+    def greet(self, far=False):
+        pl.when(self.has_up)(lambda: self.signal(dp=self.up))
+        pl.when(self.has_down)(lambda: self.signal(dp=self.down))
+        self.signal(dp=self.side)
+        self.signal(task=self.core)
+        self.signal(task=self.across)
         if far:
-            signal(task=self.far)
-        for bit in bits:
-            signal(dp=self.partner(bit))
-        others = 3 + int(far) + len(bits)
-        pl.semaphore_wait(
-            barrier, others + self.has_up.astype(jnp.int32) + self.has_down.astype(jnp.int32)
-        )
+            self.signal(task=self.far)
+        others = 3 + int(far) + self.has_up.astype(jnp.int32) + self.has_down.astype(jnp.int32)
+        pl.semaphore_wait(pltpu.get_barrier_semaphore(), others)
+
+    def greet_all(self, groups):
+        size = 2 * self.outers
+        for ahead in range(1, size):
+            self.signal(dp=lax.rem(self.dp + ahead, size))
+        for ahead in range(1, groups):
+            self.signal(task=lax.rem(self.task + ahead, groups))
+        pl.semaphore_wait(pltpu.get_barrier_semaphore(), size + groups - 2)
 
 
 class Gather:
@@ -305,30 +307,37 @@
         if 0 <= turn - step < len(units):
             units[turn - step].hop(step)
     last = turn - outers + 1
-    if 0 <= last < len(units) and stores[last]:
+    if 0 <= last < len(units):
         units[last].finish(stores[last])
 
 
-class PairSum:
-    def __init__(self, stage, land, sent, landed):
-        self.stage, self.land, self.sent, self.landed = stage, land, sent, landed
-
-    def swap(self, step, **device):
+class Spread:
+    def __init__(self, axis, place, count, land, sent, landed):
+        self.axis, self.me, self.count = axis, getattr(place, axis), count
+        self.land, self.sent, self.landed = land, sent, landed
+
+    def move(self, source, ahead):
         return remote(
-            self.stage.at[step],
-            self.land.at[step],
-            self.sent.at[step],
-            self.landed.at[step],
-            **device,
-        )
-
-    def give(self, step, rows, **device):
-        self.stage[step] = rows.astype(self.stage.dtype)
-        self.swap(step, **device).start()
-
-    def take(self, step, **device):
-        self.swap(step, **device).wait()
-        return self.stage[step].astype(f32) + self.land[step].astype(f32)
+            self.land.at[source],
+            self.land.at[source],
+            self.sent.at[ahead - 1],
+            self.landed.at[ahead - 1],
+            **{self.axis: lax.rem(self.me + ahead, self.count)},
+        )
+
+    def give(self, rows):
+        self.land[self.me] = rows.astype(self.land.dtype)
+        for ahead in range(1, self.count):
+            self.move(self.me, ahead).start()
+
+    def take(self):
+        for ahead in range(1, self.count):
+            self.move(lax.rem(self.me + self.count - ahead, self.count), ahead).wait_recv()
+            self.move(self.me, ahead).wait_send()
+        total = self.land[0].astype(f32)
+        for index in range(1, self.count):
+            total += self.land[index].astype(f32)
+        return total
 
 
 class Return:
@@ -1202,11 +1211,13 @@
     land, joint, back_sent, back_landed = refs[35:39]
     in_bufs, out_bufs, shared_bufs = refs[39:42], refs[42:45], refs[45:48]
     scatter_sems = refs[48:52]
-    norm_pair, router_pair, task_pair = refs[52:56], refs[56:60], refs[60:64]
     place = Place(outers)
-    bits = [1 << step for step in range((2 * outers).bit_length() - 1)]
-    place.greet(bits=bits[2:])
-    count = grad_in.shape[0]
+    count, groups, size = grad_in.shape[0], mixes.shape[0], 2 * outers
+    place.greet_all(groups)
+    norms = Spread("dp", place, size, *refs[52:55])
+    norms_task = Spread("task", place, groups, *refs[55:58])
+    routers = Spread("dp", place, size, *refs[58:61])
+    task_refs = refs[61:64]
 
     def scatter(unit, block, size, bufs, at):
         return Scatter(
@@ -1269,25 +1280,18 @@
     first_norm(image, gain, bias, normed_first)
     shared[pieces - 1] = dot_lt(mixed[...], grad_low[...]).astype(bf16)
     small[pieces - 1].start()
-    routers = PairSum(*router_pair)
+    routers.give(router_sums[...])
     blocks = SEQ // QUERY_BWD
-
-    units, keeps = big + small, stores + [None] * pieces
+    totals = [
+        Spread("task", place, groups, *[ref.at[piece] for ref in task_refs])
+        for piece in range(pieces)
+    ]
+    units, keeps = big + small, stores + [one.give for one in totals]
 
     def between(pair, index):
         for turn, at in enumerate(TURNS):
             if at // blocks == pair:
                 pl.when(index == at % blocks)(lambda turn=turn: scatter_turn(units, keeps, turn))
-        if pair == 1:
-            for step, bit in enumerate(bits):
-
-                @pl.when(index == step)
-                def _():
-                    if step:
-                        rows = routers.take(step - 1, dp=place.partner(bits[step - 1]))
-                    else:
-                        rows = router_sums[...]
-                    routers.give(step, rows, dp=place.partner(bit))
 
     def done(pair, columns):
         both = jnp.concatenate([grad_packed[:, part] for part in columns], axis=1)
@@ -1298,37 +1302,22 @@
         packed, grad_mixed, logs, grad_packed, grad_keys, grad_values, between, done
     )
     first_back(image, gain, w_qkv, grad_packed, grad_mid, grad_image, norm_sums)
-    norms = PairSum(*norm_pair)
-    ways = [dict(dp=place.partner(bit)) for bit in bits]
-    ways += [dict(task=place.core), dict(task=place.across)]
-    norms.give(0, norm_sums[...], **ways[0])
-    grad_router[...] = routers.take(len(bits) - 1, dp=place.partner(bits[-1]))
+    norms.give(norm_sums[...])
     activations[...] = mid[...] + back.finish(0)
-    for turn in range(len(TURNS), len(units) + outers):
-        step = turn - len(TURNS) + 1
-        if step < len(ways):
-            norms.give(step, norms.take(step - 1, **ways[step - 1]), **ways[step])
+    grad_router[...] = routers.take()
+    for turn in range(len(TURNS), len(units) + outers - 1):
         scatter_turn(units, keeps, turn)
-    grad_norm[...] = norms.take(len(ways) - 1, **ways[-1])
-    tasks = PairSum(*task_pair)
-    stage, land_task = task_pair[0], task_pair[1]
+        if turn == len(units) - 1:
+            norms_task.give(norms.take())
+    grad_norm[...] = norms_task.take()
     for piece in range(pieces):
-
-        def keep(rows, piece=piece):
-            stage[0, :, piece * D : (piece + 1) * D] = rows.astype(bf16)
-
-        small[piece].finish(keep)
-    tasks.swap(0, task=place.core).start()
-    rows = tasks.take(0, task=place.core)
-    tasks.give(1, rows, task=place.across)
-    rows = tasks.take(1, task=place.across)
-    shard_proj[...] = rows[:, (pieces - 1) * D :]
-    for pair in range(pieces - 1):
-        for part in range(3):
-            at = pair * D + part * PAIR
-            shard_qkv[:, part * D + pair * PAIR : part * D + (pair + 1) * PAIR] = rows[
-                :, at : at + PAIR
-            ]
+        rows = totals[piece].take()
+        if piece == pieces - 1:
+            shard_proj[...] = rows
+        else:
+            for part in range(3):
+                at = part * D + piece * PAIR
+                shard_qkv[:, at : at + PAIR] = rows[:, part * PAIR : (part + 1) * PAIR]
 
 
 def backward_sending(*operands):
@@ -1336,10 +1325,12 @@
     experts, size = router.shape[0], lax.axis_size("dp")
     outers, count = size // 2, grad_in.shape[0]
     thin, wide, pieces = D // size, FF // size, HEADS // 2 + 1
-    units, steps = 2 * count + pieces, size.bit_length() - 1
-
-    def pair_sum(steps, *dims, dtype=f32):
-        return [pltpu.VMEM((steps, *dims), dtype)] * 2 + [pltpu.SemaphoreType.DMA((steps,))] * 2
+    units, groups = 2 * count + pieces, lax.axis_size("task")
+
+    def spread(peers, *dims, lead=(), dtype=f32):
+        return [pltpu.VMEM((*lead, peers, *dims), dtype)] + [
+            pltpu.SemaphoreType.DMA((*lead, peers - 1))
+        ] * 2
 
     return pl.pallas_call(
         functools.partial(backward_sending_kernel, outers),
@@ -1369,9 +1360,10 @@
         + scatter_buffers(count, outers, wide, D)
         + scatter_buffers(pieces, outers, thin, D)
         + scatter_semaphores(units, outers)
-        + pair_sum(steps + 2, 8, D)
-        + pair_sum(steps, experts, D)
-        + pair_sum(2, thin, 4 * D, dtype=bf16),
+        + spread(size, 8, D)
+        + spread(groups, 8, D)
+        + spread(size, experts, D)
+        + spread(groups, thin, D, lead=(pieces,), dtype=bf16),
         compiler_params=params(collective_id=2, has_side_effects=True),
     )(*operands)
 

time: 366 us -> 330 us (0.902)
  Pallas kernels: 348 us -> 312 us
    pallas_call x1, Pallas kernels: 130 us -> 93.7 us  [backward_sending(): pl.pallas_call(functools.partial(backward_sending_kernel, outers), out_sh...]
where the time goes in v5:
time: 330 us; the launch traced here: 326 us
  Pallas kernels  312 us (95%)
  local copies, waits for them, and re-layouts  8.95 us (3%)
    pallas_call x1, Pallas kernels, expert_sending(): pl.pallas_call(functools.partial(expert_sending_kernel, outers, early), o...  139 us
    pallas_call x1, Pallas kernels, backward_sending(): pl.pallas_call(functools.partial(backward_sending_kernel, outers), out_sh...  93.7 us
    pallas_call x1, Pallas kernels, forward_sending(): pl.pallas_call(functools.partial(forward_sending_kernel, size // 2), out_...  79.4 us
    unnamed x22, local copies, waits for them, and re-layouts  7.55 us

profile of v5, /device:TPU:0, one launch (start us, length us, event | category | flops | bytes accessed | tf_op | source)
XLA Modules:
  0.0 325.7 jit_solution(11100337445663610455)
XLA Ops:
  1.3 1.7 copy.20
  3.0 79.4 %shard_map.178 = (f32[1024,384]{1,0:T(8,128)}, bf16[1024,1152]{1,0:T(8,128)(2,1)}, bf16[1024,384]{1,0:T(8,128)(2,1)}, f32[8,1024]{1,0:T(8,128)}, f32[16,1024]{1,...) custom-call(s32[1]{0:T(128)S(6)} %copy.26.top_count, ...), custom_call_target="tpu_custom_call" | custom-call | tf_op jit(solution)/shard_map/pallas_call | solution.py:631
  82.5 138.5 %shard_map.179 = (bf16[2,384,1536]{2,1,0:T(8,128)(2,1)}, bf16[2,1536,384]{2,1,0:T(8,128)(2,1)}, f32[4,4,1024]{2,1,0:T(4,128)}, bf16[4,1024,384]{2,1,0:T(8,128)(2...) custom-call(bf16[4,1024,384]{2,1,0:T(8,128)(2,1)} %get-tuple-element, ...), custom_call_target="tpu_custom_call" | custom-call | tf_op jit(solution)/shard_map/pallas_call | solution.py:992
  221.0 0.0 copy-start.3
  221.0 93.7 %shard_map.180 = (f32[1024,384]{1,0:T(8,128)}, f32[1024,384]{1,0:T(8,128)}, f32[8,384]{1,0:T(8,128)}, f32[16,384]{1,0:T(8,128)}, f32[48,1152]{1,0:T(8,128)}, /*i...) custom-call(f32[1024,384]{1,0:T(8,128)} %bitcast.12, f32[1024,384]{1,0:T(8,128)} %bitcast.14, ...), custom_call_target="tpu_custom_call" | custom-call | tf_op jit(solution)/shard_map/pallas_call | solution.py:1335
  314.7 0.0 copy-start.2
  314.7 0.0 copy-start.4
  314.8 1.4 fusion
  316.2 0.0 copy-done.3
  316.2 2.2 pad_maximum_fusion
  318.3 0.0 copy-done.2
  318.3 0.0 copy-done.4
  318.3 0.0 copy-start.1
  318.3 1.1 pad_maximum_fusion.1
  319.4 0.7 copy-done.1
  320.2 0.0 copy-start
  320.2 1.1 copy.27
  321.3 0.8 copy-done
  322.1 0.0 copy-start.5
  322.1 0.0 copy-start.6
  322.1 0.0 copy-start.7
  322.1 1.1 copy.28
  323.3 0.0 copy-done.5
  323.3 0.7 copy.29
  324.0 0.0 copy-done.6
  324.0 0.6 copy.30
  324.6 0.0 copy-done.7
  324.6 0.6 copy.31
Async XLA Ops:
  221.0 95.2 %copy-start.3 = (f32[2,48,1536]{2,1,0:T(8,128)S(1)}, f32[2,48,1536]{2,1,0:T(8,128)}, u32[]{:S(2)}) copy-start(f32[2,48,1536]{2,1,0:T(8,128)} %get-tuple-element.61) | copy-start | bytes 1769476
  314.7 3.6 %copy-start.2 = (f32[2,192,384]{2,1,0:T(8,128)S(1)}, f32[2,192,384]{2,1,0:T(8,128)}, u32[]{:S(2)}) copy-start(f32[2,192,384]{2,1,0:T(8,128)} %get-tuple-element.63) | copy-start | bytes 1769476
  314.7 3.6 %copy-start.4 = (f32[2,192,384]{2,1,0:T(8,128)S(1)}, f32[2,192,384]{2,1,0:T(8,128)}, u32[]{:S(2)}) copy-start(f32[2,192,384]{2,1,0:T(8,128)} %get-tuple-element.64) | copy-start | bytes 1769476
  318.3 1.8 copy-start.1
  320.2 2.0 copy-start
  322.1 1.2 copy-start.5
  322.1 1.8 copy-start.6
  322.1 2.5 copy-start.7

commit v6 on v5

--- a/solution.py
+++ b/solution.py
@@ -29,7 +29,29 @@
 QUERY_BWD = 256
 ROWS = 256
 RETURNS = 2
-TURNS = (2, 5, 8, 11)
+
+GATHER_WHOLE = ((0, 0), (0, 1), (1, 0), (1, 1))
+GATHER_SPLIT = ((2, 0), (2, 1))
+GATHER_LATE = ((3, 0), (3, 1))
+SCATTER_EARLY = ((0, 0), (0, 1), (1, 0))
+SCATTER_SPLIT = ((1, 1), (2, 0))
+SCATTER_LATE = ((2, 1), (3, 0), (3, 1))
+EARLY_EXPERTS = 2
+
+GATHER_POINTS = ((0, 2), (1, 1), (1, 4))
+SCATTER_POINTS = ((3, 1), (3, 3))
+COMBINE_TURNS = (1, 2, 3)
+
+BACKWARD_POINTS = {
+    3: ("s1", "u0",),
+    8: ("t1", "s2", "v0",),
+    11: ("u1",),
+}
+BACKWARD_THEN = (
+    ("w0", "t2", "s3", "v1", "u2", "30", "00", "10",),
+    ("w1", "t3", "v2", "u3", "20", "31", "01", "11", "w2", "v3", "21", "32", "02", "12", "33", "03", "22", "13", "23", "w3",),
+)
+
 
 VMEM = pl.BlockSpec(memory_space=pltpu.VMEM)
 SMEM = pl.BlockSpec(memory_space=pltpu.SMEM)
@@ -140,59 +162,103 @@
         self.place, self.shards = place, shards
         self.sent, self.landed, self.stay = sent, landed, stay
 
-    def move(self, unit, source, way, device, first=False):
-        own, size, full = self.shards[unit]
+    def move(self, unit, source, way, device, first=None):
+        _, size, full, _ = self.shards[unit]
         target = full.at[rows_at(source, size)]
         return remote(
-            own if first else target,
+            target if first is None else first,
             target,
             self.sent.at[unit, source, way],
             self.landed.at[unit, source],
             dp=device,
         )
 
-    def local(self, unit):
-        own, size, full = self.shards[unit]
-        target = full.at[rows_at(self.place.dp, size)]
-        return pltpu.make_async_copy(own, target, self.stay.at[unit])
+    def local(self, unit, outer):
+        own, size, full, mode = self.shards[unit]
+        rows = rows_at(2 * outer + self.place.inner, size)
+        source = own.at[rows] if mode == "side" else own
+        return pltpu.make_async_copy(source, full.at[rows], self.stay.at[unit, outer])
+
+    def along(self, unit, source, up, down):
+        place = self.place
+        if up:
+            pl.when(place.has_up)(lambda: self.move(unit, source, 0, place.up).start())
+        if down:
+            pl.when(place.has_down)(lambda: self.move(unit, source, 1, place.down).start())
+
+    def to_side(self, unit, outer):
+        own, size = self.shards[unit][:2]
+        source = 2 * outer + self.place.inner
+        return self.move(unit, source, 2, self.place.side, own.at[rows_at(source, size)])
 
     def start(self, unit):
         place = self.place
-        pl.when(place.has_up)(lambda: self.move(unit, place.dp, 0, place.up, True).start())
-        pl.when(place.has_down)(lambda: self.move(unit, place.dp, 1, place.down, True).start())
-        self.move(unit, place.dp, 2, place.side, True).start()
-        self.local(unit).start()
+        own, mode = self.shards[unit][0], self.shards[unit][3]
+        if mode == "side":
+            for outer in range(place.outers):
+                self.to_side(unit, outer).start()
+                self.local(unit, outer).start()
+            return
+        if mode == "turned":
+            self.move(unit, place.dp, 2, place.side, own).start()
+        pl.when(place.has_up)(lambda: self.move(unit, place.dp, 0, place.up, own).start())
+        pl.when(place.has_down)(lambda: self.move(unit, place.dp, 1, place.down, own).start())
+        if mode == "both":
+            self.move(unit, place.dp, 2, place.side, own).start()
+        self.local(unit, place.outer).start()
 
     def step(self, unit, hop):
-        place = self.place
-
-        @pl.when(place.outer >= hop)
-        def _():
-            source = place.dp - 2 * hop
-            self.move(unit, source, 0, place.dp).wait_recv()
-            pl.when(place.has_up)(lambda: self.move(unit, source, 0, place.up).start())
-            self.move(unit, source, 2, place.side).start()
-
-        @pl.when(place.outer + hop < place.outers)
-        def _():
-            source = place.dp + 2 * hop
-            self.move(unit, source, 1, place.dp).wait_recv()
-            pl.when(place.has_down)(lambda: self.move(unit, source, 1, place.down).start())
-            self.move(unit, source, 2, place.side).start()
+        place, mode = self.place, self.shards[unit][3]
+        if hop == 0:
+            self.move(unit, place.side, 0, place.dp).wait_recv()
+            self.along(unit, place.side, True, True)
+            return
+        for column in (place.dp, place.side) if mode == "turned" else (place.dp,):
+
+            @pl.when(place.outer >= hop)
+            def _():
+                self.move(unit, column - 2 * hop, 0, place.dp).wait_recv()
+                self.along(unit, column - 2 * hop, True, False)
+                if mode == "both":
+                    self.move(unit, column - 2 * hop, 2, place.side).start()
+
+            @pl.when(place.outer + hop < place.outers)
+            def _():
+                self.move(unit, column + 2 * hop, 1, place.dp).wait_recv()
+                self.along(unit, column + 2 * hop, False, True)
+                if mode == "both":
+                    self.move(unit, column + 2 * hop, 2, place.side).start()
 
     def finish(self, unit):
-        place = self.place
-        self.local(unit).wait()
+        place, mode = self.place, self.shards[unit][3]
+        if mode != "side":
+            self.local(unit, place.outer).wait()
+        if mode == "turned":
+            self.move(unit, place.dp, 2, place.side).wait_send()
         for outer in range(place.outers):
             own, other = 2 * outer + place.inner, 2 * outer + 1 - place.inner
-            self.move(unit, other, 2, place.dp).wait_recv()
-            self.move(unit, own, 2, place.side).wait_send()
-            pl.when((outer <= place.outer) & place.has_up)(
-                lambda own=own: self.move(unit, own, 0, place.up).wait_send()
-            )
-            pl.when((outer >= place.outer) & place.has_down)(
-                lambda own=own: self.move(unit, own, 1, place.down).wait_send()
-            )
+            if mode == "side":
+                self.local(unit, outer).wait()
+            if mode in ("both", "side"):
+                self.move(unit, other, 2, place.dp).wait_recv()
+                self.move(unit, own, 2, place.side).wait_send()
+            if mode == "side":
+                continue
+            for source in (own, other) if mode == "turned" else (own,):
+                pl.when((outer <= place.outer) & place.has_up)(
+                    lambda source=source: self.move(unit, source, 0, place.up).wait_send()
+                )
+                pl.when((outer >= place.outer) & place.has_down)(
+                    lambda source=source: self.move(unit, source, 1, place.down).wait_send()
+                )
+
+
+def gather_semaphores(units, size):
+    return [
+        pltpu.SemaphoreType.DMA((units, size, 3)),
+        pltpu.SemaphoreType.DMA((units, size)),
+        pltpu.SemaphoreType.DMA((units, size // 2)),
+    ]
 
 
 class Share:
@@ -226,22 +292,18 @@
 
 
 class Scatter:
-    def __init__(self, place, block, size, side, line, fold, sems):
-        self.place, self.block, self.size = place, block, size
+    def __init__(self, place, mine, theirs, side, line, fold, sems):
+        self.place, self.mine, self.theirs = place, mine, theirs
         self.side, self.line, self.fold = side, line, fold
         self.side_sent, self.side_landed, self.line_sent, self.line_landed = sems
 
-    def own(self, outer, inner):
-        return self.block(rows_at(2 * outer + inner, self.size))
-
     def to_side(self, outer):
-        place = self.place
         return remote(
-            self.own(outer, 1 - place.inner),
+            self.theirs(outer),
             self.side.at[outer],
             self.side_sent.at[outer],
             self.side_landed.at[outer],
-            dp=place.side,
+            dp=self.place.side,
         )
 
     def along(self, outer, slot, device):
@@ -260,13 +322,19 @@
             self.to_side(near).start()
 
     def total(self, outer, *slots):
-        self.to_side(outer).wait_recv()
-        rows = self.own(outer, self.place.inner)[...].astype(f32)
-        rows += self.side[outer].astype(f32)
+        rows = self.mine(outer)[...].astype(f32)
+        if self.side is not None:
+            self.to_side(outer).wait_recv()
+            rows += self.side[outer].astype(f32)
         for slot in slots:
             self.along(outer, slot, self.place.dp).wait_recv()
             rows += self.line[slot].astype(f32)
         return rows
+
+    def settle(self, store):
+        for outer in range(self.place.outers):
+            store(outer, self.total(outer).astype(bf16))
+            self.to_side(outer).wait_send()
 
     def hop(self, step):
         place, outers = self.place, self.place.outers
@@ -298,7 +366,8 @@
                     if other != outer:
                         self.along(other, other, place.dp).wait_send()
 
-            self.to_side(outer).wait_send()
+            if self.side is not None:
+                self.to_side(outer).wait_send()
 
 
 def scatter_turn(units, stores, turn):
@@ -309,6 +378,41 @@
     last = turn - outers + 1
     if 0 <= last < len(units):
         units[last].finish(stores[last])
+
+
+def blocks_of(place, ref, size):
+    return (
+        lambda outer: ref.at[rows_at(2 * outer + place.inner, size)],
+        lambda outer: ref.at[rows_at(2 * outer + 1 - place.inner, size)],
+    )
+
+
+def tile_of(kind, thin, wide):
+    return (wide, D) if kind else (thin, FF)
+
+
+def scatter_scratch(units, outers, tiles, side=True, line=True):
+    scratch = []
+    for unit in units:
+        tile = tiles[unit[1]] if isinstance(unit, tuple) else tiles
+        for asked, slots in ((side, outers), (line, outers + 1), (line, outers)):
+            if asked:
+                scratch.append(pltpu.VMEM((slots, *tile), bf16))
+        for asked, count in ((side, outers), (side, outers), (line, outers), (line, outers + 1)):
+            if asked:
+                scratch.append(pltpu.SemaphoreType.DMA((count,)))
+    return scratch
+
+
+def make_scatters(place, blocks, refs, side=True, line=True):
+    count = 3 * side + 4 * line
+    scatters = []
+    for index, (mine, theirs) in enumerate(blocks):
+        own = list(refs[index * count : (index + 1) * count])
+        buffers = [own.pop(0) if asked else None for asked in (side, line, line)]
+        sems = [own.pop(0) if asked else None for asked in (side, side, line, line)]
+        scatters.append(Scatter(place, mine, theirs, *buffers, sems))
+    return scatters
 
 
 class Spread:
@@ -552,12 +656,14 @@
 ):
     place = Place(outers)
     task = place.task
-    shards = [(w_qkv, w_qkv.shape[0], full_qkv), (w_proj, w_proj.shape[0], full_proj)]
-    for expert in range(full_in.shape[0]):
-        shards += [
-            (w_in.at[expert], w_in.shape[1], full_in.at[expert]),
-            (w_out.at[expert], w_out.shape[1], full_out.at[expert]),
-        ]
+    shards = [
+        (w_qkv, w_qkv.shape[0], full_qkv, "both"),
+        (w_proj, w_proj.shape[0], full_proj, "both"),
+    ]
+    for expert, kind in GATHER_WHOLE + GATHER_SPLIT:
+        own, full = ((w_in, full_in), (w_out, full_out))[kind]
+        mode = "line" if (expert, kind) in GATHER_SPLIT else "both"
+        shards.append((own.at[expert], own.shape[1], full.at[expert], mode))
     gather = Gather(place, shards, sent, landed, stay)
     shared, routed = range(2), range(2, len(shards))
     cot_all[task] = cotangent[...].astype(bf16)
@@ -626,8 +732,8 @@
 def forward_sending(top_count, image, cotangent, gain, bias, shards, router, choices):
     w_qkv, w_proj, w_in, w_out = shards
     experts, size = router.shape[0], lax.axis_size("dp")
-    groups, early = lax.axis_size("task"), w_in.shape[0] // 2
-    units, shares = 2 + 2 * early, 3 + SEQ // QUERY_FWD
+    groups, early = lax.axis_size("task"), 1 + GATHER_SPLIT[-1][0]
+    units, shares = 2 + len(GATHER_WHOLE + GATHER_SPLIT), 3 + SEQ // QUERY_FWD
     return pl.pallas_call(
         functools.partial(forward_sending_kernel, size // 2),
         out_shape=(
@@ -650,9 +756,7 @@
         scratch_shapes=[
             pltpu.VMEM((SEQ, D), bf16),
             pltpu.VMEM((SEQ, 8), f32),
-            pltpu.SemaphoreType.DMA((units, size, 3)),
-            pltpu.SemaphoreType.DMA((units, size)),
-            pltpu.SemaphoreType.DMA((units,)),
+            *gather_semaphores(units, size),
             pltpu.SemaphoreType.DMA((shares, 3)),
             pltpu.SemaphoreType.DMA((shares, 3)),
         ],
@@ -674,6 +778,7 @@
     grad_in, grad_out, grad_gates = grads
     groups = normed.shape[0]
     width = groups * CAP
+    between(0)
     for source in range(groups):
         own = slice(source * CAP, (source + 1) * CAP)
         hits = slot_hits(slots, source, first + expert)
@@ -688,7 +793,7 @@
         rows_cot[own, :] = cot_rows.astype(bf16)
         rows_grad[own, :] = (gate * cot_rows).astype(bf16)
         rows_gate[own, :] = jnp.broadcast_to(gate, (CAP, 128))
-    between(0)
+    between(1)
 
     def tile(index, _):
         units = rows_at(index // (width // ROW_TILE), FF_TILE)
@@ -702,7 +807,7 @@
         return 0
 
     lax.fori_loop(0, (FF // FF_TILE) * (width // ROW_TILE), tile, 0)
-    between(1)
+    between(2)
     for source in range(groups):
         own = slice(source * CAP, (source + 1) * CAP)
         kept = rows_at(expert, CAP)
@@ -714,10 +819,10 @@
         grad_gates[source, pl.ds(expert, 1), :] = jnp.sum(
             jnp.where(hits, grad_gate, 0.0), axis=0, keepdims=True
         )
-    between(2)
+    between(3)
     grad_in[expert] = dot_lt(rows_in[...], grad_pre[...]).astype(bf16)
     grad_out[expert] = dot_lt(rows_grad[...], hidden[...]).astype(bf16).T
-    between(3)
+    between(4)
 
 
 def combine(slots, first, local_count, sent, columns, source, store):
@@ -788,119 +893,128 @@
     )(*operands)
 
 
-def expert_sending_kernel(outers, early, *refs):
-    normed, cotangent, slots, gates, early_in, early_out, w_in, w_out = refs[:8]
-    late_in, late_out, gate_all, mixes, grad_rows, shard_in, shard_out = refs[8:15]
-    full_in, full_out = refs[15:17]
-    work, columns = refs[17:24], refs[24]
-    slot_in, slot_out, grad_in, grad_out, grad_gates, land = refs[25:31]
-    in_bufs, out_bufs = refs[31:34], refs[34:37]
-    sent, landed, gate_sent, gate_landed, mix_sem, late_sem, slot_sem = refs[37:44]
-    gather_sems, scatter_sems = refs[44:47], refs[47:51]
+def expert_sending_kernel(outers, *refs):
+    normed_all, cot_all, slots, gates, early_in, early_out, w_in, w_out = refs[:8]
+    late_in, late_out, gate_all, mixes, grad_rows, shard_in, shard_out, parts_in, parts_out = refs[8:17]
+    full_in, full_out = refs[17:19]
+    work, columns = refs[19:26], refs[26]
+    normed, cotangent, slot_in, slot_out, grad_in, grad_out, grad_gates, land = refs[27:35]
+    sent, landed, gate_sent, gate_landed, mix_sem, late_sem, slot_sem, token_sem = refs[35:43]
+    gather_sems, scatter_refs = refs[43:46], refs[46:]
     place = Place(outers)
-    local_count, size = grad_in.shape[0], 2 * outers
-    late = local_count - early
+    groups, local_count, size = normed.shape[0], grad_in.shape[0], 2 * outers
+    late = local_count - EARLY_EXPERTS
     first = place.task * local_count
-    place.greet(far=True)
-
-    shards = []
-    for expert in range(late):
-        shards += [
-            (w_in.at[early + expert], w_in.shape[1], full_in.at[expert]),
-            (w_out.at[early + expert], w_out.shape[1], full_out.at[expert]),
+    grads, shares = (grad_in, grad_out), (w_in.shape[1], w_out.shape[1])
+
+    def tokens():
+        return [
+            pltpu.make_async_copy(whole.at[source], ref.at[source], token_sem.at[kind, source])
+            for source in range(groups)
+            for kind, (whole, ref) in enumerate(((normed_all, normed), (cot_all, cotangent)))
         ]
-    gather = Gather(place, shards, *gather_sems)
-    for unit in range(len(shards)):
-        gather.start(unit)
-
-    def load(source, expert, slot):
+
+    def load(expert):
+        slot = expert % EARLY_EXPERTS
+        whole = (early_in, early_out) if expert < EARLY_EXPERTS else (full_in, full_out)
+        place_in = expert if expert < EARLY_EXPERTS else expert - EARLY_EXPERTS
         return [
-            pltpu.make_async_copy(source[0].at[expert], slot_in.at[slot], slot_sem.at[slot, 0]),
-            pltpu.make_async_copy(source[1].at[expert], slot_out.at[slot], slot_sem.at[slot, 1]),
+            pltpu.make_async_copy(
+                whole[kind].at[place_in], (slot_in, slot_out)[kind].at[slot], slot_sem.at[slot, kind]
+            )
+            for kind in range(2)
         ]
-
-    for expert in range(early):
-        for copy in load((early_in, early_out), expert, expert):
-            copy.start()
-
-    scatters, stores = [], []
-    for expert in range(early):
-        for source, bufs, shard in ((grad_in, in_bufs, shard_in), (grad_out, out_bufs, shard_out)):
-            unit = len(scatters)
-            scatters.append(
-                Scatter(
-                    place,
-                    lambda rows, source=source, expert=expert: source.at[expert, rows],
-                    shard.shape[1],
-                    *[buf.at[expert] for buf in bufs],
-                    [sem.at[unit] for sem in scatter_sems],
-                )
-            )
-
-            def store(rows, shard=shard, expert=expert):
-                shard[expert] = rows
-
-            stores.append(store)
 
     def keep(expert):
         return [
             pltpu.make_async_copy(
-                grad_in.at[early + expert], late_in.at[expert], late_sem.at[expert, 0]
-            ),
-            pltpu.make_async_copy(
-                grad_out.at[early + expert], late_out.at[expert], late_sem.at[expert, 1]
-            ),
+                grads[kind].at[EARLY_EXPERTS + expert],
+                (late_in, late_out)[kind].at[expert],
+                late_sem.at[expert, kind],
+            )
+            for kind in range(2)
         ]
 
-    def plan(expert, point):
-        steps = []
-        if point == 0:
-            if expert < early:
-                steps += [copy.wait for copy in load((early_in, early_out), expert, expert)]
-            else:
-                steps += [
-                    copy.wait
-                    for copy in load((full_in, full_out), expert - early, expert - early)
-                ]
-        if expert == 0:
-            for unit in range(len(shards)):
-                hop = point - unit // 2 + 1
-                if 0 < hop < outers:
-                    steps.append(lambda unit=unit, hop=hop: gather.step(unit, hop))
-        if expert == 1 and point == 0:
-            for unit in range(len(shards)):
-                for hop in range(5 - unit // 2, outers):
-                    steps.append(lambda unit=unit, hop=hop: gather.step(unit, hop))
-        if point == 3:
-            if expert < early:
-                steps += [scatters[2 * expert].start, scatters[2 * expert + 1].start]
-            else:
-                steps += [copy.start for copy in keep(expert - early)]
-        if expert == local_count - 1 and point in (0, 2):
-            steps.append(lambda: scatter_turn(scatters, stores, point // 2))
-        return steps
+    for copy in tokens() + load(0):
+        copy.start()
+    place.greet(far=True)
+    shards = []
+    for expert, kind in GATHER_LATE + GATHER_SPLIT:
+        full = (full_in, full_out)[kind].at[expert - EARLY_EXPERTS]
+        if (expert, kind) in GATHER_SPLIT:
+            shards.append(((early_in, early_out)[kind].at[expert], shares[kind], full, "side"))
+        else:
+            shards.append(((w_in, w_out)[kind].at[expert], shares[kind], full, "turned"))
+    gather = Gather(place, shards, *gather_sems)
+    turned = range(len(GATHER_LATE))
+    for unit in range(len(shards)):
+        gather.start(unit)
+    for copy in load(1):
+        copy.start()
+    per_full, per_side = 7 * len(SCATTER_EARLY), 3 * len(SCATTER_SPLIT)
+
+    def scatters(units, refs, **parts):
+        return make_scatters(
+            place,
+            [blocks_of(place, grads[kind].at[expert], shares[kind]) for expert, kind in units],
+            refs,
+            **parts,
+        )
+
+    whole = scatters(SCATTER_EARLY, scatter_refs[:per_full])
+    split = scatters(SCATTER_SPLIT, scatter_refs[per_full : per_full + per_side], line=False)
+    stores, keeps = [], []
+    for expert, kind in SCATTER_EARLY:
+
+        def store(rows, shard=(shard_in, shard_out)[kind], expert=expert):
+            shard[expert] = rows
+
+        stores.append(store)
+    for index, (_, kind) in enumerate(SCATTER_SPLIT):
+        at = [other[1] for other in SCATTER_SPLIT[:index]].count(kind)
+
+        def settle(outer, rows, parts=(parts_in, parts_out)[kind], at=at):
+            parts[at, outer] = rows
+
+        keeps.append(settle)
+    steps = {}
+
+    def plan(expert, point, *acts):
+        steps.setdefault((expert, point), []).extend(acts)
+
+    plan(0, 0, *[copy.wait for copy in tokens()])
+    for expert in range(EARLY_EXPERTS):
+        plan(expert, 1, *[copy.wait for copy in load(expert)])
+    for hop in range(outers):
+        at = GATHER_POINTS[hop] if hop < outers - 1 else (3, 0)
+        plan(*at, *[lambda unit=unit, hop=hop: gather.step(unit, hop) for unit in turned])
+    for expert in range(EARLY_EXPERTS, local_count):
+        units = [
+            unit
+            for unit, (owner, _) in enumerate(GATHER_LATE + GATHER_SPLIT)
+            if owner == expert
+        ]
+        plan(expert, 0, *[lambda unit=unit: gather.finish(unit) for unit in units])
+        plan(expert, 0, *[copy.start for copy in load(expert)])
+        plan(expert, 1, *[copy.wait for copy in load(expert)])
+        plan(expert, 4, *[copy.start for copy in keep(expert - EARLY_EXPERTS)])
+    for index, (expert, _) in enumerate(SCATTER_EARLY):
+        plan(expert, 4, whole[index].start)
+    for index, (expert, _) in enumerate(SCATTER_SPLIT):
+        plan(expert, 4, split[index].start)
+    for turn, at in enumerate(SCATTER_POINTS):
+        plan(*at, lambda turn=turn: scatter_turn(whole, stores, turn))
 
     def body(expert, _):
-        @pl.when(expert >= early)
-        def _():
-            for other in range(late):
-
-                @pl.when(expert == early + other)
-                def _():
-                    gather.finish(2 * other)
-                    gather.finish(2 * other + 1)
-                    for copy in load((full_in, full_out), other, other):
-                        copy.start()
-
         def between(point):
             for at in range(local_count):
-                steps = plan(at, point)
-                if steps:
+                acts = steps.get((at, point))
+                if acts:
 
                     @pl.when(expert == at)
                     def _():
-                        for step in steps:
-                            step()
+                        for act in acts:
+                            act()
 
         one_expert(
             (normed, cotangent, slots, gates, slot_in, slot_out),
@@ -908,7 +1022,7 @@
             (grad_in, grad_out, grad_gates),
             expert,
             first,
-            lax.rem(expert, early),
+            lax.rem(expert, EARLY_EXPERTS),
             between,
         )
         return 0
@@ -936,6 +1050,7 @@
     back = Return(
         place, lambda source: part(hidden, source), RETURNS, land, joint, sent, landed
     )
+    turns = list(range(len(SCATTER_POINTS), len(whole) + outers - 1))
     for order, (source, after) in enumerate(
         (
             (place.far, back.by_core),
@@ -952,82 +1067,76 @@
                 after(piece)
 
         combine(slots, first, local_count, work[6], columns, source, store)
-        if order:
-            scatter_turn(scatters, stores, 1 + order)
-    keeps = [
-        pltpu.make_async_copy(part(grad_pre, source), mixes.at[source], mix_sem.at[source])
-        for source in range(mixes.shape[0])
-    ]
-    for copy in keeps:
-        copy.start()
-    for turn in range(5, len(scatters) + outers):
-        scatter_turn(scatters, stores, turn)
+        pltpu.make_async_copy(part(grad_pre, source), mixes.at[source], mix_sem.at[order]).start()
+        if order in COMBINE_TURNS and turns:
+            scatter_turn(whole, stores, turns.pop(0))
+    for turn in turns:
+        scatter_turn(whole, stores, turn)
+    for index, one in enumerate(split):
+        one.settle(keeps[index])
     for piece in range(RETURNS):
         grad_rows[back.rows(piece), :] = back.finish(piece)
     for way in range(3):
         gate_move(way).wait()
-    for copy in keeps:
-        copy.wait()
+    for order in range(groups):
+        pltpu.make_async_copy(
+            part(grad_pre, place.task), mixes.at[place.task], mix_sem.at[order]
+        ).wait()
     for expert in range(late):
         for copy in keep(expert):
             copy.wait()
 
 
-def scatter_buffers(number, outers, *dims):
-    return [pltpu.VMEM((number, slots, *dims), bf16) for slots in (outers, outers + 1, outers)]
-
-
-def scatter_semaphores(units, outers):
-    return [pltpu.SemaphoreType.DMA((units, outers))] * 3 + [
-        pltpu.SemaphoreType.DMA((units, outers + 1))
-    ]
+def kinds(units, kind):
+    return [unit for unit in units if unit[1] == kind]
 
 
 def expert_sending(*operands):
     groups, experts = operands[2].shape[:2]
     local_count, thin = operands[6].shape[:2]
-    wide, early = operands[7].shape[1], operands[4].shape[0]
-    late, size = local_count - early, lax.axis_size("dp")
-    outers = size // 2
+    wide, size = operands[7].shape[1], lax.axis_size("dp")
+    late, outers = local_count - EARLY_EXPERTS, size // 2
+    tiles = ((thin, FF), (wide, D))
     return pl.pallas_call(
-        functools.partial(expert_sending_kernel, outers, early),
+        functools.partial(expert_sending_kernel, outers),
         out_shape=(
             shape(late, D, FF, dtype=bf16),
             shape(late, FF, D, dtype=bf16),
             shape(groups, local_count, SEQ),
             shape(groups, SEQ, D, dtype=bf16),
             shape(SEQ, D),
-            shape(early, thin, FF),
-            shape(early, wide, D),
+            *[shape(len(kinds(SCATTER_EARLY, kind)), *tiles[kind]) for kind in range(2)],
+            *[
+                shape(len(kinds(SCATTER_SPLIT, kind)), outers, *tiles[kind], dtype=bf16)
+                for kind in range(2)
+            ],
             shape(late, D, FF, dtype=bf16),
             shape(late, FF, D, dtype=bf16),
         ),
-        in_specs=[VMEM] * 4 + [ANY] * 4,
-        out_specs=[ANY] * 2 + [VMEM, ANY, VMEM, VMEM, VMEM] + [ANY] * 2,
+        in_specs=[ANY] * 2 + [VMEM] * 2 + [ANY] * 4,
+        out_specs=[ANY] * 2 + [VMEM, ANY] + [VMEM] * 5 + [ANY] * 2,
         scratch_shapes=expert_scratch(groups, local_count, experts)
         + [
-            pltpu.VMEM((early, D, FF), bf16),
-            pltpu.VMEM((early, FF, D), bf16),
+            pltpu.VMEM((groups, SEQ, D), bf16),
+            pltpu.VMEM((groups, SEQ, D), bf16),
+            pltpu.VMEM((EARLY_EXPERTS, D, FF), bf16),
+            pltpu.VMEM((EARLY_EXPERTS, FF, D), bf16),
             pltpu.VMEM((local_count, D, FF), bf16),
             pltpu.VMEM((local_count, FF, D), bf16),
             pltpu.VMEM((groups, local_count, SEQ), f32),
             pltpu.VMEM((3, SEQ, D), bf16),
-        ]
-        + scatter_buffers(early, outers, thin, FF)
-        + scatter_buffers(early, outers, wide, D)
-        + [
             pltpu.SemaphoreType.DMA((3, RETURNS)),
             pltpu.SemaphoreType.DMA((3, RETURNS)),
             pltpu.SemaphoreType.DMA((3,)),
             pltpu.SemaphoreType.DMA((3,)),
             pltpu.SemaphoreType.DMA((groups,)),
             pltpu.SemaphoreType.DMA((late, 2)),
-            pltpu.SemaphoreType.DMA((early, 2)),
-            pltpu.SemaphoreType.DMA((2 * late, size, 3)),
-            pltpu.SemaphoreType.DMA((2 * late, size)),
-            pltpu.SemaphoreType.DMA((2 * late,)),
+            pltpu.SemaphoreType.DMA((EARLY_EXPERTS, 2)),
+            pltpu.SemaphoreType.DMA((2, groups)),
         ]
-        + scatter_semaphores(2 * early, outers),
+        + gather_semaphores(len(GATHER_LATE + GATHER_SPLIT), size)
+        + scatter_scratch(SCATTER_EARLY, outers, tiles)
+        + scatter_scratch(SCATTER_SPLIT, outers, tiles, line=False),
         compiler_params=params(collective_id=1, has_side_effects=True),
     )(*operands)
 
@@ -1201,63 +1310,80 @@
     )(*operands)
 
 
-def backward_sending_kernel(outers, *refs):
+def backward_sending_kernel(outers, groups, *refs):
     image, cotangent, gain, bias, mid, w_qkv, w_proj, router = refs[:8]
-    packed, mixed, logs, mixes, grad_rows, grad_gates, probs, grad_in, grad_out = refs[8:17]
-    activations, grad_image, grad_norm, grad_router, shard_qkv, shard_proj = refs[17:23]
-    shard_in, shard_out = refs[23:25]
-    grad_mid, grad_low, grad_mixed, grad_packed, grad_keys, grad_values, normed_first = refs[25:32]
-    norm_sums, router_sums, shared = refs[32:35]
-    land, joint, back_sent, back_landed = refs[35:39]
-    in_bufs, out_bufs, shared_bufs = refs[39:42], refs[42:45], refs[45:48]
-    scatter_sems = refs[48:52]
+    packed, mixed, logs, mixes_all, grad_rows, grad_gates, probs, late_in, late_out = refs[8:17]
+    parts_in, parts_out = refs[17:19]
+    activations, grad_image, grad_norm, grad_router, shard_qkv, shard_proj = refs[19:25]
+    shard_in, shard_out = refs[25:27]
+    grad_mid, grad_low, grad_mixed, grad_packed, grad_keys, grad_values, normed_first = refs[27:34]
+    norm_sums, router_sums, shared, mixes, land, joint, back_sent, back_landed = refs[34:42]
+    mix_sem, grad_sem, grad_refs = refs[42], refs[43], refs[44 : 44 + len(SCATTER_LATE)]
+    refs = refs[44 + len(SCATTER_LATE) :]
     place = Place(outers)
-    count, groups, size = grad_in.shape[0], mixes.shape[0], 2 * outers
+    size, pieces = 2 * outers, HEADS // 2 + 1
+    shards = (shard_in, shard_out)
+    loads = [
+        pltpu.make_async_copy(
+            (late_in, late_out)[kind].at[expert - EARLY_EXPERTS],
+            grad_refs[index],
+            grad_sem.at[index],
+        )
+        for index, (expert, kind) in enumerate(SCATTER_LATE)
+    ]
+    mix_load = pltpu.make_async_copy(mixes_all, mixes, mix_sem)
+    for copy in (*loads, mix_load):
+        copy.start()
     place.greet_all(groups)
-    norms = Spread("dp", place, size, *refs[52:55])
-    norms_task = Spread("task", place, groups, *refs[55:58])
-    routers = Spread("dp", place, size, *refs[58:61])
-    task_refs = refs[61:64]
-
-    def scatter(unit, block, size, bufs, at):
-        return Scatter(
-            place,
-            block,
-            size,
-            *[buf.at[at] for buf in bufs],
-            [sem.at[unit] for sem in scatter_sems],
-        )
-
-    big, stores = [], []
-    for expert in range(count):
-        for source, bufs, shard in ((grad_in, in_bufs, shard_in), (grad_out, out_bufs, shard_out)):
-            big.append(
-                scatter(
-                    len(big),
-                    lambda rows, source=source, expert=expert: source.at[expert, rows],
-                    shard.shape[1],
-                    bufs,
-                    expert,
-                )
+    at = 7 * len(SCATTER_LATE)
+    late = make_scatters(
+        place,
+        [
+            blocks_of(place, grad_refs[index], shards[kind].shape[1])
+            for index, (_, kind) in enumerate(SCATTER_LATE)
+        ],
+        refs[:at],
+    )
+    split_blocks = []
+    for index, (_, kind) in enumerate(SCATTER_SPLIT):
+        number = [other[1] for other in SCATTER_SPLIT[:index]].count(kind)
+        split_blocks.append(
+            (
+                lambda outer, parts=(parts_in, parts_out)[kind], number=number: parts.at[
+                    number, outer
+                ],
+                None,
             )
-
-            def store(rows, shard=shard, expert=expert):
-                shard[expert] = rows
-
-            stores.append(store)
-    pieces = HEADS // 2 + 1
-    small = [
-        scatter(
-            len(big) + piece,
-            lambda rows, piece=piece: shared.at[piece, rows],
-            shard_proj.shape[0],
-            shared_bufs,
-            piece,
-        )
+        )
+    split = make_scatters(place, split_blocks, refs[at:], side=False)
+    at += 4 * len(SCATTER_SPLIT)
+    small = make_scatters(
+        place,
+        [blocks_of(place, shared.at[piece], shard_proj.shape[0]) for piece in range(pieces)],
+        refs[at:],
+    )
+    at += 7 * pieces
+    norms = Spread("dp", place, size, *refs[at : at + 3])
+    norms_task = Spread("task", place, groups, *refs[at + 3 : at + 6])
+    routers = Spread("dp", place, size, *refs[at + 6 : at + 9])
+    totals = [
+        Spread("task", place, groups, *[ref.at[piece] for ref in refs[at + 9 : at + 12]])
         for piece in range(pieces)
     ]
-    for unit in big:
-        unit.start()
+    stores = []
+    for unit in SCATTER_SPLIT + SCATTER_LATE:
+        number = sorted(kinds(SCATTER_SPLIT + SCATTER_LATE, unit[1])).index(unit)
+
+        def store(rows, shard=shards[unit[1]], number=number):
+            shard[number] = rows
+
+        stores.append(store)
+    for one in split:
+        one.hop(0)
+    for copy, one in zip(loads, late):
+        copy.wait()
+        one.start()
+    mix_load.wait()
     back = Return(
         place, lambda source: mixes.at[source], 1, land, joint, back_sent, back_landed
     )
@@ -1282,16 +1408,23 @@
     small[pieces - 1].start()
     routers.give(router_sums[...])
     blocks = SEQ // QUERY_BWD
-    totals = [
-        Spread("task", place, groups, *[ref.at[piece] for ref in task_refs])
-        for piece in range(pieces)
-    ]
-    units, keeps = big + small, stores + [one.give for one in totals]
+    units, keeps = split + late, stores
+    names = dict(zip("stuvwxyz", range(len(units))))
+    names.update({str(piece): len(units) + piece for piece in range(pieces)})
+    units, keeps = units + small, keeps + [one.give for one in totals]
+
+    def run(acts):
+        for act in acts:
+            unit, hop = names[act[0]], int(act[1])
+            if hop < outers - 1:
+                units[unit].hop(hop)
+            else:
+                units[unit].finish(keeps[unit])
 
     def between(pair, index):
-        for turn, at in enumerate(TURNS):
+        for at, acts in BACKWARD_POINTS.items():
             if at // blocks == pair:
-                pl.when(index == at % blocks)(lambda turn=turn: scatter_turn(units, keeps, turn))
+                pl.when(index == at % blocks)(lambda acts=acts: run(acts))
 
     def done(pair, columns):
         both = jnp.concatenate([grad_packed[:, part] for part in columns], axis=1)
@@ -1304,28 +1437,28 @@
     first_back(image, gain, w_qkv, grad_packed, grad_mid, grad_image, norm_sums)
     norms.give(norm_sums[...])
     activations[...] = mid[...] + back.finish(0)
+    run(BACKWARD_THEN[0])
     grad_router[...] = routers.take()
-    for turn in range(len(TURNS), len(units) + outers - 1):
-        scatter_turn(units, keeps, turn)
-        if turn == len(units) - 1:
-            norms_task.give(norms.take())
+    norms_task.give(norms.take())
+    run(BACKWARD_THEN[1])
     grad_norm[...] = norms_task.take()
-    for piece in range(pieces):
+    for piece in (pieces - 1, *range(pieces - 1)):
         rows = totals[piece].take()
         if piece == pieces - 1:
             shard_proj[...] = rows
         else:
             for part in range(3):
-                at = part * D + piece * PAIR
-                shard_qkv[:, at : at + PAIR] = rows[:, part * PAIR : (part + 1) * PAIR]
+                column = part * D + piece * PAIR
+                shard_qkv[:, column : column + PAIR] = rows[:, part * PAIR : (part + 1) * PAIR]
 
 
 def backward_sending(*operands):
-    router, grad_in = operands[7], operands[15]
+    router = operands[7]
     experts, size = router.shape[0], lax.axis_size("dp")
-    outers, count = size // 2, grad_in.shape[0]
-    thin, wide, pieces = D // size, FF // size, HEADS // 2 + 1
-    units, groups = 2 * count + pieces, lax.axis_size("task")
+    outers, thin, wide, pieces = size // 2, D // size, FF // size, HEADS // 2 + 1
+    groups = lax.axis_size("task")
+    tiles, wholes = ((thin, FF), (wide, D)), ((D, FF), (FF, D))
+    ends = SCATTER_SPLIT + SCATTER_LATE
 
     def spread(peers, *dims, lead=(), dtype=f32):
         return [pltpu.VMEM((*lead, peers, *dims), dtype)] + [
@@ -1333,7 +1466,7 @@
         ] * 2
 
     return pl.pallas_call(
-        functools.partial(backward_sending_kernel, outers),
+        functools.partial(backward_sending_kernel, outers, groups),
         out_shape=(
             shape(SEQ, D),
             shape(SEQ, D),
@@ -1341,25 +1474,27 @@
             shape(experts, D),
             shape(thin, 3 * D),
             shape(thin, D),
-            shape(count, thin, FF),
-            shape(count, wide, D),
+            *[shape(len(kinds(ends, kind)), *tiles[kind]) for kind in range(2)],
         ),
-        in_specs=[VMEM] * 17,
+        in_specs=[VMEM] * 11 + [ANY] + [VMEM] * 3 + [ANY] * 2 + [VMEM] * 2,
         out_specs=[VMEM] * 8,
         scratch_shapes=backward_scratch()
         + [
             pltpu.VMEM((8, D), f32),
             pltpu.VMEM((experts, D), f32),
             pltpu.VMEM((pieces, D, D), bf16),
+            pltpu.VMEM((groups, SEQ, D), bf16),
             pltpu.VMEM((3, SEQ, D), bf16),
             pltpu.VMEM((SEQ, D), bf16),
             pltpu.SemaphoreType.DMA((3, 1)),
             pltpu.SemaphoreType.DMA((3, 1)),
+            pltpu.SemaphoreType.DMA,
+            pltpu.SemaphoreType.DMA((len(SCATTER_LATE),)),
         ]
-        + scatter_buffers(count, outers, thin, FF)
-        + scatter_buffers(count, outers, wide, D)
-        + scatter_buffers(pieces, outers, thin, D)
-        + scatter_semaphores(units, outers)
+        + [pltpu.VMEM(wholes[kind], bf16) for _, kind in SCATTER_LATE]
+        + scatter_scratch(SCATTER_LATE, outers, tiles)
+        + scatter_scratch(SCATTER_SPLIT, outers, tiles, side=False)
+        + scatter_scratch(range(pieces), outers, (thin, D))
         + spread(size, 8, D)
         + spread(groups, 8, D)
         + spread(size, experts, D)
@@ -1392,7 +1527,7 @@
     def swap(array):
         return lax.all_to_all(array, "task", split_axis=0, concat_axis=0, tiled=True)
 
-    sending = groups == 4 and lax.axis_size("dp") in (4, 8) and w_in.shape[1] % 16 == 0
+    sending = groups == 4 and lax.axis_size("dp") == 8 and local_count == 4
     if sending:
         (
             mid,
@@ -1426,6 +1561,8 @@
             grad_normed,
             early_in,
             early_out,
+            parts_in,
+            parts_out,
             _,
             _,
         ) = expert_sending(normed, cot_rows, slots, gates, full_in, full_out, w_in, w_out)
@@ -1456,6 +1593,8 @@
             probs,
             late_in,
             late_out,
+            parts_in,
+            parts_out,
         )
         grad_in = jnp.concatenate([early_in, grad_in], axis=0)
         grad_out = jnp.concatenate([early_out, grad_out], axis=0)

time: 330 us -> 316 us (0.958)
  Pallas kernels: 312 us -> 297 us
    pallas_call x2, Pallas kernels: 232 us -> 204 us  [the longest x1 122 us: expert_sending(): pl.pallas_call(functools.partial(expert_sending_kernel, outers), out_shap...]
    pallas_call x1, Pallas kernels: 79.4 us -> 93.7 us  [forward_sending(): pl.pallas_call(functools.partial(forward_sending_kernel, size // 2), out_...]
where the time goes in v6:
time: 316 us; the launch traced here: 311 us
  Pallas kernels  297 us (94%)
  local copies, waits for them, and re-layouts  8.95 us (3%)
  other arithmetic  3.24 us (1%)
    pallas_call x1, Pallas kernels, expert_sending(): pl.pallas_call(functools.partial(expert_sending_kernel, outers), out_shap...  122 us
    pallas_call x1, Pallas kernels, forward_sending(): pl.pallas_call(functools.partial(forward_sending_kernel, size // 2), out_...  93.7 us
    pallas_call x1, Pallas kernels, backward_sending(): pl.pallas_call(functools.partial(backward_sending_kernel, outers, groups)...  82 us
    unnamed x22, local copies, waits for them, and re-layouts  7.55 us

profile of v6, /device:TPU:0, one launch (start us, length us, event | category | flops | bytes accessed | tf_op | source)
XLA Modules:
  0.0 311.4 jit_solution(8711832072236345741)
XLA Ops:
  1.3 1.7 copy.20
  3.0 93.7 %shard_map.178 = (f32[1024,384]{1,0:T(8,128)}, bf16[1024,1152]{1,0:T(8,128)(2,1)}, bf16[1024,384]{1,0:T(8,128)(2,1)}, f32[8,1024]{1,0:T(8,128)}, f32[16,1024]{1,...) custom-call(s32[1]{0:T(128)S(6)} %copy.26.top_count, ...), custom_call_target="tpu_custom_call" | custom-call | tf_op jit(solution)/shard_map/pallas_call | solution.py:737
  96.7 121.7 %shard_map.179 = (bf16[2,384,1536]{2,1,0:T(8,128)(2,1)}, bf16[2,1536,384]{2,1,0:T(8,128)(2,1)}, f32[4,4,1024]{2,1,0:T(4,128)}, bf16[4,1024,384]{2,1,0:T(8,128)(2...) custom-call(bf16[4,1024,384]{2,1,0:T(8,128)(2,1)} %get-tuple-element, ...), custom_call_target="tpu_custom_call" | custom-call | tf_op jit(solution)/shard_map/pallas_call | solution.py:1100
  218.5 0.0 copy-start.3
  218.5 82.0 %shard_map.180 = (f32[1024,384]{1,0:T(8,128)}, f32[1024,384]{1,0:T(8,128)}, f32[8,384]{1,0:T(8,128)}, f32[16,384]{1,0:T(8,128)}, f32[48,1152]{1,0:T(8,128)}, /*i...) custom-call(f32[1024,384]{1,0:T(8,128)} %bitcast.12, f32[1024,384]{1,0:T(8,128)} %bitcast.14, ...), custom_call_target="tpu_custom_call" | custom-call | tf_op jit(solution)/shard_map/pallas_call | solution.py:1468
  300.5 0.0 copy-start.2
  300.5 0.0 copy-start.4
  300.5 1.4 fusion
  301.9 0.0 copy-done.3
  301.9 2.2 pad_maximum_fusion
  304.1 0.0 copy-done.2
  304.1 0.0 copy-done.4
  304.1 0.0 copy-start.1
  304.1 1.1 pad_maximum_fusion.1
  305.2 0.7 copy-done.1
  305.9 0.0 copy-start
  305.9 1.1 copy.27
  307.0 0.8 copy-done
  307.9 0.0 copy-start.5
  307.9 0.0 copy-start.6
  307.9 0.0 copy-start.7
  307.9 1.1 copy.28
  309.0 0.0 copy-done.5
  309.0 0.7 copy.29
  309.7 0.0 copy-done.6
  309.7 0.6 copy.30
  310.4 0.0 copy-done.7
  310.4 0.6 copy.31
Async XLA Ops:
  218.5 83.4 %copy-start.3 = (f32[2,48,1536]{2,1,0:T(8,128)S(1)}, f32[2,48,1536]{2,1,0:T(8,128)}, u32[]{:S(2)}) copy-start(f32[2,48,1536]{2,1,0:T(8,128)} %get-tuple-element.65) | copy-start | bytes 1769476
  300.5 3.6 %copy-start.2 = (f32[3,192,384]{2,1,0:T(8,128)S(1)}, f32[3,192,384]{2,1,0:T(8,128)}, u32[]{:S(2)}) copy-start(f32[3,192,384]{2,1,0:T(8,128)} %get-tuple-element.68) | copy-start | bytes 2654212
  300.5 3.6 %copy-start.4 = (f32[1,192,384]{2,1,0:T(8,128)S(1)}, f32[1,192,384]{2,1,0:T(8,128)}, u32[]{:S(2)}) copy-start(f32[1,192,384]{2,1,0:T(8,128)} %get-tuple-element.67) | copy-start | bytes 884740
  304.1 1.8 copy-start.1
  305.9 2.0 copy-start
  307.9 1.2 copy-start.5
  307.9 1.8 copy-start.6
  307.9 2.5 copy-start.7

commit v7 on v6

--- a/solution.py
+++ b/solution.py
@@ -38,9 +38,19 @@
 SCATTER_LATE = ((2, 1), (3, 0), (3, 1))
 EARLY_EXPERTS = 2
 
-GATHER_POINTS = ((0, 2), (1, 1), (1, 4))
+GATHER_POINTS = {2: ((0, 1), (0, 3), (1, 0), (1, 4)), 3: ((0, 2), (1, 1), (1, 4), (3, 0))}
 SCATTER_POINTS = ((3, 1), (3, 3))
 COMBINE_TURNS = (1, 2, 3)
+
+AHEAD = 2
+FORWARD_FIRST = ((0, 1), (1, 1))
+FORWARD_POINTS = {
+    0: ((2, 1), (3, 1)),
+    3: ((4, 1), (5, 1)),
+    8: ((0, 2), (1, 2)),
+    11: ((2, 2), (3, 2)),
+}
+FORWARD_THEN = (((4, 2), (5, 2)), ((0, 3), (1, 3), (2, 3), (3, 3), (4, 3), (5, 3)))
 
 BACKWARD_POINTS = {
     3: ("s1", "u0",),
@@ -173,11 +183,10 @@
             dp=device,
         )
 
-    def local(self, unit, outer):
-        own, size, full, mode = self.shards[unit]
-        rows = rows_at(2 * outer + self.place.inner, size)
-        source = own.at[rows] if mode == "side" else own
-        return pltpu.make_async_copy(source, full.at[rows], self.stay.at[unit, outer])
+    def local(self, unit):
+        own, size, full, _ = self.shards[unit]
+        target = full.at[rows_at(self.place.dp, size)]
+        return pltpu.make_async_copy(own, target, self.stay.at[unit])
 
     def along(self, unit, source, up, down):
         place = self.place
@@ -197,7 +206,6 @@
         if mode == "side":
             for outer in range(place.outers):
                 self.to_side(unit, outer).start()
-                self.local(unit, outer).start()
             return
         if mode == "turned":
             self.move(unit, place.dp, 2, place.side, own).start()
@@ -205,7 +213,8 @@
         pl.when(place.has_down)(lambda: self.move(unit, place.dp, 1, place.down, own).start())
         if mode == "both":
             self.move(unit, place.dp, 2, place.side, own).start()
-        self.local(unit, place.outer).start()
+        if self.stay is not None:
+            self.local(unit).start()
 
     def step(self, unit, hop):
         place, mode = self.place, self.shards[unit][3]
@@ -231,14 +240,12 @@
 
     def finish(self, unit):
         place, mode = self.place, self.shards[unit][3]
-        if mode != "side":
-            self.local(unit, place.outer).wait()
+        if self.stay is not None:
+            self.local(unit).wait()
         if mode == "turned":
             self.move(unit, place.dp, 2, place.side).wait_send()
         for outer in range(place.outers):
             own, other = 2 * outer + place.inner, 2 * outer + 1 - place.inner
-            if mode == "side":
-                self.local(unit, outer).wait()
             if mode in ("both", "side"):
                 self.move(unit, other, 2, place.dp).wait_recv()
                 self.move(unit, own, 2, place.side).wait_send()
@@ -257,7 +264,6 @@
     return [
         pltpu.SemaphoreType.DMA((units, size, 3)),
         pltpu.SemaphoreType.DMA((units, size)),
-        pltpu.SemaphoreType.DMA((units, size // 2)),
     ]
 
 
@@ -491,7 +497,7 @@
         return total + self.land[0, rows, :].astype(f32) + self.land[2, rows, :].astype(f32)
 
 
-def attend(packed, mixed, totals, index):
+def attend(packed, mixed, totals, index, between):
     zero = jnp.array(0, bf16)
     rows = rows_at(index, QUERY_FWD)
 
@@ -515,6 +521,7 @@
             logs[0],
             jnp.where(lanes == 2 * pair + 1, logs[1], totals[rows, :]),
         )
+        between(index * (HEADS // 2) + pair)
         return 0
 
     lax.fori_loop(0, HEADS // 2, head_pair, 0)
@@ -588,7 +595,7 @@
     totals[...] = jnp.zeros_like(totals)
 
     def block(index, _):
-        attend(packed, mixed, totals, index)
+        attend(packed, mixed, totals, index, lambda point: None)
         normed[rows_at(index, QUERY_FWD), :] = mid_block(
             index, image, gain, bias, w_proj, router, mixed, mid, probs
         )
@@ -677,12 +684,14 @@
     cot = share(0, lambda source: cot_all.at[source])
     slot = share(1, lambda source: slots_all.at[source])
     gate = share(2, lambda source: gates_all.at[source])
+    for unit in routed[:AHEAD]:
+        gather.start(unit)
     cot.start()
     first_norm(image, gain, bias, normed_first)
     for hop in range(1, outers):
         for unit in shared:
             gather.step(unit, hop)
-    for unit in routed:
+    for unit in routed[AHEAD:]:
         gather.start(unit)
     slots_all[task] = number_slots(choices, top_count, router.shape[0])
     slot.start()
@@ -696,33 +705,35 @@
     def chunk(index):
         return share(3 + index, lambda source: normed_all.at[source, rows_at(index, QUERY_FWD)])
 
+    def run(acts):
+        for unit, hop in acts:
+            if unit < len(routed):
+                gather.step(routed[unit], hop)
+
     blocks = SEQ // QUERY_FWD
+    run(FORWARD_FIRST)
 
     def block(index, _):
-        attend(packed, mixed, totals, index)
+        def between(point):
+            for at, acts in FORWARD_POINTS.items():
+                pl.when(point == at)(lambda acts=acts: run(acts))
+
+        attend(packed, mixed, totals, index, between)
         normed_all[task, rows_at(index, QUERY_FWD), :] = mid_block(
             index, image, gain, bias, full_proj, router, mixed, mid, probs
         )
         chunk(index).start()
         pl.when(index > 0)(lambda: chunk(index - 1).relay())
-        for hop in range(1, outers):
-
-            @pl.when(index == hop - 1)
-            def _():
-                for unit in routed:
-                    gather.step(unit, hop)
-
         return 0
 
     lax.fori_loop(0, blocks, block, 0)
-    for hop in range(blocks + 1, outers):
-        for unit in routed:
-            gather.step(unit, hop)
     gates_all[task] = jnp.where(slots_all[task] >= 0, probs[...], 0.0)
     gate.start()
     logs[...] = totals[...].T
+    run(FORWARD_THEN[0])
     chunk(blocks - 1).relay()
     gate.relay()
+    run(FORWARD_THEN[1])
     for one in [cot, slot, gate] + [chunk(index) for index in range(blocks)]:
         one.finish()
     for unit in routed:
@@ -751,12 +762,13 @@
             shape(early, D, FF, dtype=bf16),
             shape(early, FF, D, dtype=bf16),
         ),
-        in_specs=[SMEM] + [VMEM] * 6 + [ANY] * 2 + [VMEM] * 2,
+        in_specs=[SMEM] + [VMEM] * 10,
         out_specs=[VMEM] * 11 + [ANY] * 2,
         scratch_shapes=[
             pltpu.VMEM((SEQ, D), bf16),
             pltpu.VMEM((SEQ, 8), f32),
             *gather_semaphores(units, size),
+            pltpu.SemaphoreType.DMA((units,)),
             pltpu.SemaphoreType.DMA((shares, 3)),
             pltpu.SemaphoreType.DMA((shares, 3)),
         ],
@@ -900,7 +912,7 @@
     work, columns = refs[19:26], refs[26]
     normed, cotangent, slot_in, slot_out, grad_in, grad_out, grad_gates, land = refs[27:35]
     sent, landed, gate_sent, gate_landed, mix_sem, late_sem, slot_sem, token_sem = refs[35:43]
-    gather_sems, scatter_refs = refs[43:46], refs[46:]
+    gather_sems, scatter_refs = refs[43:45], refs[45:]
     place = Place(outers)
     groups, local_count, size = normed.shape[0], grad_in.shape[0], 2 * outers
     late = local_count - EARLY_EXPERTS
@@ -915,15 +927,25 @@
         ]
 
     def load(expert):
-        slot = expert % EARLY_EXPERTS
-        whole = (early_in, early_out) if expert < EARLY_EXPERTS else (full_in, full_out)
-        place_in = expert if expert < EARLY_EXPERTS else expert - EARLY_EXPERTS
-        return [
-            pltpu.make_async_copy(
-                whole[kind].at[place_in], (slot_in, slot_out)[kind].at[slot], slot_sem.at[slot, kind]
-            )
-            for kind in range(2)
-        ]
+        slot, copies = expert % EARLY_EXPERTS, []
+        for kind in range(2):
+            target, sem = (slot_in, slot_out)[kind].at[slot], slot_sem.at[slot, kind]
+            early, own = (early_in, early_out)[kind], (w_in, w_out)[kind]
+            full = (full_in, full_out)[kind]
+            if expert < EARLY_EXPERTS:
+                copies.append(pltpu.make_async_copy(early.at[expert], target, sem.at[0]))
+                continue
+            for ahead in range(size):
+                block = lax.rem(place.dp + ahead, size)
+                rows = rows_at(block, shares[kind])
+                source = full.at[expert - EARLY_EXPERTS, rows]
+                if (expert, kind) in GATHER_SPLIT:
+                    if ahead % 2 == 0:
+                        source = early.at[expert, rows]
+                elif ahead == 0:
+                    source = own.at[expert]
+                copies.append(pltpu.make_async_copy(source, target.at[rows], sem.at[ahead]))
+        return copies
 
     def keep(expert):
         return [
@@ -945,7 +967,7 @@
             shards.append(((early_in, early_out)[kind].at[expert], shares[kind], full, "side"))
         else:
             shards.append(((w_in, w_out)[kind].at[expert], shares[kind], full, "turned"))
-    gather = Gather(place, shards, *gather_sems)
+    gather = Gather(place, shards, *gather_sems, None)
     turned = range(len(GATHER_LATE))
     for unit in range(len(shards)):
         gather.start(unit)
@@ -985,9 +1007,9 @@
     plan(0, 0, *[copy.wait for copy in tokens()])
     for expert in range(EARLY_EXPERTS):
         plan(expert, 1, *[copy.wait for copy in load(expert)])
-    for hop in range(outers):
-        at = GATHER_POINTS[hop] if hop < outers - 1 else (3, 0)
-        plan(*at, *[lambda unit=unit, hop=hop: gather.step(unit, hop) for unit in turned])
+    for unit in turned:
+        for hop, at in enumerate(GATHER_POINTS[GATHER_LATE[unit][0]]):
+            plan(*at, lambda unit=unit, hop=hop: gather.step(unit, hop))
     for expert in range(EARLY_EXPERTS, local_count):
         units = [
             unit
@@ -1131,7 +1153,7 @@
             pltpu.SemaphoreType.DMA((3,)),
             pltpu.SemaphoreType.DMA((groups,)),
             pltpu.SemaphoreType.DMA((late, 2)),
-            pltpu.SemaphoreType.DMA((EARLY_EXPERTS, 2)),
+            pltpu.SemaphoreType.DMA((EARLY_EXPERTS, 2, size)),
             pltpu.SemaphoreType.DMA((2, groups)),
         ]
         + gather_semaphores(len(GATHER_LATE + GATHER_SPLIT), size)

time: 316 us -> 295 us (0.934)
  Pallas kernels: 297 us -> 276 us
    pallas_call x1, Pallas kernels: 93.7 us -> 82.9 us  [forward_sending(): pl.pallas_call(functools.partial(forward_sending_kernel, size // 2), out_...]
    pallas_call x1, Pallas kernels: 122 us -> 111 us  [expert_sending(): pl.pallas_call(functools.partial(expert_sending_kernel, outers), out_shap...]
where the time goes in v7:
time: 295 us; the launch traced here: 290 us
  Pallas kernels  276 us (94%)
  local copies, waits for them, and re-layouts  8.95 us (3%)
  other arithmetic  3.24 us (1%)
    pallas_call x1, Pallas kernels, expert_sending(): pl.pallas_call(functools.partial(expert_sending_kernel, outers), out_shap...  111 us
    pallas_call x1, Pallas kernels, forward_sending(): pl.pallas_call(functools.partial(forward_sending_kernel, size // 2), out_...  82.9 us
    pallas_call x1, Pallas kernels, backward_sending(): pl.pallas_call(functools.partial(backward_sending_kernel, outers, groups)...  81.6 us
    unnamed x22, local copies, waits for them, and re-layouts  7.55 us

profile of v7, /device:TPU:0, one launch (start us, length us, event | category | flops | bytes accessed | tf_op | source)
XLA Modules:
  0.0 289.9 jit_solution(8095610101052234733)
XLA Ops:
  1.3 1.7 copy.20
  3.0 82.9 %shard_map.178 = (f32[1024,384]{1,0:T(8,128)}, bf16[1024,1152]{1,0:T(8,128)(2,1)}, bf16[1024,384]{1,0:T(8,128)(2,1)}, f32[8,1024]{1,0:T(8,128)}, f32[16,1024]{1,...) custom-call(s32[1]{0:T(128)S(6)} %copy.26.top_count, ...), custom_call_target="tpu_custom_call" | custom-call | tf_op jit(solution)/shard_map/pallas_call | solution.py:748
  85.9 111.4 %shard_map.179 = (bf16[2,384,1536]{2,1,0:T(8,128)(2,1)}, bf16[2,1536,384]{2,1,0:T(8,128)(2,1)}, f32[4,4,1024]{2,1,0:T(4,128)}, bf16[4,1024,384]{2,1,0:T(8,128)(2...) custom-call(bf16[4,1024,384]{2,1,0:T(8,128)(2,1)} %get-tuple-element, ...), custom_call_target="tpu_custom_call" | custom-call | tf_op jit(solution)/shard_map/pallas_call | solution.py:1122
  197.3 0.0 copy-start.3
  197.3 81.6 %shard_map.180 = (f32[1024,384]{1,0:T(8,128)}, f32[1024,384]{1,0:T(8,128)}, f32[8,384]{1,0:T(8,128)}, f32[16,384]{1,0:T(8,128)}, f32[48,1152]{1,0:T(8,128)}, /*i...) custom-call(f32[1024,384]{1,0:T(8,128)} %bitcast.12, f32[1024,384]{1,0:T(8,128)} %bitcast.14, ...), custom_call_target="tpu_custom_call" | custom-call | tf_op jit(solution)/shard_map/pallas_call | solution.py:1490
  279.0 0.0 copy-start.2
  279.0 0.0 copy-start.4
  279.0 1.4 fusion
  280.4 0.0 copy-done.3
  280.4 2.2 pad_maximum_fusion
  282.5 0.0 copy-done.2
  282.5 0.0 copy-done.4
  282.6 0.0 copy-start.1
  282.6 1.1 pad_maximum_fusion.1
  283.6 0.7 copy-done.1
  284.4 0.0 copy-start
  284.4 1.1 copy.27
  285.5 0.8 copy-done
  286.4 0.0 copy-start.5
  286.4 0.0 copy-start.6
  286.4 0.0 copy-start.7
  286.4 1.1 copy.28
  287.5 0.0 copy-done.5
  287.5 0.7 copy.29
  288.2 0.0 copy-done.6
  288.2 0.6 copy.30
  288.8 0.0 copy-done.7
  288.8 0.6 copy.31
Async XLA Ops:
  197.3 83.1 %copy-start.3 = (f32[2,48,1536]{2,1,0:T(8,128)S(1)}, f32[2,48,1536]{2,1,0:T(8,128)}, u32[]{:S(2)}) copy-start(f32[2,48,1536]{2,1,0:T(8,128)} %get-tuple-element.65) | copy-start | bytes 1769476
  279.0 3.6 %copy-start.2 = (f32[3,192,384]{2,1,0:T(8,128)S(1)}, f32[3,192,384]{2,1,0:T(8,128)}, u32[]{:S(2)}) copy-start(f32[3,192,384]{2,1,0:T(8,128)} %get-tuple-element.68) | copy-start | bytes 2654212
  279.0 3.6 %copy-start.4 = (f32[1,192,384]{2,1,0:T(8,128)S(1)}, f32[1,192,384]{2,1,0:T(8,128)}, u32[]{:S(2)}) copy-start(f32[1,192,384]{2,1,0:T(8,128)} %get-tuple-element.67) | copy-start | bytes 884740
  282.6 1.8 copy-start.1
  284.4 2.0 copy-start
  286.4 1.2 copy-start.5
  286.4 1.8 copy-start.6
  286.4 2.5 copy-start.7

commit v8 on v7

--- a/solution.py
+++ b/solution.py
@@ -35,22 +35,27 @@
 GATHER_LATE = ((3, 0), (3, 1))
 SCATTER_EARLY = ((0, 0), (0, 1), (1, 0))
 SCATTER_SPLIT = ((1, 1), (2, 0))
-SCATTER_LATE = ((2, 1), (3, 0), (3, 1))
+SCATTER_LATE = ((2, 1), (3, 0), (3, 1, 0), (3, 1, 1))
 EARLY_EXPERTS = 2
 
 GATHER_POINTS = {2: ((0, 1), (0, 3), (1, 0), (1, 4)), 3: ((0, 2), (1, 1), (1, 4), (3, 0))}
-SCATTER_POINTS = ((3, 1), (3, 3))
-COMBINE_TURNS = (1, 2, 3)
+SCATTER_POINTS = {1: (2, 4), 3: (3, 6)}
 
 AHEAD = 2
 FORWARD_FIRST = ((0, 1), (1, 1))
 FORWARD_POINTS = {
-    0: ((2, 1), (3, 1)),
-    3: ((4, 1), (5, 1)),
-    8: ((0, 2), (1, 2)),
-    11: ((2, 2), (3, 2)),
+    0: ((2, 1),),
+    1: ((3, 1),),
+    2: ((4, 1),),
+    3: ((5, 1),),
+    5: ((0, 2),),
+    6: ((1, 2),),
+    8: ((2, 2),),
+    9: ((3, 2),),
+    10: ((4, 2),),
+    11: ((5, 2),),
 }
-FORWARD_THEN = (((4, 2), (5, 2)), ((0, 3), (1, 3), (2, 3), (3, 3), (4, 3), (5, 3)))
+FORWARD_THEN = (((0, 3), (1, 3)), ((2, 3), (3, 3), (4, 3), (5, 3)))
 
 BACKWARD_POINTS = {
     3: ("s1", "u0",),
@@ -58,8 +63,9 @@
     11: ("u1",),
 }
 BACKWARD_THEN = (
-    ("w0", "t2", "s3", "v1", "u2", "30", "00", "10",),
-    ("w1", "t3", "v2", "u3", "20", "31", "01", "11", "w2", "v3", "21", "32", "02", "12", "33", "03", "22", "13", "23", "w3",),
+    ("t2", "s3", "v1", "u2", "w0"),
+    ("x0", "t3", "v2", "u3", "w1", "00", "x1", "01", "v3", "w2", "02", "x2", "w3", "03"),
+    ("x3",),
 )
 
 
@@ -73,7 +79,7 @@
 
 
 def params(**more):
-    return pltpu.CompilerParams(vmem_limit_bytes=62 * 2**20, **more)
+    return pltpu.CompilerParams(vmem_limit_bytes=63 * 2**20, **more)
 
 
 def dot(a, b):
@@ -298,9 +304,9 @@
 
 
 class Scatter:
-    def __init__(self, place, mine, theirs, side, line, fold, sems):
+    def __init__(self, place, mine, theirs, side, line, sems):
         self.place, self.mine, self.theirs = place, mine, theirs
-        self.side, self.line, self.fold = side, line, fold
+        self.side, self.line = side, line
         self.side_sent, self.side_landed, self.line_sent, self.line_landed = sems
 
     def to_side(self, outer):
@@ -312,9 +318,12 @@
             dp=self.place.side,
         )
 
+    def fold(self, outer):
+        return self.mine(outer) if self.side is None else self.side.at[outer]
+
     def along(self, outer, slot, device):
         return remote(
-            self.fold.at[outer],
+            self.fold(outer),
             self.line.at[slot],
             self.line_sent.at[outer],
             self.line_landed.at[slot],
@@ -337,10 +346,13 @@
             rows += self.line[slot].astype(f32)
         return rows
 
-    def settle(self, store):
+    def settle(self, parts, sem):
         for outer in range(self.place.outers):
-            store(outer, self.total(outer).astype(bf16))
+            self.fold(outer)[...] = self.total(outer).astype(bf16)
             self.to_side(outer).wait_send()
+        copy = pltpu.make_async_copy(self.side, parts, sem)
+        copy.start()
+        return copy
 
     def hop(self, step):
         place, outers = self.place, self.place.outers
@@ -349,14 +361,14 @@
         def _():
             for outer in range(outers - 1, step, -1):
                 rows = self.total(outer, *([outer] if step else []))
-                self.fold[outer] = rows.astype(bf16)
+                self.fold(outer)[...] = rows.astype(bf16)
                 self.along(outer, outer, place.up).start()
 
         @pl.when(place.outer == outers - 1 - step)
         def _():
             for outer in range(outers - 1 - step):
                 rows = self.total(outer, *([outer] if step else []))
-                self.fold[outer] = rows.astype(bf16)
+                self.fold(outer)[...] = rows.astype(bf16)
                 slot = outers if outer == outers - 2 - step else outer
                 self.along(outer, slot, place.down).start()
 
@@ -374,6 +386,44 @@
 
             if self.side is not None:
                 self.to_side(outer).wait_send()
+
+
+class Turned:
+    def __init__(self, place, mine, theirs, refs):
+        self.place = place
+        self.own = Scatter(place, mine, None, None, refs[0], (None, None, *refs[1:3]))
+        self.other = Scatter(place, theirs, None, None, refs[3], (None, None, *refs[4:6]))
+        self.stage, self.land, self.sent, self.landed = refs[6:]
+
+    def move(self):
+        return remote(self.stage, self.land, self.sent, self.landed, dp=self.place.side)
+
+    def start(self):
+        self.own.hop(0)
+        self.other.hop(0)
+
+    def hop(self, step):
+        if step:
+            self.own.hop(step)
+            self.other.hop(step)
+
+    def finish(self, store):
+        def send(rows):
+            self.stage[...] = rows.astype(bf16)
+            self.move().start()
+
+        self.other.finish(send)
+        self.own.finish(store)
+
+    def add(self, shard):
+        self.move().wait()
+        shard[...] += self.land[...].astype(f32)
+
+
+def turned_scratch(outers, tile):
+    line = [pltpu.VMEM((outers + 1, *tile), bf16)]
+    line += [pltpu.SemaphoreType.DMA((count,)) for count in (outers, outers + 1)]
+    return line * 2 + [pltpu.VMEM(tile, bf16)] * 2 + [pltpu.SemaphoreType.DMA] * 2
 
 
 def scatter_turn(units, stores, turn):
@@ -386,22 +436,25 @@
         units[last].finish(stores[last])
 
 
-def blocks_of(place, ref, size):
+def blocks_of(place, ref, size, half=()):
+    def block(index):
+        if half:
+            return ref.at[rows_at(2 * index + half[0], size // 2)]
+        return ref.at[rows_at(index, size)]
+
     return (
-        lambda outer: ref.at[rows_at(2 * outer + place.inner, size)],
-        lambda outer: ref.at[rows_at(2 * outer + 1 - place.inner, size)],
-    )
-
-
-def tile_of(kind, thin, wide):
-    return (wide, D) if kind else (thin, FF)
+        lambda outer: block(2 * outer + place.inner),
+        lambda outer: block(2 * outer + 1 - place.inner),
+    )
 
 
 def scatter_scratch(units, outers, tiles, side=True, line=True):
     scratch = []
     for unit in units:
         tile = tiles[unit[1]] if isinstance(unit, tuple) else tiles
-        for asked, slots in ((side, outers), (line, outers + 1), (line, outers)):
+        if isinstance(unit, tuple) and len(unit) > 2:
+            tile = (tile[0] // 2, tile[1])
+        for asked, slots in ((side, outers), (line, outers + 1)):
             if asked:
                 scratch.append(pltpu.VMEM((slots, *tile), bf16))
         for asked, count in ((side, outers), (side, outers), (line, outers), (line, outers + 1)):
@@ -411,11 +464,11 @@
 
 
 def make_scatters(place, blocks, refs, side=True, line=True):
-    count = 3 * side + 4 * line
+    count = 3 * side + 3 * line
     scatters = []
     for index, (mine, theirs) in enumerate(blocks):
         own = list(refs[index * count : (index + 1) * count])
-        buffers = [own.pop(0) if asked else None for asked in (side, line, line)]
+        buffers = [own.pop(0) if asked else None for asked in (side, line)]
         sems = [own.pop(0) if asked else None for asked in (side, side, line, line)]
         scatters.append(Scatter(place, mine, theirs, *buffers, sems))
     return scatters
@@ -440,10 +493,13 @@
         for ahead in range(1, self.count):
             self.move(self.me, ahead).start()
 
-    def take(self):
+    def arrive(self):
         for ahead in range(1, self.count):
             self.move(lax.rem(self.me + self.count - ahead, self.count), ahead).wait_recv()
             self.move(self.me, ahead).wait_send()
+
+    def take(self):
+        self.arrive()
         total = self.land[0].astype(f32)
         for index in range(1, self.count):
             total += self.land[index].astype(f32)
@@ -451,10 +507,10 @@
 
 
 class Return:
-    def __init__(self, place, parts, pieces, land, joint, sent, landed):
+    def __init__(self, place, parts, pieces, land, sent, landed):
         self.place, self.parts, self.pieces = place, parts, pieces
-        self.land, self.joint, self.sent, self.landed = land, joint, sent, landed
-        self.size = SEQ // pieces
+        self.land, self.sent, self.landed = land, sent, landed
+        self.size = land.shape[1] // pieces
 
     def rows(self, piece):
         return pl.ds(piece * self.size, self.size)
@@ -462,9 +518,9 @@
     def move(self, way, piece):
         place, rows = self.place, self.rows(piece)
         source = [
-            self.parts(place.core).at[rows],
-            self.parts(place.far).at[rows],
-            self.joint.at[rows],
+            self.parts[0].at[rows],
+            self.parts[1].at[rows],
+            self.parts[2].at[rows],
         ][way]
         return remote(
             source,
@@ -483,9 +539,9 @@
     def to_across(self, piece):
         rows = self.rows(piece)
         self.move(1, piece).wait_recv()
-        joint = self.parts(self.place.across)[rows, :].astype(f32)
+        joint = self.parts[2][rows, :].astype(f32)
         joint += self.land[1, rows, :].astype(f32)
-        self.joint[rows, :] = joint.astype(bf16)
+        self.parts[2][rows, :] = joint.astype(bf16)
         self.move(2, piece).start()
 
     def finish(self, piece):
@@ -493,7 +549,7 @@
         self.move(0, piece).wait()
         self.move(1, piece).wait_send()
         self.move(2, piece).wait()
-        total = self.parts(self.place.task)[rows, :].astype(f32)
+        total = self.parts[3][rows, :].astype(f32)
         return total + self.land[0, rows, :].astype(f32) + self.land[2, rows, :].astype(f32)
 
 
@@ -638,7 +694,7 @@
     w_proj,
     w_in,
     w_out,
-    router,
+    router_columns,
     choices,
     mid,
     packed,
@@ -649,12 +705,13 @@
     cot_all,
     slots_all,
     gates_all,
-    full_qkv,
-    full_proj,
+    quarters,
     full_in,
     full_out,
     normed_first,
     totals,
+    router,
+    own_quarter,
     sent,
     landed,
     stay,
@@ -663,20 +720,22 @@
 ):
     place = Place(outers)
     task = place.task
-    shards = [
-        (w_qkv, w_qkv.shape[0], full_qkv, "both"),
-        (w_proj, w_proj.shape[0], full_proj, "both"),
-    ]
+    for part in range(4):
+
+        @pl.when(task == part)
+        def _():
+            own_quarter[...] = w_proj[...] if part == 3 else w_qkv[:, part * D : (part + 1) * D]
+
+    shards = [(own_quarter, w_qkv.shape[0], quarters.at[task], "both")]
     for expert, kind in GATHER_WHOLE + GATHER_SPLIT:
         own, full = ((w_in, full_in), (w_out, full_out))[kind]
         mode = "line" if (expert, kind) in GATHER_SPLIT else "both"
         shards.append((own.at[expert], own.shape[1], full.at[expert], mode))
     gather = Gather(place, shards, sent, landed, stay)
-    shared, routed = range(2), range(2, len(shards))
+    routed = range(1, len(shards))
     cot_all[task] = cotangent[...].astype(bf16)
     place.greet()
-    for unit in shared:
-        gather.start(unit)
+    gather.start(0)
 
     def share(index, view):
         return Share(place, view, share_sent.at[index], share_landed.at[index])
@@ -684,34 +743,38 @@
     cot = share(0, lambda source: cot_all.at[source])
     slot = share(1, lambda source: slots_all.at[source])
     gate = share(2, lambda source: gates_all.at[source])
-    for unit in routed[:AHEAD]:
-        gather.start(unit)
-    cot.start()
-    first_norm(image, gain, bias, normed_first)
-    for hop in range(1, outers):
-        for unit in shared:
-            gather.step(unit, hop)
-    for unit in routed[AHEAD:]:
-        gather.start(unit)
-    slots_all[task] = number_slots(choices, top_count, router.shape[0])
-    slot.start()
-    totals[...] = jnp.zeros_like(totals)
-    for unit in shared:
-        gather.finish(unit)
-    packed[...] = dot(normed_first[...], full_qkv[...]).astype(bf16)
-    cot.relay()
-    slot.relay()
-
-    def chunk(index):
-        return share(3 + index, lambda source: normed_all.at[source, rows_at(index, QUERY_FWD)])
-
     def run(acts):
         for unit, hop in acts:
             if unit < len(routed):
                 gather.step(routed[unit], hop)
 
+    for unit in routed[:AHEAD]:
+        gather.start(unit)
+    cot.start()
+    router[...] = router_columns[...].T
+    first_norm(image, gain, bias, normed_first)
+    for hop in range(1, outers):
+        gather.step(0, hop)
+    for unit in routed[AHEAD:]:
+        gather.start(unit)
+    gather.finish(0)
+    quarter = share(3 + SEQ // QUERY_FWD, lambda source: quarters.at[source])
+    quarter.start()
+    slots_all[task] = number_slots(choices, top_count, router.shape[0])
+    slot.start()
+    totals[...] = jnp.zeros_like(totals)
+    run(FORWARD_FIRST)
+    quarter.relay()
+    quarter.finish()
+    for part in range(3):
+        packed[:, part * D : (part + 1) * D] = dot(normed_first[...], quarters[part]).astype(bf16)
+    cot.relay()
+    slot.relay()
+
+    def chunk(index):
+        return share(3 + index, lambda source: normed_all.at[source, rows_at(index, QUERY_FWD)])
+
     blocks = SEQ // QUERY_FWD
-    run(FORWARD_FIRST)
 
     def block(index, _):
         def between(point):
@@ -720,7 +783,7 @@
 
         attend(packed, mixed, totals, index, between)
         normed_all[task, rows_at(index, QUERY_FWD), :] = mid_block(
-            index, image, gain, bias, full_proj, router, mixed, mid, probs
+            index, image, gain, bias, quarters.at[3], router, mixed, mid, probs
         )
         chunk(index).start()
         pl.when(index > 0)(lambda: chunk(index - 1).relay())
@@ -742,9 +805,9 @@
 
 def forward_sending(top_count, image, cotangent, gain, bias, shards, router, choices):
     w_qkv, w_proj, w_in, w_out = shards
-    experts, size = router.shape[0], lax.axis_size("dp")
+    experts, size = router.shape[1], lax.axis_size("dp")
     groups, early = lax.axis_size("task"), 1 + GATHER_SPLIT[-1][0]
-    units, shares = 2 + len(GATHER_WHOLE + GATHER_SPLIT), 3 + SEQ // QUERY_FWD
+    units, shares = 1 + len(GATHER_WHOLE + GATHER_SPLIT), 4 + SEQ // QUERY_FWD
     return pl.pallas_call(
         functools.partial(forward_sending_kernel, size // 2),
         out_shape=(
@@ -757,16 +820,17 @@
             shape(groups, SEQ, D, dtype=bf16),
             shape(groups, experts, SEQ, dtype=jnp.int32),
             shape(groups, experts, SEQ),
-            shape(D, 3 * D, dtype=bf16),
-            shape(D, D, dtype=bf16),
+            shape(groups, D, D, dtype=bf16),
             shape(early, D, FF, dtype=bf16),
             shape(early, FF, D, dtype=bf16),
         ),
         in_specs=[SMEM] + [VMEM] * 10,
-        out_specs=[VMEM] * 11 + [ANY] * 2,
+        out_specs=[VMEM] * 10 + [ANY] * 2,
         scratch_shapes=[
             pltpu.VMEM((SEQ, D), bf16),
             pltpu.VMEM((SEQ, 8), f32),
+            pltpu.VMEM((experts, D), f32),
+            pltpu.VMEM(w_proj.shape, bf16),
             *gather_semaphores(units, size),
             pltpu.SemaphoreType.DMA((units,)),
             pltpu.SemaphoreType.DMA((shares, 3)),
@@ -784,32 +848,28 @@
     return jnp.where(hits, 1.0, 0.0).astype(bf16)
 
 
-def one_expert(operands, work, grads, expert, first, slot, between):
-    normed, cotangent, slots, gates, w_in, w_out = operands
-    rows_in, rows_grad, rows_cot, rows_gate, hidden, grad_pre, sent = work
-    grad_in, grad_out, grad_gates = grads
-    groups = normed.shape[0]
-    width = groups * CAP
-    between(0)
-    for source in range(groups):
-        own = slice(source * CAP, (source + 1) * CAP)
-        hits = slot_hits(slots, source, first + expert)
-        picks = ones_at(hits)
-        rows_in[own, :] = dot(picks, normed[source]).astype(bf16)
-        cot_rows = dot(picks, cotangent[source])
-        gate = jnp.sum(
-            jnp.where(hits, gates[source, pl.ds(first + expert, 1), :], 0.0),
-            axis=1,
-            keepdims=True,
-        )
-        rows_cot[own, :] = cot_rows.astype(bf16)
-        rows_grad[own, :] = (gate * cot_rows).astype(bf16)
-        rows_gate[own, :] = jnp.broadcast_to(gate, (CAP, 128))
-    between(1)
+def dispatch(operands, work, expert, first, block, source):
+    tokens, slots, gates = operands[:3]
+    rows_in, rows_grad, rows_cot, rows_gate = work[:4]
+    own = slice(block * CAP, (block + 1) * CAP)
+    hits = slot_hits(slots, source, first + expert)
+    both = dot(ones_at(hits), tokens[source])
+    gate = jnp.sum(
+        jnp.where(hits, gates[source, pl.ds(first + expert, 1), :], 0.0), axis=1, keepdims=True
+    )
+    rows_in[own, :] = both[:, :D].astype(bf16)
+    rows_cot[own, :] = both[:, D:].astype(bf16)
+    rows_grad[own, :] = (gate * both[:, D:]).astype(bf16)
+    rows_gate[own, :] = jnp.broadcast_to(gate, (CAP, 128))
+
+
+def hidden_tiles(operands, work, slot, start, count):
+    w_in, w_out = operands[3:]
+    rows_in, rows_grad, _, _, hidden, grad_pre, _ = work
 
     def tile(index, _):
-        units = rows_at(index // (width // ROW_TILE), FF_TILE)
-        rows = rows_at(lax.rem(index, width // ROW_TILE), ROW_TILE)
+        units = rows_at(index // count, FF_TILE)
+        rows = rows_at(start + lax.rem(index, count), ROW_TILE)
         pre = dot(rows_in[rows, :], w_in[slot, :, units])
         grad_hidden = dot_rt(rows_grad[rows, :], w_out[slot, units, :])
         share = 0.5 * lax.erf(pre * ROOT_HALF) + 0.5
@@ -818,23 +878,49 @@
         grad_pre[rows, units] = (grad_hidden * slope).astype(bf16)
         return 0
 
-    lax.fori_loop(0, (FF // FF_TILE) * (width // ROW_TILE), tile, 0)
-    between(2)
-    for source in range(groups):
-        own = slice(source * CAP, (source + 1) * CAP)
-        kept = rows_at(expert, CAP)
-        out_rows = dot(hidden[own, :], w_out[slot]).astype(bf16).astype(f32)
-        sent[source, kept, :D] = (rows_gate[own, 0:1] * out_rows).astype(bf16)
-        sent[source, kept, D:] = dot_rt(grad_pre[own, :], w_in[slot]).astype(bf16)
-        grad_gate = jnp.sum(rows_cot[own, :].astype(f32) * out_rows, axis=1, keepdims=True)
-        hits = slot_hits(slots, source, first + expert)
-        grad_gates[source, pl.ds(expert, 1), :] = jnp.sum(
-            jnp.where(hits, grad_gate, 0.0), axis=0, keepdims=True
-        )
-    between(3)
-    grad_in[expert] = dot_lt(rows_in[...], grad_pre[...]).astype(bf16)
-    grad_out[expert] = dot_lt(rows_grad[...], hidden[...]).astype(bf16).T
-    between(4)
+    lax.fori_loop(0, (FF // FF_TILE) * count, tile, 0)
+
+
+def expert_rows_out(operands, work, grad_gates, expert, first, slot, block, source):
+    slots, (w_in, w_out) = operands[1], operands[3:]
+    _, _, rows_cot, rows_gate, hidden, grad_pre, sent = work
+    own = slice(block * CAP, (block + 1) * CAP)
+    kept = rows_at(expert, CAP)
+    out_rows = dot(hidden[own, :], w_out[slot]).astype(bf16).astype(f32)
+    sent[source, kept, :D] = (rows_gate[own, 0:1] * out_rows).astype(bf16)
+    sent[source, kept, D:] = dot_rt(grad_pre[own, :], w_in[slot]).astype(bf16)
+    grad_gate = jnp.sum(rows_cot[own, :].astype(f32) * out_rows, axis=1, keepdims=True)
+    hits = slot_hits(slots, source, first + expert)
+    grad_gates[source, pl.ds(expert, 1), :] = jnp.sum(
+        jnp.where(hits, grad_gate, 0.0), axis=0, keepdims=True
+    )
+
+
+def weight_grads(work, grads, expert):
+    rows_in, rows_grad, _, _, hidden, grad_pre, _ = work
+    grads[0][expert] = dot_lt(rows_in[...], grad_pre[...]).astype(bf16)
+    grads[1][expert] = dot_lt(rows_grad[...], hidden[...]).astype(bf16).T
+
+
+def one_expert(operands, work, grads, expert, first, slot, sources, between, halfway=None):
+    halves = 1 if halfway is None else 2
+    size, tiles = len(sources) // halves, len(sources) * CAP // ROW_TILE // halves
+    between(0)
+    for block, source in enumerate(sources):
+        dispatch(operands, work, expert, first, block, source)
+    between(1)
+    for half in range(halves):
+        hidden_tiles(operands, work, slot, half * tiles, tiles)
+        between(2 + half * 2)
+        for block in range(half * size, (half + 1) * size):
+            expert_rows_out(
+                operands, work, grads[2], expert, first, slot, block, sources[block]
+            )
+        if half + 1 < halves:
+            halfway()
+    between(3 if halves == 1 else 5)
+    weight_grads(work, grads, expert)
+    between(4 if halves == 1 else 6)
 
 
 def combine(slots, first, local_count, sent, columns, source, store):
@@ -869,12 +955,14 @@
 
 
 def expert_kernel(*refs):
-    operands, grads, (mixes, grad_normed) = refs[:6], refs[6:9], refs[9:11]
-    work, columns = refs[11:18], refs[18]
-    groups, local_count = operands[0].shape[0], operands[4].shape[0]
+    operands, grads, (mixes, grad_normed) = refs[:5], refs[5:8], refs[8:10]
+    work, columns = refs[10:17], refs[17]
+    groups, local_count = operands[0].shape[0], operands[3].shape[0]
 
     def body(expert, _):
-        one_expert(operands, work, grads, expert, 0, expert, lambda point: None)
+        one_expert(
+            operands, work, grads, expert, 0, expert, range(groups), lambda point: None
+        )
         return 0
 
     lax.fori_loop(0, local_count, body, 0)
@@ -884,11 +972,11 @@
             mixes[source, rows, :] = mix
             grad_normed[source, rows, :] = grad
 
-        combine(operands[2], 0, local_count, work[6], columns, source, store)
+        combine(operands[1], 0, local_count, work[6], columns, source, store)
 
 
 def expert_part(*operands):
-    groups, local_count = operands[0].shape[0], operands[4].shape[0]
+    groups, local_count = operands[0].shape[0], operands[3].shape[0]
     return pl.pallas_call(
         expert_kernel,
         out_shape=(
@@ -898,9 +986,9 @@
             shape(groups, SEQ, D, dtype=bf16),
             shape(groups, SEQ, D, dtype=bf16),
         ),
-        in_specs=[VMEM] * 6,
+        in_specs=[VMEM] * 5,
         out_specs=[VMEM] * 5,
-        scratch_shapes=expert_scratch(groups, local_count, operands[2].shape[1]),
+        scratch_shapes=expert_scratch(groups, local_count, operands[1].shape[1]),
         compiler_params=params(),
     )(*operands)
 
@@ -910,20 +998,24 @@
     late_in, late_out, gate_all, mixes, grad_rows, shard_in, shard_out, parts_in, parts_out = refs[8:17]
     full_in, full_out = refs[17:19]
     work, columns = refs[19:26], refs[26]
-    normed, cotangent, slot_in, slot_out, grad_in, grad_out, grad_gates, land = refs[27:35]
+    both, slot_in, slot_out, grad_in, grad_out, grad_gates, land, first_parts = refs[27:35]
     sent, landed, gate_sent, gate_landed, mix_sem, late_sem, slot_sem, token_sem = refs[35:43]
-    gather_sems, scatter_refs = refs[43:45], refs[45:]
+    part_sem, gather_sems, scatter_refs = refs[43], refs[44:46], refs[46:]
     place = Place(outers)
-    groups, local_count, size = normed.shape[0], grad_in.shape[0], 2 * outers
+    groups, local_count, size = both.shape[0], grad_in.shape[0], 2 * outers
     late = local_count - EARLY_EXPERTS
     first = place.task * local_count
     grads, shares = (grad_in, grad_out), (w_in.shape[1], w_out.shape[1])
 
     def tokens():
         return [
-            pltpu.make_async_copy(whole.at[source], ref.at[source], token_sem.at[kind, source])
+            pltpu.make_async_copy(
+                whole.at[source],
+                both.at[source, :, pl.ds(kind * D, D)],
+                token_sem.at[kind, source],
+            )
             for source in range(groups)
-            for kind, (whole, ref) in enumerate(((normed_all, normed), (cot_all, cotangent)))
+            for kind, whole in enumerate((normed_all, cot_all))
         ]
 
     def load(expert):
@@ -973,7 +1065,7 @@
         gather.start(unit)
     for copy in load(1):
         copy.start()
-    per_full, per_side = 7 * len(SCATTER_EARLY), 3 * len(SCATTER_SPLIT)
+    per_full, per_side = 6 * len(SCATTER_EARLY[1:]), 3 * len(SCATTER_SPLIT)
 
     def scatters(units, refs, **parts):
         return make_scatters(
@@ -983,7 +1075,13 @@
             **parts,
         )
 
-    whole = scatters(SCATTER_EARLY, scatter_refs[:per_full])
+    expert, kind = SCATTER_EARLY[0]
+    turned_scatter = Turned(
+        place,
+        *blocks_of(place, grads[kind].at[expert], shares[kind]),
+        scatter_refs[per_full + per_side :],
+    )
+    whole = [turned_scatter] + scatters(SCATTER_EARLY[1:], scatter_refs[:per_full])
     split = scatters(SCATTER_SPLIT, scatter_refs[per_full : per_full + per_side], line=False)
     stores, keeps = [], []
     for expert, kind in SCATTER_EARLY:
@@ -995,10 +1093,7 @@
     for index, (_, kind) in enumerate(SCATTER_SPLIT):
         at = [other[1] for other in SCATTER_SPLIT[:index]].count(kind)
 
-        def settle(outer, rows, parts=(parts_in, parts_out)[kind], at=at):
-            parts[at, outer] = rows
-
-        keeps.append(settle)
+        keeps.append((parts_in, parts_out)[kind].at[at])
     steps = {}
 
     def plan(expert, point, *acts):
@@ -1019,17 +1114,22 @@
         plan(expert, 0, *[lambda unit=unit: gather.finish(unit) for unit in units])
         plan(expert, 0, *[copy.start for copy in load(expert)])
         plan(expert, 1, *[copy.wait for copy in load(expert)])
-        plan(expert, 4, *[copy.start for copy in keep(expert - EARLY_EXPERTS)])
+        point = 4 if expert < local_count - 1 else 6
+        plan(expert, point, *[copy.start for copy in keep(expert - EARLY_EXPERTS)])
     for index, (expert, _) in enumerate(SCATTER_EARLY):
         plan(expert, 4, whole[index].start)
     for index, (expert, _) in enumerate(SCATTER_SPLIT):
         plan(expert, 4, split[index].start)
-    for turn, at in enumerate(SCATTER_POINTS):
+    for turn, at in SCATTER_POINTS.items():
         plan(*at, lambda turn=turn: scatter_turn(whole, stores, turn))
+
+    operands = (both, slots, gates, slot_in, slot_out)
+    every_grad = (grad_in, grad_out, grad_gates)
+    sources = (place.far, place.across, place.core, place.task)
 
     def body(expert, _):
         def between(point):
-            for at in range(local_count):
+            for at in range(local_count - 1):
                 acts = steps.get((at, point))
                 if acts:
 
@@ -1039,17 +1139,71 @@
                             act()
 
         one_expert(
-            (normed, cotangent, slots, gates, slot_in, slot_out),
+            operands,
             work,
-            (grad_in, grad_out, grad_gates),
+            every_grad,
             expert,
             first,
             lax.rem(expert, EARLY_EXPERTS),
+            sources,
             between,
         )
         return 0
 
-    lax.fori_loop(0, local_count, body, 0)
+    lax.fori_loop(0, local_count - 1, body, 0)
+    hidden, grad_pre = work[4], work[5]
+
+    def part(ref, block):
+        return ref.at[pl.ds(0, SEQ), pl.ds(block * D, D)]
+
+    parts = [first_parts.at[0], first_parts.at[1], part(hidden, 0), part(hidden, 1)]
+    mix_parts = [first_parts.at[2], first_parts.at[2], part(grad_pre, 0), part(grad_pre, 1)]
+    back = Return(
+        place,
+        (parts[2], parts[0], parts[1], parts[3]),
+        RETURNS,
+        land,
+        sent,
+        landed,
+    )
+    sends = (back.by_core, back.to_across, back.to_core, None)
+
+    def mix_copy(block):
+        return pltpu.make_async_copy(
+            mix_parts[block], mixes.at[sources[block]], mix_sem.at[block]
+        )
+
+    def returned(block):
+        def store(piece, rows, mix, grad):
+            mix_parts[block][rows, :] = mix
+            parts[block][rows, :] = grad
+            if sends[block]:
+                sends[block](piece)
+
+        combine(slots, first, local_count, work[6], columns, sources[block], store)
+        mix_copy(block).start()
+
+    def halfway():
+        returned(0)
+        mix_copy(0).wait()
+        returned(1)
+        scatter_turn(whole, stores, 2)
+
+    def last(point):
+        for act in steps.get((local_count - 1, point), ()):
+            act()
+
+    one_expert(
+        operands,
+        work,
+        every_grad,
+        local_count - 1,
+        first,
+        (local_count - 1) % EARLY_EXPERTS,
+        sources,
+        last,
+        halfway,
+    )
     gate_all[place.task] = grad_gates[place.task]
     peers = (place.core, place.across, place.far)
 
@@ -1064,53 +1218,30 @@
 
     for way in range(3):
         gate_move(way).start()
-    hidden, grad_pre, joint = work[4], work[5], work[2]
-
-    def part(ref, source):
-        return ref.at[pl.ds(0, SEQ), pl.ds(pl.multiple_of(source * D, 128), D)]
-
-    back = Return(
-        place, lambda source: part(hidden, source), RETURNS, land, joint, sent, landed
-    )
-    turns = list(range(len(SCATTER_POINTS), len(whole) + outers - 1))
-    for order, (source, after) in enumerate(
-        (
-            (place.far, back.by_core),
-            (place.across, back.to_across),
-            (place.core, back.to_core),
-            (place.task, None),
-        )
-    ):
-
-        def store(piece, rows, mix, grad, source=source, after=after):
-            part(grad_pre, source)[rows, :] = mix
-            part(hidden, source)[rows, :] = grad
-            if after:
-                after(piece)
-
-        combine(slots, first, local_count, work[6], columns, source, store)
-        pltpu.make_async_copy(part(grad_pre, source), mixes.at[source], mix_sem.at[order]).start()
-        if order in COMBINE_TURNS and turns:
-            scatter_turn(whole, stores, turns.pop(0))
-    for turn in turns:
+    returned(2)
+    returned(3)
+    for turn in range(4, len(whole) + outers - 1):
         scatter_turn(whole, stores, turn)
-    for index, one in enumerate(split):
-        one.settle(keeps[index])
+    expert, kind = SCATTER_EARLY[0]
+    turned_scatter.add((shard_in, shard_out)[kind].at[expert])
+    settled = [
+        one.settle(keeps[index], part_sem.at[index]) for index, one in enumerate(split)
+    ]
     for piece in range(RETURNS):
         grad_rows[back.rows(piece), :] = back.finish(piece)
     for way in range(3):
         gate_move(way).wait()
-    for order in range(groups):
-        pltpu.make_async_copy(
-            part(grad_pre, place.task), mixes.at[place.task], mix_sem.at[order]
-        ).wait()
+    for block in range(1, groups):
+        mix_copy(block).wait()
     for expert in range(late):
         for copy in keep(expert):
             copy.wait()
+    for copy in settled:
+        copy.wait()
 
 
 def kinds(units, kind):
-    return [unit for unit in units if unit[1] == kind]
+    return sorted({unit[0] for unit in units if unit[1] == kind})
 
 
 def expert_sending(*operands):
@@ -1136,16 +1267,16 @@
             shape(late, FF, D, dtype=bf16),
         ),
         in_specs=[ANY] * 2 + [VMEM] * 2 + [ANY] * 4,
-        out_specs=[ANY] * 2 + [VMEM, ANY] + [VMEM] * 5 + [ANY] * 2,
+        out_specs=[ANY] * 2 + [VMEM, ANY] + [VMEM] * 3 + [ANY] * 4,
         scratch_shapes=expert_scratch(groups, local_count, experts)
         + [
-            pltpu.VMEM((groups, SEQ, D), bf16),
-            pltpu.VMEM((groups, SEQ, D), bf16),
+            pltpu.VMEM((groups, SEQ, 2 * D), bf16),
             pltpu.VMEM((EARLY_EXPERTS, D, FF), bf16),
             pltpu.VMEM((EARLY_EXPERTS, FF, D), bf16),
             pltpu.VMEM((local_count, D, FF), bf16),
             pltpu.VMEM((local_count, FF, D), bf16),
             pltpu.VMEM((groups, local_count, SEQ), f32),
+            pltpu.VMEM((3, SEQ, D), bf16),
             pltpu.VMEM((3, SEQ, D), bf16),
             pltpu.SemaphoreType.DMA((3, RETURNS)),
             pltpu.SemaphoreType.DMA((3, RETURNS)),
@@ -1155,10 +1286,12 @@
             pltpu.SemaphoreType.DMA((late, 2)),
             pltpu.SemaphoreType.DMA((EARLY_EXPERTS, 2, size)),
             pltpu.SemaphoreType.DMA((2, groups)),
+            pltpu.SemaphoreType.DMA((len(SCATTER_SPLIT),)),
         ]
         + gather_semaphores(len(GATHER_LATE + GATHER_SPLIT), size)
-        + scatter_scratch(SCATTER_EARLY, outers, tiles)
-        + scatter_scratch(SCATTER_SPLIT, outers, tiles, line=False),
+        + scatter_scratch(SCATTER_EARLY[1:], outers, tiles)
+        + scatter_scratch(SCATTER_SPLIT, outers, tiles, line=False)
+        + turned_scratch(outers, tiles[SCATTER_EARLY[0][1]]),
         compiler_params=params(collective_id=1, has_side_effects=True),
     )(*operands)
 
@@ -1241,10 +1374,12 @@
         grad_mixed[rows, :] = dot_rt(low_rows, w_proj[...]).astype(bf16)
 
 
-def first_back(image, gain, w_qkv, grad_packed, grad_mid, grad_image, grad_norm):
+def first_back(image, gain, parts, grad_packed, grad_mid, grad_image, grad_norm):
     def block(index, _):
         rows = rows_at(index, ROWS)
-        grad_rows = dot_rt(grad_packed[rows, :], w_qkv[...])
+        grad_rows = sum(
+            dot_rt(grad_packed[rows, part * D : (part + 1) * D], parts(part)) for part in range(3)
+        )
         grad_in, grad_gain, grad_bias, _ = norm_back(image[rows, :], grad_rows, gain[0:1, :])
         grad_image[rows, :] = grad_mid[rows, :] + grad_in
         grad_norm[0:1, :] += grad_gain
@@ -1310,7 +1445,15 @@
         lambda pair, index: None,
         lambda pair, columns: None,
     )
-    first_back(image, gain, w_qkv, grad_packed, grad_mid, grad_image, grad_norm)
+    first_back(
+        image,
+        gain,
+        lambda part: w_qkv[:, part * D : (part + 1) * D],
+        grad_packed,
+        grad_mid,
+        grad_image,
+        grad_norm,
+    )
     grad_shared[:, : 3 * D] = dot_lt(normed_first[...], grad_packed[...]).astype(bf16)
 
 
@@ -1333,15 +1476,23 @@
 
 
 def backward_sending_kernel(outers, groups, *refs):
-    image, cotangent, gain, bias, mid, w_qkv, w_proj, router = refs[:8]
-    packed, mixed, logs, mixes_all, grad_rows, grad_gates, probs, late_in, late_out = refs[8:17]
-    parts_in, parts_out = refs[17:19]
-    activations, grad_image, grad_norm, grad_router, shard_qkv, shard_proj = refs[19:25]
+    whole, (gain, bias, router_columns, logs, grad_gates, probs) = refs[:9], refs[9:15]
+    mixes_all, late_in, late_out = refs[15:18]
+    activations, grad_image, grad_gain, grad_bias, grad_router, shard_qkv, shard_proj = refs[18:25]
     shard_in, shard_out = refs[25:27]
     grad_mid, grad_low, grad_mixed, grad_packed, grad_keys, grad_values, normed_first = refs[27:34]
-    norm_sums, router_sums, shared, mixes, land, joint, back_sent, back_landed = refs[34:42]
-    mix_sem, grad_sem, grad_refs = refs[42], refs[43], refs[44 : 44 + len(SCATTER_LATE)]
-    refs = refs[44 + len(SCATTER_LATE) :]
+    norm_sums, router_sums, shared, mixes, land, back_sent, back_landed = refs[34:41]
+    router, own_shared, shared_land, shared_sent, shared_landed = refs[41:46]
+    here, here_sem = refs[46:55], refs[55]
+    parts_in, parts_out, image, cotangent, mid, quarters, packed, mixed, grad_rows = here
+    refs = refs[56:]
+    late_grads = sorted({unit[:2] for unit in SCATTER_LATE})
+    mix_sem, grad_sem, grad_refs = refs[0], refs[1], refs[2 : 2 + len(late_grads)]
+    refs = refs[2 + len(late_grads) :]
+    inputs = [
+        pltpu.make_async_copy(source, target, here_sem.at[index])
+        for index, (source, target) in enumerate(zip(whole, here))
+    ]
     place = Place(outers)
     size, pieces = 2 * outers, HEADS // 2 + 1
     shards = (shard_in, shard_out)
@@ -1351,18 +1502,20 @@
             grad_refs[index],
             grad_sem.at[index],
         )
-        for index, (expert, kind) in enumerate(SCATTER_LATE)
+        for index, (expert, kind) in enumerate(late_grads)
     ]
     mix_load = pltpu.make_async_copy(mixes_all, mixes, mix_sem)
-    for copy in (*loads, mix_load):
+    for copy in (*inputs[:2], *loads, *inputs[2:], mix_load):
         copy.start()
     place.greet_all(groups)
-    at = 7 * len(SCATTER_LATE)
+    at = 6 * len(SCATTER_LATE)
     late = make_scatters(
         place,
         [
-            blocks_of(place, grad_refs[index], shards[kind].shape[1])
-            for index, (_, kind) in enumerate(SCATTER_LATE)
+            blocks_of(
+                place, grad_refs[late_grads.index(unit[:2])], shards[unit[1]].shape[1], unit[2:]
+            )
+            for unit in SCATTER_LATE
         ],
         refs[:at],
     )
@@ -1378,46 +1531,48 @@
             )
         )
     split = make_scatters(place, split_blocks, refs[at:], side=False)
-    at += 4 * len(SCATTER_SPLIT)
-    small = make_scatters(
-        place,
-        [blocks_of(place, shared.at[piece], shard_proj.shape[0]) for piece in range(pieces)],
-        refs[at:],
-    )
-    at += 7 * pieces
+    at += 3 * len(SCATTER_SPLIT)
+    small = make_scatters(place, [blocks_of(place, own_shared, shard_proj.shape[0])], refs[at:])
+    at += 6
     norms = Spread("dp", place, size, *refs[at : at + 3])
     norms_task = Spread("task", place, groups, *refs[at + 3 : at + 6])
     routers = Spread("dp", place, size, *refs[at + 6 : at + 9])
-    totals = [
-        Spread("task", place, groups, *[ref.at[piece] for ref in refs[at + 9 : at + 12]])
-        for piece in range(pieces)
-    ]
+    quarter = Spread("task", place, groups, *refs[at + 9 : at + 12])
     stores = []
     for unit in SCATTER_SPLIT + SCATTER_LATE:
-        number = sorted(kinds(SCATTER_SPLIT + SCATTER_LATE, unit[1])).index(unit)
-
-        def store(rows, shard=shards[unit[1]], number=number):
-            shard[number] = rows
+        number = kinds(SCATTER_SPLIT + SCATTER_LATE, unit[1]).index(unit[0])
+
+        def store(rows, shard=shards[unit[1]], number=number, half=unit[2:]):
+            start = half[0] * rows.shape[0] if half else 0
+            shard[number, start : start + rows.shape[0], :] = rows
 
         stores.append(store)
+    for copy in inputs[:2]:
+        copy.wait()
     for one in split:
         one.hop(0)
-    for copy, one in zip(loads, late):
-        copy.wait()
+    for index, one in enumerate(late):
+        unit = SCATTER_LATE[index]
+        if unit[2:] in ((), (0,)):
+            loads[late_grads.index(unit[:2])].wait()
         one.start()
     mix_load.wait()
+    roles = (place.core, place.far, place.across, place.task)
     back = Return(
-        place, lambda source: mixes.at[source], 1, land, joint, back_sent, back_landed
+        place, [mixes.at[role] for role in roles], 1, land, back_sent, back_landed
     )
     back.by_core(0)
     back.to_core(0)
+    router[...] = router_columns[...].T
+    for copy in inputs[2:]:
+        copy.wait()
     second_back(
         lambda rows: grad_rows[rows, :],
         cotangent,
         gain,
         bias,
         mid,
-        w_proj,
+        quarters.at[3],
         router,
         logit_grads(probs, grad_gates),
         norm_sums,
@@ -1427,13 +1582,20 @@
     back.to_across(0)
     first_norm(image, gain, bias, normed_first)
     shared[pieces - 1] = dot_lt(mixed[...], grad_low[...]).astype(bf16)
-    small[pieces - 1].start()
     routers.give(router_sums[...])
     blocks = SEQ // QUERY_BWD
     units, keeps = split + late, stores
     names = dict(zip("stuvwxyz", range(len(units))))
-    names.update({str(piece): len(units) + piece for piece in range(pieces)})
-    units, keeps = units + small, keeps + [one.give for one in totals]
+    names["0"] = len(units)
+    units, keeps = units + small, keeps + [quarter.give]
+    joined = Return(
+        place,
+        [shared.at[role] for role in roles],
+        1,
+        shared_land,
+        shared_sent,
+        shared_landed,
+    )
 
     def run(acts):
         for act in acts:
@@ -1451,55 +1613,70 @@
     def done(pair, columns):
         both = jnp.concatenate([grad_packed[:, part] for part in columns], axis=1)
         shared[pair] = dot_lt(normed_first[...], both).astype(bf16)
-        small[pair].start()
 
     attend_back(
         packed, grad_mixed, logs, grad_packed, grad_keys, grad_values, between, done
     )
-    first_back(image, gain, w_qkv, grad_packed, grad_mid, grad_image, norm_sums)
+    joined.by_core(0)
+    joined.to_core(0)
+    first_back(
+        image,
+        gain,
+        lambda part: quarters[part],
+        grad_packed,
+        grad_mid,
+        grad_image,
+        norm_sums,
+    )
     norms.give(norm_sums[...])
+    joined.to_across(0)
     activations[...] = mid[...] + back.finish(0)
     run(BACKWARD_THEN[0])
-    grad_router[...] = routers.take()
+    own_shared[...] = joined.finish(0).astype(bf16)
+    small[0].start()
+    grad_router[...] = routers.take().T
     norms_task.give(norms.take())
     run(BACKWARD_THEN[1])
-    grad_norm[...] = norms_task.take()
-    for piece in (pieces - 1, *range(pieces - 1)):
-        rows = totals[piece].take()
-        if piece == pieces - 1:
-            shard_proj[...] = rows
-        else:
-            for part in range(3):
-                column = part * D + piece * PAIR
-                shard_qkv[:, column : column + PAIR] = rows[:, part * PAIR : (part + 1) * PAIR]
+    rows = norms_task.take()
+    grad_gain[...] = rows[:2]
+    grad_bias[...] = rows[2:4]
+    quarter.arrive()
+    shard_proj[...] = quarter.land[pieces - 1]
+    for piece in range(pieces - 1):
+        for part in range(3):
+            column = part * D + piece * PAIR
+            shard_qkv[:, column : column + PAIR] = quarter.land[
+                piece, :, part * PAIR : (part + 1) * PAIR
+            ]
+    run(BACKWARD_THEN[2])
 
 
 def backward_sending(*operands):
-    router = operands[7]
-    experts, size = router.shape[0], lax.axis_size("dp")
+    router, whole = operands[11], operands[:9]
+    experts, size = router.shape[1], lax.axis_size("dp")
     outers, thin, wide, pieces = size // 2, D // size, FF // size, HEADS // 2 + 1
     groups = lax.axis_size("task")
     tiles, wholes = ((thin, FF), (wide, D)), ((D, FF), (FF, D))
     ends = SCATTER_SPLIT + SCATTER_LATE
-
-    def spread(peers, *dims, lead=(), dtype=f32):
-        return [pltpu.VMEM((*lead, peers, *dims), dtype)] + [
-            pltpu.SemaphoreType.DMA((*lead, peers - 1))
-        ] * 2
+    late_grads = sorted({unit[:2] for unit in SCATTER_LATE})
+
+    def spread(peers, *dims):
+        return [pltpu.VMEM((peers, *dims), f32)] + [pltpu.SemaphoreType.DMA((peers - 1,))] * 2
 
     return pl.pallas_call(
         functools.partial(backward_sending_kernel, outers, groups),
         out_shape=(
             shape(SEQ, D),
             shape(SEQ, D),
-            shape(8, D),
-            shape(experts, D),
+            shape(2, D),
+            shape(2, D),
+            shape(D, experts),
             shape(thin, 3 * D),
             shape(thin, D),
             *[shape(len(kinds(ends, kind)), *tiles[kind]) for kind in range(2)],
         ),
-        in_specs=[VMEM] * 11 + [ANY] + [VMEM] * 3 + [ANY] * 2 + [VMEM] * 2,
-        out_specs=[VMEM] * 8,
+        in_specs=[ANY] * 9 + [VMEM] * 6 + [ANY] * 3,
+        out_specs=[VMEM] * 9,
         scratch_shapes=backward_scratch()
         + [
             pltpu.VMEM((8, D), f32),
@@ -1507,20 +1684,26 @@
             pltpu.VMEM((pieces, D, D), bf16),
             pltpu.VMEM((groups, SEQ, D), bf16),
             pltpu.VMEM((3, SEQ, D), bf16),
-            pltpu.VMEM((SEQ, D), bf16),
             pltpu.SemaphoreType.DMA((3, 1)),
             pltpu.SemaphoreType.DMA((3, 1)),
+            pltpu.VMEM((experts, D), f32),
+            pltpu.VMEM((D, D), bf16),
+            pltpu.VMEM((3, D, D), bf16),
+            pltpu.SemaphoreType.DMA((3, 1)),
+            pltpu.SemaphoreType.DMA((3, 1)),
+            *[pltpu.VMEM(operand.shape, operand.dtype) for operand in whole],
+            pltpu.SemaphoreType.DMA((len(whole),)),
             pltpu.SemaphoreType.DMA,
-            pltpu.SemaphoreType.DMA((len(SCATTER_LATE),)),
+            pltpu.SemaphoreType.DMA((len(late_grads),)),
         ]
-        + [pltpu.VMEM(wholes[kind], bf16) for _, kind in SCATTER_LATE]
+        + [pltpu.VMEM(wholes[kind], bf16) for _, kind in late_grads]
         + scatter_scratch(SCATTER_LATE, outers, tiles)
         + scatter_scratch(SCATTER_SPLIT, outers, tiles, side=False)
-        + scatter_scratch(range(pieces), outers, (thin, D))
+        + scatter_scratch(range(1), outers, (thin, D))
         + spread(size, 8, D)
         + spread(groups, 8, D)
         + spread(size, experts, D)
-        + spread(groups, thin, D, lead=(pieces,), dtype=bf16),
+        + spread(groups, thin, D),
         compiler_params=params(collective_id=2, has_side_effects=True),
     )(*operands)
 
@@ -1542,8 +1725,6 @@
     local_count = w_in.shape[0]
     image = layer_input.reshape(SEQ, D)
     grad_rows = cotangent.reshape(SEQ, D)
-    router_rows = router[0].T
-    experts = router_rows.shape[0]
     routes = choices.reshape(SEQ, TOPMAX)
 
     def swap(array):
@@ -1561,8 +1742,7 @@
             cot_rows,
             slots,
             gates,
-            full_qkv,
-            full_proj,
+            quarters,
             full_in,
             full_out,
         ) = forward_sending(
@@ -1572,7 +1752,7 @@
             norm_gain,
             norm_bias,
             (w_qkv, w_proj, w_in, w_out),
-            router_rows,
+            router[0],
             routes,
         )
         (
@@ -1591,36 +1771,37 @@
         (
             activations,
             grad_image,
-            grad_norm,
+            grad_gain,
+            grad_bias,
             grad_router,
             grad_qkv,
             grad_proj,
             grad_in,
             grad_out,
         ) = backward_sending(
+            parts_in,
+            parts_out,
             image,
             grad_rows,
+            mid,
+            quarters,
+            packed,
+            mixed,
+            grad_normed,
             norm_gain,
             norm_bias,
-            mid,
-            full_qkv,
-            full_proj,
-            router_rows,
-            packed,
-            mixed,
+            router[0],
             logs,
-            mixes,
-            grad_normed,
             grad_gates,
             probs,
+            mixes,
             late_in,
             late_out,
-            parts_in,
-            parts_out,
         )
         grad_in = jnp.concatenate([early_in, grad_in], axis=0)
         grad_out = jnp.concatenate([early_out, grad_out], axis=0)
     else:
+        router_rows = router[0].T
         full_qkv, full_proj, full_in, full_out = (
             lax.all_gather(w_qkv, "dp", axis=0, tiled=True),
             lax.all_gather(w_proj, "dp", axis=0, tiled=True),
@@ -1641,8 +1822,9 @@
         cot_rows = lax.all_gather(grad_rows.astype(bf16), "task")
         slots = swap(slots.reshape(groups, local_count, SEQ))
         gates = swap(gates.reshape(groups, local_count, SEQ))
+        tokens = jnp.concatenate([normed, cot_rows], axis=-1)
         grad_in, grad_out, grad_gates, mixes, grad_normed = expert_part(
-            normed, cot_rows, slots, gates, full_in, full_out
+            tokens, slots, gates, full_in, full_out
         )
         activations, grad_image, grad_norm, grad_router, grad_shared = backward_part(
             image,
@@ -1666,16 +1848,17 @@
         grad_shared = lax.psum_scatter(grad_shared, "dp", scatter_dimension=0, tiled=True)
         grad_shared = lax.psum(grad_shared, "task").astype(f32)
         grad_qkv, grad_proj = grad_shared[:, : 3 * D], grad_shared[:, 3 * D :]
-        grad_router = lax.psum(grad_router, "dp")
+        grad_router = lax.psum(grad_router, "dp").T
         grad_norm = lax.psum(grad_norm, ("task", "dp"))
+        grad_gain, grad_bias = grad_norm[:2], grad_norm[2:]
     return (
         activations.reshape(layer_input.shape),
         grad_image.reshape(layer_input.shape),
-        grad_norm[:2],
-        grad_norm[2:4],
+        grad_gain,
+        grad_bias,
         grad_qkv,
         grad_proj,
-        grad_router.T[None],
+        grad_router[None],
         grad_in,
         grad_out,
     )

time: 295 us -> 281 us (0.953)
  Pallas kernels: 276 us -> 260 us
    pallas_call x1, Pallas kernels: 81.6 us -> 72.2 us  [backward_sending(): pl.pallas_call(functools.partial(backward_sending_kernel, outers, groups)...]
    pallas_call x1, Pallas kernels: 111 us -> 107 us  [expert_sending(): pl.pallas_call(functools.partial(expert_sending_kernel, outers), out_shap...]
    unnamed x22 -> x27, local copies, waits for them, and re-layouts: 7.55 us -> 11.4 us
where the time goes in v8:
time: 281 us; the launch traced here: 276 us
  Pallas kernels  260 us (93%)
  local copies, waits for them, and re-layouts  11.4 us (4%)
  other arithmetic  3.24 us (1%)
    pallas_call x1, Pallas kernels, expert_sending(): pl.pallas_call(functools.partial(expert_sending_kernel, outers), out_shap...  107 us
    pallas_call x1, Pallas kernels, forward_sending(): pl.pallas_call(functools.partial(forward_sending_kernel, size // 2), out_...  80.4 us
    pallas_call x1, Pallas kernels, backward_sending(): pl.pallas_call(functools.partial(backward_sending_kernel, outers, groups)...  72.2 us
    unnamed x27, local copies, waits for them, and re-layouts  11.4 us

profile of v8, /device:TPU:0, one launch (start us, length us, event | category | flops | bytes accessed | tf_op | source)
XLA Modules:
  0.0 276.1 jit_solution(4482203474628213617)
XLA Ops:
  1.3 1.5 copy.20
  2.8 1.7 copy.21
  4.6 80.4 %shard_map.178 = (f32[1024,384]{1,0:T(8,128)}, bf16[1024,1152]{1,0:T(8,128)(2,1)}, bf16[1024,384]{1,0:T(8,128)(2,1)}, f32[8,1024]{1,0:T(8,128)}, f32[16,1024]{1,...) custom-call(s32[1]{0:T(128)S(6)} %copy.29.top_count, ...), custom_call_target="tpu_custom_call" | custom-call | tf_op jit(solution)/shard_map/pallas_call | solution.py:811
  85.0 107.1 %shard_map.179 = (bf16[2,384,1536]{2,1,0:T(8,128)(2,1)}, bf16[2,1536,384]{2,1,0:T(8,128)(2,1)}, f32[4,4,1024]{2,1,0:T(4,128)}, bf16[4,1024,384]{2,1,0:T(8,128)(2...) custom-call(bf16[4,1024,384]{2,1,0:T(8,128)(2,1)} %get-tuple-element, ...), custom_call_target="tpu_custom_call" | custom-call | tf_op jit(solution)/shard_map/pallas_call | solution.py:1253
  192.1 0.0 copy-start.3
  192.1 72.2 %shard_map.180 = (f32[1024,384]{1,0:T(8,128)}, f32[1024,384]{1,0:T(8,128)}, f32[2,384]{1,0:T(2,128)}, f32[2,384]{1,0:T(2,128)}, f32[384,16]{1,0:T(8,128)}, /*ind...) custom-call(bf16[1,4,48,1536]{3,2,1,0:T(8,128)(2,1)} %get-tuple-element.45.refs_0_, ...), custom_call_target="tpu_custom_call" | custom-call | tf_op jit(solution)/shard_map/pallas_call | solution.py:1666
  264.3 0.0 copy-start.2
  264.3 0.0 copy-start.4
  264.3 1.7 copy.22
  266.0 0.0 copy-done.3
  266.0 2.2 pad_maximum_fusion
  268.2 0.0 copy-done.2
  268.2 0.0 copy-done.4
  268.2 0.0 copy-start.1
  268.2 1.1 pad_maximum_fusion.1
  269.3 0.7 copy-done.1
  270.0 0.0 copy-start
  270.0 1.1 copy.30
  271.1 0.8 copy-done
  272.0 0.0 copy-start.8
  272.0 0.0 copy-start.7
  272.0 0.0 copy-start.5
  272.0 0.0 copy-start.6
  272.0 1.1 copy.31
  273.1 0.0 copy-done.8
  273.1 0.6 copy.32
  273.7 0.0 copy-done.7
  273.7 0.6 copy.33
  274.3 0.0 copy-done.5
  274.3 0.7 copy.34
  275.0 0.0 copy-done.6
  275.0 0.6 copy.35
Async XLA Ops:
  192.1 73.9 %copy-start.3 = (f32[2,48,1536]{2,1,0:T(8,128)S(1)}, f32[2,48,1536]{2,1,0:T(8,128)}, u32[]{:S(2)}) copy-start(f32[2,48,1536]{2,1,0:T(8,128)} %get-tuple-element.65) | copy-start | bytes 1769476
  264.3 3.9 %copy-start.2 = (f32[3,192,384]{2,1,0:T(8,128)S(1)}, f32[3,192,384]{2,1,0:T(8,128)}, u32[]{:S(2)}) copy-start(f32[3,192,384]{2,1,0:T(8,128)} %get-tuple-element.68) | copy-start | bytes 2654212
  264.3 3.9 %copy-start.4 = (f32[1,192,384]{2,1,0:T(8,128)S(1)}, f32[1,192,384]{2,1,0:T(8,128)}, u32[]{:S(2)}) copy-start(f32[1,192,384]{2,1,0:T(8,128)} %get-tuple-element.67) | copy-start | bytes 884740
  268.2 1.8 copy-start.1
  270.0 2.0 copy-start
  272.0 1.2 copy-start.8
  272.0 1.7 copy-start.7
  272.0 2.3 copy-start.5
  272.0 3.0 %copy-start.6 = (f32[48,384]{1,0:T(8,128)S(1)}, f32[48,384]{1,0:T(8,128)}, u32[]{:S(2)}) copy-start(f32[48,384]{1,0:T(8,128)} %get-tuple-element.92) | copy-start | bytes 221188

commit v9 on v8

--- a/solution.py
+++ b/solution.py
@@ -64,8 +64,9 @@
 }
 BACKWARD_THEN = (
     ("t2", "s3", "v1", "u2", "w0"),
-    ("x0", "t3", "v2", "u3", "w1", "00", "x1", "01", "v3", "w2", "02", "x2", "w3", "03"),
-    ("x3",),
+    ("x0", "t3", "v2", "u3", "w1"),
+    ("x1", "v3", "w2", "x2"),
+    ("w3", "x3"),
 )
 
 
@@ -506,6 +507,38 @@
         return total
 
 
+class Deal:
+    def __init__(self, place, ref, size, land, sent, landed):
+        self.place, self.ref, self.size = place, ref, size
+        self.land, self.sent, self.landed = land, sent, landed
+        self.count = land.shape[0]
+
+    def block(self, index):
+        return self.ref.at[rows_at(index, self.size)]
+
+    def move(self, ahead):
+        target = lax.rem(self.place.dp + ahead, self.count)
+        return remote(
+            self.block(target),
+            self.land.at[self.place.dp],
+            self.sent.at[ahead - 1],
+            self.landed.at[ahead - 1],
+            dp=target,
+        )
+
+    def start(self):
+        for ahead in range(1, self.count):
+            self.move(ahead).start()
+
+    def total(self):
+        rows = self.block(self.place.dp)[...].astype(f32)
+        for ahead in range(1, self.count):
+            self.move(ahead).wait()
+            source = lax.rem(self.place.dp + self.count - ahead, self.count)
+            rows += self.land[source].astype(f32)
+        return rows
+
+
 class Return:
     def __init__(self, place, parts, pieces, land, sent, landed):
         self.place, self.parts, self.pieces = place, parts, pieces
@@ -594,7 +627,7 @@
 
 
 def number_slots(choices, top_count, experts):
-    named = choices[...].T
+    named = choices[...]
     numbers = lax.broadcasted_iota(jnp.int32, (experts, SEQ), 0)
     used = jnp.zeros((experts, SEQ), f32)
     for choice in range(TOPMAX):
@@ -694,7 +727,7 @@
     w_proj,
     w_in,
     w_out,
-    router_columns,
+    router,
     choices,
     mid,
     packed,
@@ -710,7 +743,6 @@
     full_out,
     normed_first,
     totals,
-    router,
     own_quarter,
     sent,
     landed,
@@ -751,7 +783,6 @@
     for unit in routed[:AHEAD]:
         gather.start(unit)
     cot.start()
-    router[...] = router_columns[...].T
     first_norm(image, gain, bias, normed_first)
     for hop in range(1, outers):
         gather.step(0, hop)
@@ -805,7 +836,7 @@
 
 def forward_sending(top_count, image, cotangent, gain, bias, shards, router, choices):
     w_qkv, w_proj, w_in, w_out = shards
-    experts, size = router.shape[1], lax.axis_size("dp")
+    experts, size = router.shape[0], lax.axis_size("dp")
     groups, early = lax.axis_size("task"), 1 + GATHER_SPLIT[-1][0]
     units, shares = 1 + len(GATHER_WHOLE + GATHER_SPLIT), 4 + SEQ // QUERY_FWD
     return pl.pallas_call(
@@ -829,7 +860,6 @@
         scratch_shapes=[
             pltpu.VMEM((SEQ, D), bf16),
             pltpu.VMEM((SEQ, 8), f32),
-            pltpu.VMEM((experts, D), f32),
             pltpu.VMEM(w_proj.shape, bf16),
             *gather_semaphores(units, size),
             pltpu.SemaphoreType.DMA((units,)),
@@ -1476,16 +1506,16 @@
 
 
 def backward_sending_kernel(outers, groups, *refs):
-    whole, (gain, bias, router_columns, logs, grad_gates, probs) = refs[:9], refs[9:15]
+    whole, (gain, bias, router, logs, grad_gates, probs) = refs[:9], refs[9:15]
     mixes_all, late_in, late_out = refs[15:18]
     activations, grad_image, grad_gain, grad_bias, grad_router, shard_qkv, shard_proj = refs[18:25]
     shard_in, shard_out = refs[25:27]
     grad_mid, grad_low, grad_mixed, grad_packed, grad_keys, grad_values, normed_first = refs[27:34]
     norm_sums, router_sums, shared, mixes, land, back_sent, back_landed = refs[34:41]
-    router, own_shared, shared_land, shared_sent, shared_landed = refs[41:46]
-    here, here_sem = refs[46:55], refs[55]
+    own_shared, shared_land, shared_sent, shared_landed = refs[41:45]
+    here, here_sem = refs[45:54], refs[54]
     parts_in, parts_out, image, cotangent, mid, quarters, packed, mixed, grad_rows = here
-    refs = refs[56:]
+    refs = refs[55:]
     late_grads = sorted({unit[:2] for unit in SCATTER_LATE})
     mix_sem, grad_sem, grad_refs = refs[0], refs[1], refs[2 : 2 + len(late_grads)]
     refs = refs[2 + len(late_grads) :]
@@ -1532,8 +1562,8 @@
         )
     split = make_scatters(place, split_blocks, refs[at:], side=False)
     at += 3 * len(SCATTER_SPLIT)
-    small = make_scatters(place, [blocks_of(place, own_shared, shard_proj.shape[0])], refs[at:])
-    at += 6
+    deal = Deal(place, own_shared, shard_proj.shape[0], *refs[at : at + 3])
+    at += 3
     norms = Spread("dp", place, size, *refs[at : at + 3])
     norms_task = Spread("task", place, groups, *refs[at + 3 : at + 6])
     routers = Spread("dp", place, size, *refs[at + 6 : at + 9])
@@ -1563,7 +1593,6 @@
     )
     back.by_core(0)
     back.to_core(0)
-    router[...] = router_columns[...].T
     for copy in inputs[2:]:
         copy.wait()
     second_back(
@@ -1586,8 +1615,6 @@
     blocks = SEQ // QUERY_BWD
     units, keeps = split + late, stores
     names = dict(zip("stuvwxyz", range(len(units))))
-    names["0"] = len(units)
-    units, keeps = units + small, keeps + [quarter.give]
     joined = Return(
         place,
         [shared.at[role] for role in roles],
@@ -1633,10 +1660,12 @@
     activations[...] = mid[...] + back.finish(0)
     run(BACKWARD_THEN[0])
     own_shared[...] = joined.finish(0).astype(bf16)
-    small[0].start()
-    grad_router[...] = routers.take().T
+    deal.start()
+    grad_router[...] = routers.take()
     norms_task.give(norms.take())
     run(BACKWARD_THEN[1])
+    quarter.give(deal.total())
+    run(BACKWARD_THEN[2])
     rows = norms_task.take()
     grad_gain[...] = rows[:2]
     grad_bias[...] = rows[2:4]
@@ -1648,12 +1677,12 @@
             shard_qkv[:, column : column + PAIR] = quarter.land[
                 piece, :, part * PAIR : (part + 1) * PAIR
             ]
-    run(BACKWARD_THEN[2])
+    run(BACKWARD_THEN[3])
 
 
 def backward_sending(*operands):
     router, whole = operands[11], operands[:9]
-    experts, size = router.shape[1], lax.axis_size("dp")
+    experts, size = router.shape[0], lax.axis_size("dp")
     outers, thin, wide, pieces = size // 2, D // size, FF // size, HEADS // 2 + 1
     groups = lax.axis_size("task")
     tiles, wholes = ((thin, FF), (wide, D)), ((D, FF), (FF, D))
@@ -1670,7 +1699,7 @@
             shape(SEQ, D),
             shape(2, D),
             shape(2, D),
-            shape(D, experts),
+            shape(experts, D),
             shape(thin, 3 * D),
             shape(thin, D),
             *[shape(len(kinds(ends, kind)), *tiles[kind]) for kind in range(2)],
@@ -1686,7 +1715,6 @@
             pltpu.VMEM((3, SEQ, D), bf16),
             pltpu.SemaphoreType.DMA((3, 1)),
             pltpu.SemaphoreType.DMA((3, 1)),
-            pltpu.VMEM((experts, D), f32),
             pltpu.VMEM((D, D), bf16),
             pltpu.VMEM((3, D, D), bf16),
             pltpu.SemaphoreType.DMA((3, 1)),
@@ -1699,7 +1727,11 @@
         + [pltpu.VMEM(wholes[kind], bf16) for _, kind in late_grads]
         + scatter_scratch(SCATTER_LATE, outers, tiles)
         + scatter_scratch(SCATTER_SPLIT, outers, tiles, side=False)
-        + scatter_scratch(range(1), outers, (thin, D))
+        + [
+            pltpu.VMEM((size, thin, D), bf16),
+            pltpu.SemaphoreType.DMA((size - 1,)),
+            pltpu.SemaphoreType.DMA((size - 1,)),
+        ]
         + spread(size, 8, D)
         + spread(groups, 8, D)
         + spread(size, experts, D)
@@ -1725,7 +1757,8 @@
     local_count = w_in.shape[0]
     image = layer_input.reshape(SEQ, D)
     grad_rows = cotangent.reshape(SEQ, D)
-    routes = choices.reshape(SEQ, TOPMAX)
+    routes = choices.reshape(SEQ, TOPMAX).T
+    router_rows = router[0].T
 
     def swap(array):
         return lax.all_to_all(array, "task", split_axis=0, concat_axis=0, tiled=True)
@@ -1752,7 +1785,7 @@
             norm_gain,
             norm_bias,
             (w_qkv, w_proj, w_in, w_out),
-            router[0],
+            router_rows,
             routes,
         )
         (
@@ -1790,7 +1823,7 @@
             grad_normed,
             norm_gain,
             norm_bias,
-            router[0],
+            router_rows,
             logs,
             grad_gates,
             probs,
@@ -1801,7 +1834,6 @@
         grad_in = jnp.concatenate([early_in, grad_in], axis=0)
         grad_out = jnp.concatenate([early_out, grad_out], axis=0)
     else:
-        router_rows = router[0].T
         full_qkv, full_proj, full_in, full_out = (
             lax.all_gather(w_qkv, "dp", axis=0, tiled=True),
             lax.all_gather(w_proj, "dp", axis=0, tiled=True),
@@ -1848,7 +1880,7 @@
         grad_shared = lax.psum_scatter(grad_shared, "dp", scatter_dimension=0, tiled=True)
         grad_shared = lax.psum(grad_shared, "task").astype(f32)
         grad_qkv, grad_proj = grad_shared[:, : 3 * D], grad_shared[:, 3 * D :]
-        grad_router = lax.psum(grad_router, "dp").T
+        grad_router = lax.psum(grad_router, "dp")
         grad_norm = lax.psum(grad_norm, ("task", "dp"))
         grad_gain, grad_bias = grad_norm[:2], grad_norm[2:]
     return (
@@ -1858,7 +1890,7 @@
         grad_bias,
         grad_qkv,
         grad_proj,
-        grad_router[None],
+        grad_router.T[None],
         grad_in,
         grad_out,
     )

time: 281 us -> 276 us (0.982)
  local copies, waits for them, and re-layouts: 11.4 us -> 6.98 us
    unnamed x27, local copies, waits for them, and re-layouts: 11.4 us -> 6.98 us
where the time goes in v9:
time: 276 us; the launch traced here: 271 us
  Pallas kernels  259 us (94%)
  local copies, waits for them, and re-layouts  6.98 us (3%)
  other arithmetic  3.34 us (1%)
    pallas_call x1, Pallas kernels, expert_sending(): pl.pallas_call(functools.partial(expert_sending_kernel, outers), out_shap...  107 us
    pallas_call x1, Pallas kernels, forward_sending(): pl.pallas_call(functools.partial(forward_sending_kernel, size // 2), out_...  80.2 us
    pallas_call x1, Pallas kernels, backward_sending(): pl.pallas_call(functools.partial(backward_sending_kernel, outers, groups)...  71.4 us
    unnamed x27, local copies, waits for them, and re-layouts  6.98 us

profile of v9, /device:TPU:0, one launch (start us, length us, event | category | flops | bytes accessed | tf_op | source)
XLA Modules:
  0.0 270.8 jit_solution(5725096532362159758)
XLA Ops:
  1.3 80.2 %shard_map.178 = (f32[1024,384]{1,0:T(8,128)}, bf16[1024,1152]{1,0:T(8,128)(2,1)}, bf16[1024,384]{1,0:T(8,128)(2,1)}, f32[8,1024]{1,0:T(8,128)}, f32[16,1024]{1,...) custom-call(s32[1]{0:T(128)S(6)} %copy.27.top_count, ...), custom_call_target="tpu_custom_call" | custom-call | tf_op jit(solution)/shard_map/pallas_call | solution.py:842
  81.5 107.1 %shard_map.179 = (bf16[2,384,1536]{2,1,0:T(8,128)(2,1)}, bf16[2,1536,384]{2,1,0:T(8,128)(2,1)}, f32[4,4,1024]{2,1,0:T(4,128)}, bf16[4,1024,384]{2,1,0:T(8,128)(2...) custom-call(bf16[4,1024,384]{2,1,0:T(8,128)(2,1)} %get-tuple-element, ...), custom_call_target="tpu_custom_call" | custom-call | tf_op jit(solution)/shard_map/pallas_call | solution.py:1283
  188.6 0.0 copy-start.3
  188.6 71.4 %shard_map.180 = (f32[1024,384]{1,0:T(8,128)}, f32[1024,384]{1,0:T(8,128)}, f32[2,384]{1,0:T(2,128)}, f32[2,384]{1,0:T(2,128)}, f32[16,384]{1,0:T(8,128)}, /*ind...) custom-call(bf16[1,4,48,1536]{3,2,1,0:T(8,128)(2,1)} %get-tuple-element.45.refs_0_, ...), custom_call_target="tpu_custom_call" | custom-call | tf_op jit(solution)/shard_map/pallas_call | solution.py:1695
  260.1 0.0 copy-start.2
  260.1 0.0 copy-start.4
  260.1 0.0 copy-done.3
  260.1 2.2 pad_maximum_fusion
  262.3 0.0 copy-done.2
  262.3 0.0 copy-done.4
  262.4 0.0 copy-start.1
  262.4 1.1 pad_maximum_fusion.1
  263.4 0.7 copy-done.1
  264.2 0.0 copy-start
  264.2 1.1 copy.28
  265.3 0.8 copy-done
  266.2 0.0 copy-start.9
  266.2 0.0 copy-start.8
  266.2 0.0 copy-start.5
  266.2 0.0 copy-start.6
  266.2 0.0 copy-start.7
  266.2 1.1 copy.29
  267.3 0.0 copy-done.9
  267.3 0.6 copy.30
  267.9 0.0 copy-done.8
  267.9 0.6 copy.31
  268.5 0.0 copy-done.5
  268.5 0.7 copy.32
  269.2 0.0 copy-done.6
  269.2 0.6 copy.33
  269.8 0.0 copy-done.7
  269.8 0.6 copy.34
Async XLA Ops:
  188.6 71.5 %copy-start.3 = (f32[2,48,1536]{2,1,0:T(8,128)S(1)}, f32[2,48,1536]{2,1,0:T(8,128)}, u32[]{:S(2)}) copy-start(f32[2,48,1536]{2,1,0:T(8,128)} %get-tuple-element.65) | copy-start | bytes 1769476
  260.1 2.3 copy-start.2
  260.1 2.3 copy-start.4
  262.4 1.8 copy-start.1
  264.2 2.0 copy-start
  266.2 1.2 copy-start.9
  266.2 1.7 copy-start.8
  266.2 2.3 copy-start.5
  266.2 3.0 %copy-start.6 = (f32[48,384]{1,0:T(8,128)S(1)}, f32[48,384]{1,0:T(8,128)}, u32[]{:S(2)}) copy-start(f32[48,384]{1,0:T(8,128)} %get-tuple-element.83) | copy-start | bytes 221188
  266.2 3.6 %copy-start.7 = (f32[16,384]{1,0:T(8,128)S(1)}, f32[16,384]{1,0:T(8,128)}, u32[]{:S(2)}) copy-start(f32[16,384]{1,0:T(8,128)} %get-tuple-element.64) | copy-start | bytes 73732

commit v10 on v9

--- a/solution.py
+++ b/solution.py
@@ -41,21 +41,20 @@
 GATHER_POINTS = {2: ((0, 1), (0, 3), (1, 0), (1, 4)), 3: ((0, 2), (1, 1), (1, 4), (3, 0))}
 SCATTER_POINTS = {1: (2, 4), 3: (3, 6)}
 
-AHEAD = 2
-FORWARD_FIRST = ((0, 1), (1, 1))
+AHEAD, NEXT = 2, 4
+FORWARD_FIRST = ((0, 1), (1, 1), (2, 1), (3, 1), (0, 2))
 FORWARD_POINTS = {
-    0: ((2, 1),),
-    1: ((3, 1),),
-    2: ((4, 1),),
-    3: ((5, 1),),
-    5: ((0, 2),),
-    6: ((1, 2),),
-    8: ((2, 2),),
-    9: ((3, 2),),
-    10: ((4, 2),),
-    11: ((5, 2),),
+    0: ((1, 2),),
+    1: ((2, 2), (4, 0), (5, 0)),
+    2: ((3, 2),),
+    5: ((0, 3),),
+    6: ((1, 3),),
+    7: ((2, 3),),
+    8: ((3, 3),),
+    9: ((4, 1),),
+    10: ((5, 1),),
 }
-FORWARD_THEN = (((0, 3), (1, 3)), ((2, 3), (3, 3), (4, 3), (5, 3)))
+FORWARD_THEN = (((4, 2), (5, 2)), ((4, 3), (5, 3)))
 
 BACKWARD_POINTS = {
     3: ("s1", "u0",),
@@ -777,8 +776,10 @@
     gate = share(2, lambda source: gates_all.at[source])
     def run(acts):
         for unit, hop in acts:
-            if unit < len(routed):
+            if hop:
                 gather.step(routed[unit], hop)
+            else:
+                gather.start(routed[unit])
 
     for unit in routed[:AHEAD]:
         gather.start(unit)
@@ -786,7 +787,7 @@
     first_norm(image, gain, bias, normed_first)
     for hop in range(1, outers):
         gather.step(0, hop)
-    for unit in routed[AHEAD:]:
+    for unit in routed[AHEAD:NEXT]:
         gather.start(unit)
     gather.finish(0)
     quarter = share(3 + SEQ // QUERY_FWD, lambda source: quarters.at[source])
@@ -1513,9 +1514,9 @@
     grad_mid, grad_low, grad_mixed, grad_packed, grad_keys, grad_values, normed_first = refs[27:34]
     norm_sums, router_sums, shared, mixes, land, back_sent, back_landed = refs[34:41]
     own_shared, shared_land, shared_sent, shared_landed = refs[41:45]
-    here, here_sem = refs[45:54], refs[54]
+    here, here_sem, result_sem = refs[45:54], refs[54], refs[55]
     parts_in, parts_out, image, cotangent, mid, quarters, packed, mixed, grad_rows = here
-    refs = refs[55:]
+    refs = refs[56:]
     late_grads = sorted({unit[:2] for unit in SCATTER_LATE})
     mix_sem, grad_sem, grad_refs = refs[0], refs[1], refs[2 : 2 + len(late_grads)]
     refs = refs[2 + len(late_grads) :]
@@ -1652,12 +1653,18 @@
         lambda part: quarters[part],
         grad_packed,
         grad_mid,
-        grad_image,
+        grad_mid,
         norm_sums,
     )
+    results = [
+        pltpu.make_async_copy(grad_mid, grad_image, result_sem.at[0]),
+        pltpu.make_async_copy(mid, activations, result_sem.at[1]),
+    ]
+    results[0].start()
     norms.give(norm_sums[...])
     joined.to_across(0)
-    activations[...] = mid[...] + back.finish(0)
+    mid[...] = mid[...] + back.finish(0)
+    results[1].start()
     run(BACKWARD_THEN[0])
     own_shared[...] = joined.finish(0).astype(bf16)
     deal.start()
@@ -1678,6 +1685,8 @@
                 piece, :, part * PAIR : (part + 1) * PAIR
             ]
     run(BACKWARD_THEN[3])
+    for copy in results:
+        copy.wait()
 
 
 def backward_sending(*operands):
@@ -1705,7 +1714,7 @@
             *[shape(len(kinds(ends, kind)), *tiles[kind]) for kind in range(2)],
         ),
         in_specs=[ANY] * 9 + [VMEM] * 6 + [ANY] * 3,
-        out_specs=[VMEM] * 9,
+        out_specs=[ANY] * 2 + [VMEM] * 7,
         scratch_shapes=backward_scratch()
         + [
             pltpu.VMEM((8, D), f32),
@@ -1721,6 +1730,7 @@
             pltpu.SemaphoreType.DMA((3, 1)),
             *[pltpu.VMEM(operand.shape, operand.dtype) for operand in whole],
             pltpu.SemaphoreType.DMA((len(whole),)),
+            pltpu.SemaphoreType.DMA((2,)),
             pltpu.SemaphoreType.DMA,
             pltpu.SemaphoreType.DMA((len(late_grads),)),
         ]

time: 276 us -> 271 us (0.982)
  Pallas kernels: 259 us -> 254 us
    pallas_call x1, Pallas kernels: 80.2 us -> 76.7 us  [forward_sending(): pl.pallas_call(functools.partial(forward_sending_kernel, size // 2), out_...]
where the time goes in v10:
time: 271 us; the launch traced here: 267 us
  Pallas kernels  254 us (94%)
  local copies, waits for them, and re-layouts  6.98 us (3%)
  other arithmetic  3.34 us (1%)
    pallas_call x1, Pallas kernels, expert_sending(): pl.pallas_call(functools.partial(expert_sending_kernel, outers), out_shap...  108 us
    pallas_call x1, Pallas kernels, forward_sending(): pl.pallas_call(functools.partial(forward_sending_kernel, size // 2), out_...  76.7 us
    pallas_call x1, Pallas kernels, backward_sending(): pl.pallas_call(functools.partial(backward_sending_kernel, outers, groups)...  70.1 us
    unnamed x27, local copies, waits for them, and re-layouts  6.98 us

profile of v10, /device:TPU:0, one launch (start us, length us, event | category | flops | bytes accessed | tf_op | source)
XLA Modules:
  0.0 266.5 jit_solution(15383722368329592260)
XLA Ops:
  1.3 76.7 %shard_map.178 = (f32[1024,384]{1,0:T(8,128)}, bf16[1024,1152]{1,0:T(8,128)(2,1)}, bf16[1024,384]{1,0:T(8,128)(2,1)}, f32[8,1024]{1,0:T(8,128)}, f32[16,1024]{1,...) custom-call(s32[1]{0:T(128)S(6)} %copy.27.top_count, ...), custom_call_target="tpu_custom_call" | custom-call | tf_op jit(solution)/shard_map/pallas_call | solution.py:843
  78.0 107.7 %shard_map.179 = (bf16[2,384,1536]{2,1,0:T(8,128)(2,1)}, bf16[2,1536,384]{2,1,0:T(8,128)(2,1)}, f32[4,4,1024]{2,1,0:T(4,128)}, bf16[4,1024,384]{2,1,0:T(8,128)(2...) custom-call(bf16[4,1024,384]{2,1,0:T(8,128)(2,1)} %get-tuple-element, ...), custom_call_target="tpu_custom_call" | custom-call | tf_op jit(solution)/shard_map/pallas_call | solution.py:1284
  185.7 0.0 copy-start.3
  185.7 70.1 %shard_map.180 = (f32[1024,384]{1,0:T(8,128)}, f32[1024,384]{1,0:T(8,128)}, f32[2,384]{1,0:T(2,128)}, f32[2,384]{1,0:T(2,128)}, f32[16,384]{1,0:T(8,128)}, /*ind...) custom-call(bf16[1,4,48,1536]{3,2,1,0:T(8,128)(2,1)} %get-tuple-element.45.refs_0_, ...), custom_call_target="tpu_custom_call" | custom-call | tf_op jit(solution)/shard_map/pallas_call | solution.py:1704
  255.8 0.0 copy-start.2
  255.8 0.0 copy-start.4
  255.8 0.0 copy-done.3
  255.8 2.2 pad_maximum_fusion
  258.1 0.0 copy-done.2
  258.1 0.0 copy-done.4
  258.1 0.0 copy-start.1
  258.1 1.1 pad_maximum_fusion.1
  259.2 0.7 copy-done.1
  259.9 0.0 copy-start
  259.9 1.1 copy.28
  261.0 0.8 copy-done
  261.9 0.0 copy-start.9
  261.9 0.0 copy-start.8
  261.9 0.0 copy-start.5
  261.9 0.0 copy-start.6
  261.9 0.0 copy-start.7
  261.9 1.1 copy.29
  263.0 0.0 copy-done.9
  263.0 0.6 copy.30
  263.6 0.0 copy-done.8
  263.6 0.6 copy.31
  264.2 0.0 copy-done.5
  264.2 0.7 copy.32
  264.9 0.0 copy-done.6
  264.9 0.6 copy.33
  265.5 0.0 copy-done.7
  265.5 0.6 copy.34
Async XLA Ops:
  185.7 70.1 %copy-start.3 = (f32[2,48,1536]{2,1,0:T(8,128)S(1)}, f32[2,48,1536]{2,1,0:T(8,128)}, u32[]{:S(2)}) copy-start(f32[2,48,1536]{2,1,0:T(8,128)} %get-tuple-element.65) | copy-start | bytes 1769476
  255.8 2.3 copy-start.2
  255.8 2.3 copy-start.4
  258.1 1.8 copy-start.1
  259.9 2.0 copy-start
  261.9 1.2 copy-start.9
  261.9 1.7 copy-start.8
  261.9 2.3 copy-start.5
  261.9 3.0 %copy-start.6 = (f32[48,384]{1,0:T(8,128)S(1)}, f32[48,384]{1,0:T(8,128)}, u32[]{:S(2)}) copy-start(f32[48,384]{1,0:T(8,128)} %get-tuple-element.83) | copy-start | bytes 221188
  261.9 3.6 %copy-start.7 = (f32[16,384]{1,0:T(8,128)S(1)}, f32[16,384]{1,0:T(8,128)}, u32[]{:S(2)}) copy-start(f32[16,384]{1,0:T(8,128)} %get-tuple-element.64) | copy-start | bytes 73732

commit v11 on v10

--- a/solution.py
+++ b/solution.py
@@ -956,17 +956,14 @@
 
 def combine(slots, first, local_count, sent, columns, source, store):
     size = SEQ // RETURNS
-    columns[...] = slots[source].T
+    mine = [slots[source, pl.ds(first + expert, 1), :] for expert in range(local_count)]
+    columns[...] = jnp.concatenate(mine, axis=0).T
     for piece in range(RETURNS):
         rows = pl.ds(piece * size, size)
         lanes = lax.broadcasted_iota(jnp.int32, (size, CAP), 1)
-        mine = lax.broadcasted_iota(jnp.int32, (size, columns.shape[1]), 1)
-        picks = []
-        for expert in range(local_count):
-            column = jnp.max(
-                jnp.where(mine == first + expert, columns[rows, :], -1), axis=1, keepdims=True
-            )
-            picks.append(ones_at(lanes == column))
+        picks = [
+            ones_at(lanes == columns[rows, expert : expert + 1]) for expert in range(local_count)
+        ]
         back = dot(jnp.concatenate(picks, axis=1), sent[source])
         store(piece, rows, back[:, :D].astype(bf16), back[:, D:].astype(bf16))
 
@@ -981,7 +978,7 @@
         pltpu.VMEM((width, FF), bf16),
         pltpu.VMEM((width, FF), bf16),
         pltpu.VMEM((groups, local_count * CAP, 2 * D), bf16),
-        pltpu.VMEM((SEQ, experts), jnp.int32),
+        pltpu.VMEM((SEQ, local_count), jnp.int32),
     ]
 
 

time: 271 us -> 262 us (0.967)
  Pallas kernels: 254 us -> 245 us
    pallas_call x1, Pallas kernels: 108 us -> 98.3 us  [expert_sending(): pl.pallas_call(functools.partial(expert_sending_kernel, outers), out_shap...]
where the time goes in v11:
time: 262 us; the launch traced here: 257 us
  Pallas kernels  245 us (94%)
  local copies, waits for them, and re-layouts  6.98 us (3%)
  other arithmetic  3.34 us (1%)
    pallas_call x1, Pallas kernels, expert_sending(): pl.pallas_call(functools.partial(expert_sending_kernel, outers), out_shap...  98.3 us
    pallas_call x1, Pallas kernels, forward_sending(): pl.pallas_call(functools.partial(forward_sending_kernel, size // 2), out_...  76.7 us
    pallas_call x1, Pallas kernels, backward_sending(): pl.pallas_call(functools.partial(backward_sending_kernel, outers, groups)...  70 us
    unnamed x27, local copies, waits for them, and re-layouts  6.98 us

profile of v11, /device:TPU:0, one launch (start us, length us, event | category | flops | bytes accessed | tf_op | source)
XLA Modules:
  0.0 257.0 jit_solution(12811318593753744529)
XLA Ops:
  1.3 76.7 %shard_map.178 = (f32[1024,384]{1,0:T(8,128)}, bf16[1024,1152]{1,0:T(8,128)(2,1)}, bf16[1024,384]{1,0:T(8,128)(2,1)}, f32[8,1024]{1,0:T(8,128)}, f32[16,1024]{1,...) custom-call(s32[1]{0:T(128)S(6)} %copy.27.top_count, ...), custom_call_target="tpu_custom_call" | custom-call | tf_op jit(solution)/shard_map/pallas_call | solution.py:843
  78.0 98.3 %shard_map.179 = (bf16[2,384,1536]{2,1,0:T(8,128)(2,1)}, bf16[2,1536,384]{2,1,0:T(8,128)(2,1)}, f32[4,4,1024]{2,1,0:T(4,128)}, bf16[4,1024,384]{2,1,0:T(8,128)(2...) custom-call(bf16[4,1024,384]{2,1,0:T(8,128)(2,1)} %get-tuple-element, ...), custom_call_target="tpu_custom_call" | custom-call | tf_op jit(solution)/shard_map/pallas_call | solution.py:1281
  176.2 0.0 copy-start.3
  176.2 70.0 %shard_map.180 = (f32[1024,384]{1,0:T(8,128)}, f32[1024,384]{1,0:T(8,128)}, f32[2,384]{1,0:T(2,128)}, f32[2,384]{1,0:T(2,128)}, f32[16,384]{1,0:T(8,128)}, /*ind...) custom-call(bf16[1,4,48,1536]{3,2,1,0:T(8,128)(2,1)} %get-tuple-element.45.refs_0_, ...), custom_call_target="tpu_custom_call" | custom-call | tf_op jit(solution)/shard_map/pallas_call | solution.py:1701
  246.2 0.0 copy-start.2
  246.3 0.0 copy-start.4
  246.3 0.0 copy-done.3
  246.3 2.2 pad_maximum_fusion
  248.5 0.0 copy-done.2
  248.5 0.0 copy-done.4
  248.5 0.0 copy-start.1
  248.5 1.1 pad_maximum_fusion.1
  249.6 0.7 copy-done.1
  250.4 0.0 copy-start
  250.4 1.1 copy.28
  251.5 0.8 copy-done
  252.3 0.0 copy-start.9
  252.3 0.0 copy-start.8
  252.3 0.0 copy-start.5
  252.3 0.0 copy-start.6
  252.3 0.0 copy-start.7
  252.4 1.1 copy.29
  253.5 0.0 copy-done.9
  253.5 0.6 copy.30
  254.1 0.0 copy-done.8
  254.1 0.6 copy.31
  254.7 0.0 copy-done.5
  254.7 0.7 copy.32
  255.4 0.0 copy-done.6
  255.4 0.6 copy.33
  256.0 0.0 copy-done.7
  256.0 0.6 copy.34
Async XLA Ops:
  176.2 70.0 %copy-start.3 = (f32[2,48,1536]{2,1,0:T(8,128)S(1)}, f32[2,48,1536]{2,1,0:T(8,128)}, u32[]{:S(2)}) copy-start(f32[2,48,1536]{2,1,0:T(8,128)} %get-tuple-element.65) | copy-start | bytes 1769476
  246.2 2.3 copy-start.2
  246.3 2.3 copy-start.4
  248.5 1.8 copy-start.1
  250.4 2.0 copy-start
  252.3 1.2 copy-start.9
  252.3 1.7 copy-start.8
  252.3 2.3 copy-start.5
  252.3 3.0 %copy-start.6 = (f32[48,384]{1,0:T(8,128)S(1)}, f32[48,384]{1,0:T(8,128)}, u32[]{:S(2)}) copy-start(f32[48,384]{1,0:T(8,128)} %get-tuple-element.83) | copy-start | bytes 221188
  252.3 3.6 %copy-start.7 = (f32[16,384]{1,0:T(8,128)S(1)}, f32[16,384]{1,0:T(8,128)}, u32[]{:S(2)}) copy-start(f32[16,384]{1,0:T(8,128)} %get-tuple-element.64) | copy-start | bytes 73732
